TPU v7x, 128 devices: a whole 4x4x4 slice. The times are simulated.
128 devices in a mesh: rep: 8 (over z, core), shard: 16 (over y, x).
Axes of the slice: x: 4, y: 4, z: 4, core: 2. Of those that a mesh axis runs over, the one named last changes fastest.
Arguments:
- partials: bfloat16 [8, 48, 1024, 1024], P('rep', None, 'shard'), may hold values from -2.5 to 2.5
- owned_block: int32 [128], replicated, may hold values from -1 to 47, as said below
Outputs:
- directions: bfloat16 [48, 1024, 1024], P(None, 'shard')
Inputs may be any that keep to these rules, and one draw needn't show every extreme that they name: `owned_block`: exactly 42 entries name a block, no block is named twice, every other entry is -1.
All inputs are finite; a program needn't handle non-finite values.
Results may differ from a plain program's by a relative error of at most 0.014.
Values may be sent and summed in bfloat16 or wider, within the bound.
No kernel may reach another device: no remote copies, remote signals or barrier semaphores. Data moves between devices by JAX's collectives and lax.ppermute only.
A program may use at most 128 MiB of HBM per device.

v0:
```python
import jax
import jax.numpy as jnp
from jax import lax
from jax.sharding import PartitionSpec as P

damping = 0.1


def inverse_root(statistic):
    width = statistic.shape[0]
    identity = jnp.eye(width, dtype=jnp.float32)
    norm_scale = 0.25 * jnp.sqrt(jnp.sum(statistic * statistic))
    coupled = (statistic / norm_scale).astype(jnp.bfloat16)
    factor_step = ((5.0 * identity - coupled.astype(jnp.float32)) * 0.25).astype(jnp.bfloat16)
    root_now = factor_step
    step_square = jnp.dot(factor_step, factor_step, preferred_element_type=jnp.float32).astype(
        jnp.bfloat16
    )
    step_fourth = jnp.dot(step_square, step_square, preferred_element_type=jnp.float32).astype(
        jnp.bfloat16
    )
    coupled = jnp.dot(step_fourth, coupled, preferred_element_type=jnp.float32).astype(jnp.bfloat16)
    factor_step = ((5.0 * identity - coupled.astype(jnp.float32)) * 0.25).astype(jnp.bfloat16)
    root_now = jnp.dot(root_now, factor_step, preferred_element_type=jnp.float32).astype(
        jnp.bfloat16
    )
    return root_now


def precondition(gradient):
    width = gradient.shape[0]
    identity = jnp.eye(width, dtype=jnp.float32)
    left = (
        jnp.dot(gradient, gradient.T, preferred_element_type=jnp.float32) / width
        + damping * identity
    )
    right = (
        jnp.dot(gradient.T, gradient, preferred_element_type=jnp.float32) / width
        + damping * identity
    )
    left_root = inverse_root(left)
    right_root = inverse_root(right)
    left_side = jnp.dot(left_root, gradient, preferred_element_type=jnp.float32).astype(
        jnp.bfloat16
    )
    raw_dir = jnp.dot(left_side, right_root, preferred_element_type=jnp.float32)
    grad_values = gradient.astype(jnp.float32)
    graft_ratio = jnp.sqrt(jnp.mean(grad_values * grad_values) + 1e-06) / jnp.sqrt(
        jnp.mean(raw_dir * raw_dir) + 1e-06
    )
    return (raw_dir * graft_ratio).astype(jnp.bfloat16)


def local(partials, owned_block):
    rep_count = lax.axis_size("rep")
    shard_count = lax.axis_size("shard")
    own_rows = partials[0]
    block_count, piece_rows, width = own_rows.shape
    safe_ids = jnp.maximum(owned_block, 0)
    outgoing = jnp.where(
        (owned_block >= 0)[:, None, None], own_rows[safe_ids], jnp.zeros((), jnp.bfloat16)
    )
    arrived = lax.all_to_all(outgoing, ("rep", "shard"), split_axis=0, concat_axis=0, tiled=True)
    summed = jnp.sum(
        arrived.reshape(rep_count, shard_count, piece_rows, width).astype(jnp.float32), axis=0
    )
    grad_block = summed.astype(jnp.bfloat16).reshape(shard_count * piece_rows, width)
    finished = precondition(grad_block)
    returned_rows = lax.all_to_all(
        finished.reshape(shard_count, piece_rows, width),
        "shard",
        split_axis=0,
        concat_axis=0,
        tiled=True,
    )
    row_owners = lax.dynamic_slice_in_dim(
        owned_block, lax.axis_index("rep") * shard_count, shard_count
    )
    block_ids = jnp.arange(block_count, dtype=jnp.int32)
    selector = (row_owners[None, :] == block_ids[:, None]).astype(jnp.bfloat16)
    placed = jnp.einsum("bj,jpc->bpc", selector, returned_rows, preferred_element_type=jnp.float32)
    chosen = jnp.any(owned_block[None, :] == block_ids[:, None], axis=1)
    contribution = jnp.where(chosen[:, None, None], placed, own_rows.astype(jnp.float32))
    return lax.psum(contribution.astype(jnp.bfloat16), "rep")


def solution(mesh):
    in_specs = (P("rep", None, "shard", None), P())
    out_specs = P(None, "shard", None)
    return jax.shard_map(local, mesh=mesh, in_specs=in_specs, out_specs=out_specs, check_vma=False)
```

profile of v0, /device:TPU:1, one launch (start us, length us, event | category | flops | bytes accessed | tf_op | source)
XLA Modules:
  0.0 458.5 jit_solution(4062603103343203813)
XLA Ops:
  6.5 0.7 broadcast_maximum_fusion
  7.2 0.7 broadcast_compare_fusion
  7.9 10.8 %gather_fusion = bf16[128,64,1024]{2,1,0:T(8,128)(2,1)} fusion(bf16[48,64,1024]{2,1,0:T(8,128)(2,1)} %bitcast.34, s32[1024]{0:T(1024)S(1)} %pad_clamp_fusion), kind=kCustom, calls=%fused_computation | custom fusion | bytes 33554944 | tf_op jit(solution)/shard_map/gather | solution.py:61
  18.7 8.3 %broadcast_select_fusion = bf16[128,64,1024]{2,1,0:T(8,128)(2,1)S(1)} fusion(bf16[128,64,1024]{2,1,0:T(8,128)(2,1)} %gather_fusion, pred[128]{0:T(512)(128)(4,1)S(1)} %broadcast_compare_fusion), kind=kLoop, calls=%fused_computation.1 | loop fusion | flops 8388608 | bytes 33554560 | tf_op jit(solution)/shard_map/jit(_where)/select_n | solution.py:60
  26.9 198.1 %all_to_all.10 = bf16[128,64,1024]{2,1,0:T(8,128)(2,1)} all-to-all(bf16[128,64,1024]{2,1,0:T(8,128)(2,1)S(1)} %broadcast_select_fusion), channel_id=1, replica_groups=mesh['rep'=8,'shard'=16] {'rep','shard'}, dimensions={0} | all-to-all | bytes 33554432 | tf_op jit(solution)/shard_map/all_to_all | solution.py:63
  225.1 9.9 %reduce_sum.48 = bf16[16,64,1024]{2,1,0:T(8,128)(2,1)S(1)} reduce(bf16[8,16,64,1024]{3,2,1,0:T(8,128)(2,1)} %bitcast.35, bf16[]{:T(256)} %constant.35.clone.1), dimensions={0}, to_apply=%region_1.2 | reduce | flops 7340032 | bytes 18874370 | tf_op jit(solution)/shard_map/reduce_sum | solution.py:64
  235.0 5.0 %multiply_reduce_fusion.2 = (f32[]{:T(128)}, f32[1024,1024,1]{1,0,2:T(8,128)}) fusion(bf16[16,64,1024]{2,1,0:T(8,128)(2,1)S(1)} %reduce_sum.48), kind=kOutput, calls=%fused_computation.22 | convolution fusion | flops 2153775104 | bytes 6291460 | tf_op jit(solution)/shard_map/dot_general | solution.py:38
  240.1 1.6 multiply_reduce_fusion.1
  241.7 4.9 %multiply_reduce_fusion.3 = (f32[]{:T(128)}, f32[1024,1024]{1,0:T(8,128)}) fusion(bf16[1024,1024]{1,0:T(8,128)(2,1)S(1)} %bitcast.36), kind=kOutput, calls=%fused_computation.24 | convolution fusion | flops 2153775104 | bytes 6291460 | tf_op jit(solution)/shard_map/dot_general | solution.py:34
  247.3 14.0 %fusion.26 = bf16[1024,1024]{1,0:T(8,128)(2,1)} fusion(f32[1024,1024]{1,0:T(8,128)} %get-tuple-element.8, f32[]{:T(128)S(6)} %mul.62), kind=kOutput, calls=%fused_computation.42 | convolution fusion | flops 4307550208 | bytes 6291460 | tf_op jit(solution)/shard_map/dot_general | solution.py:19
  261.3 10.1 %fusion.10 = bf16[1024,1024]{1,0:T(8,128)(2,1)} fusion(bf16[1024,1024]{1,0:T(8,128)(2,1)} %fusion.26, f32[1024,1024]{1,0:T(8,128)} %get-tuple-element.8, f32[]{:T(128)S(6)} %mul.62), kind=kOutput, calls=%fused_computation.27 | convolution fusion | flops 4320133120 | bytes 8388612 | tf_op jit(solution)/shard_map/dot_general | solution.py:24
  272.1 14.3 %fusion.18 = bf16[1024,1024]{1,0:T(8,128)(2,1)} fusion(f32[1024,1024,1]{1,0,2:T(8,128)} %get-tuple-element.6, f32[]{:T(128)S(6)} %mul.66), kind=kOutput, calls=%fused_computation.34 | convolution fusion | flops 4307550208 | bytes 6291460 | tf_op jit(solution)/shard_map/dot_general | solution.py:19
  286.4 10.2 %fusion.8 = bf16[1024,1024]{1,0:T(8,128)(2,1)} fusion(bf16[1024,1024]{1,0:T(8,128)(2,1)} %fusion.18, f32[1024,1024,1]{1,0,2:T(8,128)} %get-tuple-element.6, f32[]{:T(128)S(6)} %mul.66), kind=kOutput, calls=%fused_computation.26 | convolution fusion | flops 4320133120 | bytes 8388612 | tf_op jit(solution)/shard_map/dot_general | solution.py:24
  296.5 9.3 %multiply_reduce_fusion = (f32[]{:T(128)}, f32[1024,1024]{1,0:T(8,128)}) fusion(bf16[1024,1024]{1,0:T(8,128)(2,1)} %fusion.8, bf16[1024,1024]{1,0:T(8,128)(2,1)S(1)} %bitcast.37, bf16[1024,1024]{1,0:T(8,128)(2,1)} %fusion.10), kind=kOutput, calls=%fused_computation.19 | convolution fusion | flops 4298113024 | bytes 10485764 | tf_op jit(solution)/shard_map/dot_general | solution.py:46
  307.2 4.1 multiply_convert_fusion
  311.3 4.1 all-to-all-start.1
  315.4 0.0 all-reduce.2.cloned.1.call-start
  315.4 0.1 dynamic_slice.3
  315.5 0.1 fusion.60
  315.6 28.8 %all-to-all-done.1 = bf16[16,64,1024]{2,1,0:T(8,128)(2,1)S(1)} async-done(((bf16[16,64,1024]{2,1,0:T(8,128)(2,1)}), bf16[16,64,1024]{2,1,0:T(8,128)(2,1)S(1)}, u32[]{:S(2)}, u32[]{:S(2)}) %all-to-all-start.1) | async-done | bytes 2097184 | tf_op jit(solution)/shard_map/all_to_all | solution.py:69
  344.4 15.2 %select_convert_fusion = bf16[48,64,1024]{2,0,1:T(8,128)(2,1)} fusion(bf16[1,48,64,1024]{3,2,1,0:T(8,128)(2,1)} %param.2, pred[48]{0:T(512)(128)(4,1)S(1)} %fusion.60, bf16[16,64,1024]{2,1,0:T(8,128)(2,1)S(1)} %all-to-all-done.1, s32[16]{0:T(128)S(1)} %dynamic_slice.3), kind=kOutput, calls=%fused_computation.2 | convolution fusion | flops 110101248 | bytes 14680176 | tf_op jit(solution)/shard_map/bj,jpc->bpc/dot_general | solution.py:81
  359.6 0.0 all-reduce.2.cloned.1.call-update
  359.6 82.8 %all-reduce.2.cloned.1.call-done = bf16[48,64,1024]{2,0,1:T(8,128)(2,1)} async-done(((bf16[48,64,1024]{2,0,1:T(8,128)(2,1)}), bf16[48,64,1024]{2,0,1:T(8,128)(2,1)}) %all-reduce.2.cloned.1.call-update) | async-done | bytes 6291472 | tf_op jit(solution)/shard_map/psum | solution.py:84
  442.4 9.0 %copy.17 = bf16[48,64,1024]{2,1,0:T(8,128)(2,1)} copy(bf16[48,64,1024]{2,0,1:T(8,128)(2,1)} %all-reduce.2.cloned.1.call-done) | data formatting | bytes 12582912 | tf_op jit(solution)/shard_map/psum | solution.py:84
  (3 shorter events, 0.0 us)
Async XLA Ops:
  307.1 8.3 %copy-start = (s32[128]{0:T(128)S(1)}, s32[128]{0:T(128)}, u32[]{:S(2)}) copy-start(s32[128]{0:T(128)} %param.3) | copy-start | bytes 1540
  311.3 33.1 %all-to-all-start.1 = ((bf16[16,64,1024]{2,1,0:T(8,128)(2,1)}), bf16[16,64,1024]{2,1,0:T(8,128)(2,1)S(1)}, u32[]{:S(2)}, u32[]{:S(2)}) async-start(bf16[16,64,1024]{2,1,0:T(8,128)(2,1)} %bitcast.6), calls=%async_computation.1 | async-start | bytes 4194304 | tf_op jit(solution)/shard_map/all_to_all | solution.py:69
  315.4 127.1 %all-reduce.2.cloned.1.call-start = ((), (), s32[]{:S(2)}) async-start(), calls=%async_computation.2 | async-start | bytes 12582912 | tf_op jit(solution)/shard_map/psum | solution.py:84
Sparse Core Ops, SparseCore 0:
  359.7 82.6 all-reduce.1
where the time goes:
time: 462 us; the launch traced here: 459 us
  blocking collectives  198 us (43%)
  waiting for transfers between devices  112 us (24%)
  matrix products  83 us (18%)
  other arithmetic  25.4 us (5%)
  local copies, waits for them, and re-layouts  19.9 us (4%)
  between operations  16.3 us (4%)
    all_to_all x1, blocking collectives, local(): lax.all_to_all(outgoing, ('rep', 'shard'), split_axis=0, concat_axis=0, t...  198 us
    psum x1, waiting for transfers between devices, local(): return lax.psum(contribution.astype(jnp.bfloat16), 'rep')  82.8 us
    all_to_all x1, waiting for transfers between devices, local(): lax.all_to_all(finished.reshape(shard_count, piece_rows, width), 'shard',...  28.8 us
    dot_general x2, matrix products, inverse_root(): jnp.dot(step_square, step_square, preferred_element_type=jnp.float32)  28.4 us
    dot_general x2, matrix products, inverse_root(): jnp.dot(root_now, factor_step, preferred_element_type=jnp.float32)  20.2 us
    dot_general x1, matrix products, local(): jnp.einsum('bj,jpc->bpc', selector, returned_rows, preferred_element_type...  15.2 us
    gather x1, local copies, waits for them, and re-layouts, local(): own_rows[safe_ids]  10.8 us
    reduce_sum x1, other arithmetic, local(): jnp.sum(arrived.reshape(rep_count, shard_count, piece_rows, width).astype...  9.94 us
  transfers between devices with their start and end apart: 2, of which 2 were waited for; matrix products, arithmetic and copies ran while one was open for 0% of the time, Pallas kernels for 0%

commit v1 on v0

v1 whole, which is shorter than its diff:
```python
import functools

import jax
import jax.numpy as jnp
from jax import lax
from jax.experimental import pallas as pl
from jax.experimental.pallas import tpu as pltpu
from jax.sharding import Mesh, PartitionSpec as P

damping = 0.1
mib = 2**20
ROWS = ((0,), (0,))
COLUMNS = ((1,), (1,))


def dot(a, b, contract=((1,), (0,))):
    return lax.dot_general(a, b, (contract, ((), ())), preferred_element_type=jnp.float32)


def rows_at(start, count):
    return pl.ds(pl.multiple_of(start, count), count)


def root_kernel(place, own, sibling, root, grad, stat, step, square, coupled):
    core = place[0]
    half, width = own.shape
    grad[rows_at(core * half, half), :] = own[...]
    grad[rows_at((1 - core) * half, half), :] = sibling[...]
    low, high = slice(0, half), slice(half, width)
    upper = ((low, low), (low, high), (high, high))
    eye = lax.broadcasted_iota(jnp.int32, (half, half), 0) == lax.broadcasted_iota(
        jnp.int32, (half, half), 1
    )

    def statistic(contract):
        total = jnp.zeros((1, half), jnp.float32)
        for r, c in upper:
            if contract == ROWS:
                product = dot(grad[:, r], grad[:, c], ROWS)
            else:
                product = dot(grad[r, :], grad[c, :], COLUMNS)
            value = product * (1.0 / width)
            if r == c:
                value = value + jnp.where(eye, damping, 0.0)
            stat[r, c] = value
            squares = jnp.sum(value * value, axis=0, keepdims=True)
            total = total + (squares if r == c else 2.0 * squares)
        return total

    total = lax.cond(core == 0, lambda: statistic(COLUMNS), lambda: statistic(ROWS))
    inverse = 4.0 * lax.rsqrt(jnp.sum(total, axis=1, keepdims=True))
    across, along = {}, {}
    for r, c in upper:
        matrix = (stat[r, c] * inverse).astype(jnp.bfloat16).astype(jnp.float32)
        if r == c:
            value = ((jnp.where(eye, 5.0, 0.0) - matrix) * 0.25).astype(jnp.bfloat16)
            both = jnp.where(eye, 4.0 * value.astype(jnp.float32) + matrix, 0.0)
            across[r.start] = jnp.sum(both, axis=0, keepdims=True)
            along[r.start] = jnp.sum(both, axis=1, keepdims=True)
        else:
            value = (matrix * -0.25).astype(jnp.bfloat16)
        step[r, c] = value

    def times_itself(matrix):
        one, two, three = (matrix[block] for block in upper)
        yield upper[0], dot(one, one) + dot(two, two, COLUMNS)
        yield upper[1], dot(one, two) + dot(two, three)
        yield upper[2], dot(two, two, ROWS) + dot(three, three)

    for (r, c), product in times_itself(step):
        square[r, c] = product.astype(jnp.bfloat16)
        value = step[r, c].astype(jnp.float32)
        coupled[r, c] = (value * across[c.start] - 4.0 * product).astype(jnp.bfloat16)
        if r != c:
            coupled[high, low] = (value * along[r.start] - 4.0 * product).astype(jnp.bfloat16)
    one, two, three = (product.astype(jnp.bfloat16) for _, product in times_itself(square))
    products = (
        dot(one, coupled[low, low]) + dot(two, coupled[high, low], COLUMNS),
        dot(one, coupled[low, high]) + dot(two, coupled[high, high]),
        dot(two, coupled[low, high], ROWS) + dot(three, coupled[high, high]),
    )
    for (r, c), product in zip(upper, products):
        value = ((5.0 * step[r, c].astype(jnp.float32) - product) * 0.25).astype(jnp.bfloat16)
        root[upper.index((r, c))] = value


def from_left(root, matrix, write):
    half = root.shape[1]
    one, two, three = root[0], root[1], root[2]
    top, bottom = matrix[:half, :], matrix[half:, :]
    write(slice(0, half), slice(None), dot(one, top) + dot(two, bottom))
    write(slice(half, 2 * half), slice(None), dot(two, top, ROWS) + dot(three, bottom))


def from_right(matrix, root, write):
    half = root.shape[1]
    one, two, three = root[0], root[1], root[2]
    before, after = matrix[:, :half], matrix[:, half:]
    write(slice(None), slice(0, half), dot(before, one) + dot(after, two, COLUMNS))
    write(slice(None), slice(half, 2 * half), dot(before, two) + dot(after, three))


def side_kernel(place, root, grad, side, grad_sum):
    core = place[0]

    def write(rows, columns, product):
        side[rows, columns] = product.astype(jnp.bfloat16)

    @pl.when(core == 0)
    def _():
        from_left(root, grad, write)

    @pl.when(core == 1)
    def _():
        from_right(grad, root, write)

    value = grad[...].astype(jnp.float32)
    grad_sum[...] = jnp.sum(value * value, axis=0, keepdims=True)


def finish_kernel(place, own, side, root, grad_sum, out, raw):
    core = place[0]
    half, width = own.shape

    def write(rows, columns, product):
        raw[rows, columns] = product

    @pl.when(core == 0)
    def _():
        from_right(side, root, write)

    @pl.when(core == 1)
    def _():
        from_left(root, side, write)

    raw_sum = jnp.sum(raw[...] * raw[...], axis=0, keepdims=True)
    scale = 1.0 / (width * width)
    grad_mean = jnp.sum(grad_sum[...], axis=1, keepdims=True) * scale
    raw_mean = jnp.sum(raw_sum, axis=1, keepdims=True) * scale
    ratio = jnp.sqrt(grad_mean + 1e-06) / jnp.sqrt(raw_mean + 1e-06)
    active = place[1] > 0

    @pl.when(active)
    def _():
        out[...] = (raw[rows_at(core * half, half), :] * ratio).astype(jnp.bfloat16)

    @pl.when(jnp.logical_not(active))
    def _():
        out[...] = own[...]


def place_kernel(targets, place, *refs):
    *pieces, out, sems = refs
    core, plane = place[0], place[2]
    copies = []
    for index, (which, skip, count, shift, start, mine) in enumerate(targets):
        rows = pieces[which].shape[1]
        half = core if mine else 1 - core
        first = lax.rem(plane + shift, 4) * (out.shape[0] // 4) + start
        copies.append(
            pltpu.make_async_copy(
                pieces[which].at[pl.ds(skip, count)],
                out.at[pl.ds(first, count), rows_at(half * rows, rows), :],
                sems.at[index],
            )
        )
    for copy in copies:
        copy.start()
    for copy in copies:
        copy.wait()


def local(partials, owned_block):
    core = lax.axis_index("core")
    plane = lax.axis_index("z")
    slot = lax.axis_index("y") * 4 + lax.axis_index("x")
    _, blocks, piece_rows, width = partials.shape
    planes = 4
    per_plane = blocks // planes
    part = per_plane // 2
    rows = piece_rows // 2
    shards = 16
    half = rows * shards
    swap = [(0, 1), (1, 0)]
    up = [(i, (i + 1) % planes) for i in range(planes)]
    down = [(i, (i - 1) % planes) for i in range(planes)]
    def plus(*terms):
        total = terms[0].astype(jnp.float32)
        for term in terms[1:]:
            total = total + term.astype(jnp.float32)
        return total.astype(jnp.bfloat16)

    smem = pl.BlockSpec(memory_space=pltpu.SMEM)
    vmem = pl.BlockSpec(memory_space=pltpu.VMEM)
    anywhere = pl.BlockSpec(memory_space=pl.ANY)
    halves = partials.reshape(planes, per_plane, 2, rows, width)

    def rows_of(here, shift, which):
        sliced = lax.dynamic_slice(
            halves, ((here + shift) % planes, 0, which, 0, 0), (1, per_plane, 1, rows, width)
        )
        return sliced.reshape(per_plane, rows, width)

    with jax.named_scope("sum_over_replicas"):
        sent, next_plane = lax.optimization_barrier((rows_of(plane, 2, 1 - core), plane))
        got = lax.ppermute(sent, "core", swap)
        kept, *sent = lax.optimization_barrier(
            [rows_of(next_plane, 2, core)] + [rows_of(next_plane, k, 1 - core) for k in (1, 3, 0)]
        )
        got_above, got_below, got_mine = (lax.ppermute(each, "core", swap) for each in sent)
        far = plus(kept, got)
        far_low, far_high, here, owners = lax.optimization_barrier(
            (far[:part], far[part:], plane, owned_block)
        )
        from_above = lax.ppermute(far_low, "z", down)
        from_below = lax.ppermute(far_high, "z", up)
        kept_above, kept_below, kept_mine = lax.optimization_barrier(
            [rows_of(here, k, core) for k in (1, 3, 0)]
        )
        to_above = plus(kept_above, got_above)
        to_below = plus(kept_below, got_below)
        mine = plus(kept_mine, got_mine)
        low_below = lax.ppermute(to_above[:part], "z", up)
        high_above = lax.ppermute(to_below[part:], "z", down)
        low_above = lax.ppermute(plus(to_below[:part], from_above), "z", down)
        high_below = lax.ppermute(plus(to_above[part:], from_below), "z", up)
        summed = jnp.concatenate(
            [
                plus(mine[:part], low_below, low_above),
                plus(mine[part:], high_above, high_below),
                jnp.zeros((shards - per_plane, rows, width), jnp.bfloat16),
            ],
            axis=0,
        )

    block = plane * per_plane + slot
    active = jnp.any(owners == block) & (slot < per_plane)
    place = jnp.stack([core, active.astype(jnp.int32), plane]).astype(jnp.int32)
    summed, place = lax.optimization_barrier((summed, place))

    with jax.named_scope("rows_to_owner"):
        own = lax.all_to_all(summed, ("y", "x"), 0, 0, tiled=True).reshape(half, width)
        sibling = lax.ppermute(own, "core", swap)

    square = (width, width)
    whole = jax.ShapeDtypeStruct(square, jnp.bfloat16)
    work = 2 * width**3
    own_root, grad = pl.pallas_call(
        root_kernel,
        out_shape=[jax.ShapeDtypeStruct((3, half, half), jnp.bfloat16), whole],
        in_specs=[smem, vmem, vmem],
        out_specs=[vmem, vmem],
        scratch_shapes=[
            pltpu.VMEM(square, jnp.float32),
            pltpu.VMEM(square, jnp.bfloat16),
            pltpu.VMEM(square, jnp.bfloat16),
            pltpu.VMEM(square, jnp.bfloat16),
        ],
        compiler_params=pltpu.CompilerParams(vmem_limit_bytes=40 * mib),
        cost_estimate=pl.CostEstimate(flops=3 * work, bytes_accessed=6 * mib, transcendentals=0),
        name="inverse_root",
    )(place, own, sibling)
    sibling_root = lax.ppermute(own_root, "core", swap)
    side, grad_sum = pl.pallas_call(
        side_kernel,
        out_shape=[whole, jax.ShapeDtypeStruct((1, width), jnp.float32)],
        in_specs=[smem, vmem, vmem],
        out_specs=[vmem, vmem],
        compiler_params=pltpu.CompilerParams(vmem_limit_bytes=32 * mib),
        cost_estimate=pl.CostEstimate(flops=work, bytes_accessed=6 * mib, transcendentals=0),
        name="apply_own_root",
    )(place, own_root, grad)
    finished = pl.pallas_call(
        finish_kernel,
        out_shape=jax.ShapeDtypeStruct((half, width), jnp.bfloat16),
        in_specs=[smem, vmem, vmem, vmem, vmem],
        out_specs=vmem,
        scratch_shapes=[pltpu.VMEM(square, jnp.float32)],
        compiler_params=pltpu.CompilerParams(vmem_limit_bytes=32 * mib),
        cost_estimate=pl.CostEstimate(flops=work, bytes_accessed=6 * mib, transcendentals=0),
        name="apply_other_root",
    )(place, own, side, sibling_root, grad_sum)

    with jax.named_scope("rows_to_shards"):
        back = lax.all_to_all(
            finished.reshape(shards, rows, width), ("y", "x"), 0, 0, tiled=True
        )[:per_plane]

    out_shape = jax.ShapeDtypeStruct((blocks, piece_rows, width), jnp.bfloat16)

    def put(name, before, *entries):
        targets, operands = [], []
        for which, (array, *runs) in enumerate(entries):
            skip = 0
            for shift, start, count, mine in runs:
                targets.append((which, skip, count, shift, start, mine))
                skip += count
            operands.append(array)
        moved = sum(4 * operand.size for operand in operands)
        operands.append(before)
        first = before.shape != out_shape.shape
        return pl.pallas_call(
            functools.partial(place_kernel, targets),
            out_shape=out_shape,
            in_specs=[smem] + [vmem] * len(entries) + [vmem if first else anywhere],
            out_specs=anywhere,
            scratch_shapes=[pltpu.SemaphoreType.DMA((len(targets),))],
            input_output_aliases={} if first else {len(operands): 0},
            compiler_params=pltpu.CompilerParams(vmem_limit_bytes=24 * mib),
            cost_estimate=pl.CostEstimate(flops=0, bytes_accessed=moved, transcendentals=0),
            name=name,
        )(place, *operands)

    def other_core(piece):
        return lax.ppermute(piece, "core", swap)

    with jax.named_scope("gather_over_replicas"):
        above_low = lax.ppermute(back[:part], "z", down)
        below_high = lax.ppermute(back[part:], "z", up)
        behind = other_core(back[:1, :16, :128])
        low, high, behind = lax.optimization_barrier((back[:part], back[part:], behind))
        above_high = lax.ppermute(high, "z", down)
        below_low = lax.ppermute(low, "z", up)
        above_low, below_high, other = lax.optimization_barrier(
            (above_low, below_high, other_core(back))
        )
        far_low = lax.ppermute(above_low, "z", down)
        far_high = lax.ppermute(below_high, "z", up)
        passed = other_core(jnp.concatenate([above_low, below_high], axis=0))
        out = put(
            "place_early",
            behind,
            (back, (0, 0, per_plane, True)),
            (other, (0, 0, per_plane, False)),
            (above_low, (1, 0, part, True)),
            (below_high, (3, part, part, True)),
        )
        above_high, below_low, out = lax.optimization_barrier((above_high, below_low, out))
        return put(
            "place_late",
            out,
            (passed, (1, 0, part, False), (3, part, part, False)),
            (above_high, (1, part, part, True)),
            (below_low, (3, 0, part, True)),
            (other_core(above_high), (1, part, part, False)),
            (other_core(below_low), (3, 0, part, False)),
            (far_low, (2, 0, part, True)),
            (far_high, (2, part, part, True)),
            (other_core(far_low), (2, 0, part, False)),
            (other_core(far_high), (2, part, part, False)),
        )


def solution(mesh):
    grid = Mesh(mesh.devices.reshape(4, 2, 4, 4), ("z", "core", "y", "x"))
    in_specs = (P(("z", "core"), None, ("y", "x"), None), P())
    out_specs = P(None, ("y", "x"), None)
    return jax.shard_map(local, mesh=grid, in_specs=in_specs, out_specs=out_specs, check_vma=False)
```

time: 462 us -> 138 us (0.30)
  blocking collectives: 198 us -> 41.1 us
  matrix products: 83 us -> 0 us
  waiting for transfers between devices: 112 us -> 31.5 us
  starting transfers between devices: 4.12 us -> 29 us
  Pallas kernels: 0 us -> 19.2 us
  other arithmetic: 25.4 us -> 8.23 us
  between operations: 16.3 us -> 1.05 us
  local copies, waits for them, and re-layouts: 19.9 us -> 7.61 us
    all_to_all x1 -> x2, blocking collectives: 198 us -> 41.1 us  [the longest x1 22 us: local(): lax.all_to_all(summed, ('y', 'x'), 0, 0, tiled=True).reshape(half, width)]
    dot_general x8 -> x0, matrix products: 83 us -> none  [the longest x2 28.4 us: inverse_root(): jnp.dot(step_square, step_square, preferred_element_type=jnp.float32)]
    psum x1 -> x0, waiting for transfers between devices: 82.8 us -> none  [local(): return lax.psum(contribution.astype(jnp.bfloat16), 'rep')]
    ppermute x0 -> x25, waiting for transfers between devices: none -> 31.5 us  [the longest x1 8.42 us: local(): high_below = lax.ppermute(plus(to_above[part:], from_below), 'z', up)]
    ppermute x0 -> x25, starting transfers between devices: none -> 29 us  [the longest x7 7.68 us: other_core(): return lax.ppermute(piece, 'core', swap)]
    all_to_all x1 -> x0, waiting for transfers between devices: 28.8 us -> none  [local(): lax.all_to_all(finished.reshape(shard_count, piece_rows, width), 'shard',...]
    pallas_call x0 -> x5, Pallas kernels: none -> 19.2 us  [the longest x1 8.22 us: local(): pl.pallas_call(root_kernel, out_shape=[jax.ShapeDtypeStruct((3, half, hal...]
    reduce_sum x2 -> x0, other arithmetic: 11.6 us -> none  [the longest x1 9.94 us: local(): jnp.sum(arrived.reshape(rep_count, shard_count, piece_rows, width).astype...]
  transfers between devices with their start and end apart: 2 -> 25, of which waited for: 2 -> 11; matrix products, arithmetic and copies ran while one was open for 0% -> 10% of each run, Pallas kernels for 0% -> 4%
where the time goes in v1:
time: 138 us
  blocking collectives  41.1 us (30%)
  waiting for transfers between devices  31.5 us (23%)
  starting transfers between devices  29 us (21%)
  Pallas kernels  19.2 us (14%)
  other arithmetic  8.23 us (6%)
  local copies, waits for them, and re-layouts  7.61 us (6%)
    all_to_all x1, blocking collectives, local(): lax.all_to_all(summed, ('y', 'x'), 0, 0, tiled=True).reshape(half, width)  22 us
    all_to_all x1, blocking collectives, local(): lax.all_to_all(finished.reshape(shards, rows, width), ('y', 'x'), 0, 0, t...  19.2 us
    ppermute x1, waiting for transfers between devices, local(): high_below = lax.ppermute(plus(to_above[part:], from_below), 'z', up)  8.42 us
    pallas_call x1, Pallas kernels, local(): pl.pallas_call(root_kernel, out_shape=[jax.ShapeDtypeStruct((3, half, hal...  8.22 us
    ppermute x7, starting transfers between devices, other_core(): return lax.ppermute(piece, 'core', swap)  7.68 us
    convert_element_type x7, other arithmetic, plus(): return total.astype(jnp.bfloat16)  7.31 us
    reshape x3, local copies, waits for them, and re-layouts, rows_of(): return sliced.reshape(per_plane, rows, width)  6.54 us
    ppermute x1, waiting for transfers between devices, local(): below_high = lax.ppermute(back[part:], 'z', up)  6.39 us
  transfers between devices with their start and end apart: 25, of which 11 were waited for; matrix products, arithmetic and copies ran while one was open for 10% of the time, Pallas kernels for 4%

profile of v1, /device:TPU:1, one launch (start us, length us, event | category | flops | bytes accessed | tf_op | source)
XLA Modules:
  0.0 137.8 jit_solution(9885574313690191805)
XLA Ops:
  1.2 1.5 %collective-permute-start = (bf16[12,32,1024]{2,1,0:T(8,128)(2,1)S(1)}, bf16[12,32,1024]{2,1,0:T(8,128)(2,1)S(1)}, u32[]{:S(2)}, u32[]{:S(2)}) collective-permute-start(bf16[12,32,1024]{2,1,0:T(8,128)(2,1)S(1)} %dynamic-slice_bitcast_fusion.7), channel_id=1, source_target_pairs={{0,16},{16,0},{1,17},{17,1},{2,18},{18,2},{3,19},{19,3},{4,20},{20... | collective-permute-start | bytes 2359304 | tf_op jit(solution)/shard_map/sum_over_replicas/ppermute | solution.py:206
  2.7 3.5 %dynamic-slice_bitcast_fusion.3 = (bf16[12,32,1024]{2,1,0:T(8,128)(2,1)S(1)}, bf16[12,32,1024]{2,1,0:T(8,128)(2,1)}, bf16[12,32,1024]{2,1,0:T(8,128)(2,1)}, bf16[12,32,1024]{2,1,0:T(8,128)(2,1)S(1)}) fusion(bf16[4,12,2,32,1024]{4,3,2,1,0:T(8,128)(2,1)} %bitcast.27, s32[]{:T(128)S(6)} %select_n.82, s32[]{:T(128)S(6)} %select_n.73, s32[]{:T(128)S(6)} %select_n.80, ...), kind=kLoop, calls=%fused_computation.13 | loop fusion | bytes 6291480 | tf_op jit(solution)/shard_map/sum_over_replicas/reshape | solution.py:202
  8.0 3.8 %collective-permute-start.5 = (bf16[6,32,1024]{2,1,0:T(8,128)(2,1)S(1)}, bf16[6,32,1024]{2,1,0:T(8,128)(2,1)}, u32[]{:S(2)}, u32[]{:S(2)}) collective-permute-start(bf16[6,32,1024]{2,1,0:T(8,128)(2,1)S(1)} %get-tuple-element.43), channel_id=1, source_target_pairs={{0,96},{32,0},{64,32},{96,64},{1,97},{33,1},{65,33},{97,65},{2,98}... | collective-permute-start | bytes 1179656 | tf_op jit(solution)/shard_map/sum_over_replicas/ppermute | solution.py:215
  11.9 1.8 %dynamic-slice_bitcast_fusion = (bf16[12,32,1024]{2,1,0:T(8,128)(2,1)S(1)}, bf16[12,32,1024]{2,1,0:T(8,128)(2,1)S(1)}, bf16[12,32,1024]{2,1,0:T(8,128)(2,1)S(1)}) fusion(bf16[4,12,2,32,1024]{4,3,2,1,0:T(8,128)(2,1)} %bitcast.28, s32[]{:T(128)S(6)} %select_n.88, s32[]{:T(128)S(6)} %select_n.76, s32[]{:T(128)S(6)} %select_n.86, s32[]{:T(128)S(6)} %select_n.84), kind=kLoop, calls=%fused_computation.10 | loop fusion | bytes 4718608 | tf_op jit(solution)/shard_map/sum_over_replicas/reshape | solution.py:202
  18.1 2.7 %collective-permute-start.7 = (bf16[6,32,1024]{2,1,0:T(8,128)(2,1)S(1)}, bf16[6,32,1024]{2,1,0:T(8,128)(2,1)S(1)}, u32[]{:S(2)}, u32[]{:S(2)}) collective-permute-start(bf16[6,32,1024]{2,1,0:T(8,128)(2,1)S(1)} %slice.59), channel_id=1, source_target_pairs={{0,96},{32,0},{64,32},{96,64},{1,97},{33,1},{65,33},{97,65},{2,98}... | collective-permute-start | bytes 1179656 | tf_op jit(solution)/shard_map/sum_over_replicas/ppermute | solution.py:224
  20.9 2.5 %collective-permute-done.8 = bf16[6,32,1024]{2,1,0:T(8,128)(2,1)} collective-permute-done((bf16[6,32,1024]{2,1,0:T(8,128)(2,1)}, bf16[6,32,1024]{2,1,0:T(8,128)(2,1)}, u32[]{:S(2)}, u32[]{:S(2)}) %collective-permute-start.8) | collective-permute-done | bytes 393248 | tf_op jit(solution)/shard_map/sum_over_replicas/ppermute | solution.py:216
  25.7 2.7 %collective-permute-start.6 = (bf16[6,32,1024]{2,1,0:T(8,128)(2,1)S(1)}, bf16[6,32,1024]{2,1,0:T(8,128)(2,1)S(1)}, u32[]{:S(2)}, u32[]{:S(2)}) collective-permute-start(bf16[6,32,1024]{2,1,0:T(8,128)(2,1)S(1)} %add_convert_fusion.7), channel_id=1, source_target_pairs={{0,96},{32,0},{64,32},{96,64},{1,97},{33,1},{65,33},{97,65},{2,98}... | collective-permute-start | bytes 1179656 | tf_op jit(solution)/shard_map/sum_over_replicas/ppermute | solution.py:225
  30.0 1.7 %collective-permute-done.3 = bf16[6,32,1024]{2,1,0:T(8,128)(2,1)S(1)} collective-permute-done((bf16[6,32,1024]{2,1,0:T(8,128)(2,1)S(1)}, bf16[6,32,1024]{2,1,0:T(8,128)(2,1)S(1)}, u32[]{:S(2)}, u32[]{:S(2)}) %collective-permute-start.3) | collective-permute-done | bytes 393248 | tf_op jit(solution)/shard_map/sum_over_replicas/ppermute | solution.py:223
  31.7 8.4 %collective-permute-done.9 = bf16[6,32,1024]{2,1,0:T(8,128)(2,1)S(1)} collective-permute-done((bf16[6,32,1024]{2,1,0:T(8,128)(2,1)S(1)}, bf16[6,32,1024]{2,1,0:T(8,128)(2,1)S(1)}, u32[]{:S(2)}, u32[]{:S(2)}) %collective-permute-start.9) | collective-permute-done | bytes 393248 | tf_op jit(solution)/shard_map/sum_over_replicas/ppermute | solution.py:226
  40.7 22.0 %all_to_all.10 = bf16[16,32,1024]{2,1,0:T(8,128)(2,1)S(1)} all-to-all(bf16[16,32,1024]{2,1,0:T(8,128)(2,1)S(1)} %maximum_maximum_fusion), channel_id=1, replica_groups=mesh['z'=4,'core'=2,'y'=4,'x'=4] {'y','x'}, dimensions={0} | all-to-all | bytes 2097152 | tf_op jit(solution)/shard_map/rows_to_owner/all_to_all | solution.py:242
  62.7 2.8 %collective-permute-start.10 = (bf16[512,1024]{1,0:T(8,128)(2,1)S(1)}, bf16[512,1024]{1,0:T(8,128)(2,1)S(1)}, u32[]{:S(2)}, u32[]{:S(2)}) collective-permute-start(bf16[512,1024]{1,0:T(8,128)(2,1)S(1)} %bitcast.22), channel_id=1, source_target_pairs={{0,16},{16,0},{1,17},{17,1},{2,18},{18,2},{3,19},{19,3},{4,20},{20... | collective-permute-start | bytes 3145736 | tf_op jit(solution)/shard_map/rows_to_owner/ppermute | solution.py:243
  65.4 2.3 %collective-permute-done.10.sibling = bf16[512,1024]{1,0:T(8,128)(2,1)S(1)} collective-permute-done((bf16[512,1024]{1,0:T(8,128)(2,1)S(1)}, bf16[512,1024]{1,0:T(8,128)(2,1)S(1)}, u32[]{:S(2)}, u32[]{:S(2)}) %collective-permute-start.10) | collective-permute-done | bytes 1048608 | tf_op jit(solution)/shard_map/rows_to_owner/ppermute | solution.py:243
  67.7 8.2 %inverse_root.1 = (bf16[3,512,512]{2,1,0:T(8,128)(2,1)S(1)}, bf16[1024,1024]{1,0:T(8,128)(2,1)S(1)}) custom-call(s32[3]{0:T(128)S(1)} %pad_add_fusion.place, bf16[512,1024]{1,0:T(8,128)(2,1)S(1)} %bitcast.23, bf16[512,1024]{1,0:T(8,128)(2,1)S(1)} %collective-permute-done.10.sibling), custom_call_target="tpu_custom_call" | custom-call | flops 6442450944 | bytes 6291456 | tf_op jit(solution)/shard_map/inverse_root/pallas_call | solution.py:248
  76.4 3.0 %apply_own_root.1 = (bf16[1024,1024]{1,0:T(8,128)(2,1)S(1)}, f32[1,1024]{1,0:T(1,128)S(1)}) custom-call(s32[3]{0:T(128)S(1)} %pad_add_fusion.place, bf16[3,512,512]{2,1,0:T(8,128)(2,1)S(1)} %get-tuple-element.48.root, bf16[1024,1024]{1,0:T(8,128)(2,1)S(1)} %get-tuple-element.49.grad), custom_call_target="tpu_custom_call" | custom-call | flops 2147483648 | bytes 6291456 | tf_op jit(solution)/shard_map/apply_own_root/pallas_call | solution.py:264
  79.5 3.5 %apply_other_root.1 = bf16[512,1024]{1,0:T(8,128)(2,1)S(1)} custom-call(s32[3]{0:T(128)S(1)} %pad_add_fusion.place, bf16[512,1024]{1,0:T(8,128)(2,1)S(1)} %bitcast.24, bf16[1024,1024]{1,0:T(8,128)(2,1)S(1)} %get-tuple-element.50.side, bf16[3,512,512]{2,1,0:T(8,128)(2,1)S(1)} %collective-permute-done.11.root, f32[1,1024]{1,0:T(1,128)S(1)} %get-tuple-element.51.grad_sum), custom_call_target="tpu_custom_call" | custom-call | flops 2147483648 | bytes 6291456 | tf_op jit(solution)/shard_map/apply_other_root/pallas_call | solution.py:273
  82.9 19.2 %all_to_all.11 = bf16[16,32,1024]{2,1,0:T(8,128)(2,1)S(1)} all-to-all(bf16[16,32,1024]{2,1,0:T(8,128)(2,1)S(1)} %bitcast.25), channel_id=1, replica_groups=mesh['z'=4,'core'=2,'y'=4,'x'=4] {'y','x'}, dimensions={0} | all-to-all | bytes 2097152 | tf_op jit(solution)/shard_map/rows_to_shards/all_to_all | solution.py:285
  102.1 1.9 %collective-permute-start.14 = (bf16[12,32,1024]{2,1,0:T(8,128)(2,1)S(1)}, bf16[12,32,1024]{2,1,0:T(8,128)(2,1)S(1)}, u32[]{:S(2)}, u32[]{:S(2)}) collective-permute-start(bf16[12,32,1024]{2,1,0:T(8,128)(2,1)S(1)} %slice.63.refs_0_), channel_id=1, source_target_pairs={{0,16},{16,0},{1,17},{17,1},{2,18},{18,2},{3,19},{19,3},{4,20},{20... | collective-permute-start | bytes 2359304 | tf_op jit(solution)/shard_map/gather_over_replicas/ppermute | solution.py:315
  104.1 2.7 %collective-permute-start.12 = (bf16[6,32,1024]{2,1,0:T(8,128)(2,1)S(1)}, bf16[6,32,1024]{2,1,0:T(8,128)(2,1)S(1)}, u32[]{:S(2)}, u32[]{:S(2)}) collective-permute-start(bf16[6,32,1024]{2,1,0:T(8,128)(2,1)S(1)} %get-tuple-element.55), channel_id=1, source_target_pairs={{0,96},{32,0},{64,32},{96,64},{1,97},{33,1},{65,33},{97,65},{2,98}... | collective-permute-start | bytes 1179656 | tf_op jit(solution)/shard_map/gather_over_replicas/ppermute | solution.py:318
  109.7 6.4 %collective-permute-done.13.refs_3_ = bf16[6,32,1024]{2,1,0:T(8,128)(2,1)S(1)} collective-permute-done((bf16[6,32,1024]{2,1,0:T(8,128)(2,1)S(1)}, bf16[6,32,1024]{2,1,0:T(8,128)(2,1)S(1)}, u32[]{:S(2)}, u32[]{:S(2)}) %collective-permute-start.13) | collective-permute-done | bytes 393248 | tf_op jit(solution)/shard_map/gather_over_replicas/ppermute | solution.py:319
  116.1 2.4 %collective-permute-start.21 = (bf16[6,32,1024]{2,1,0:T(8,128)(2,1)S(1)}, bf16[6,32,1024]{2,1,0:T(8,128)(2,1)S(1)}, u32[]{:S(2)}, u32[]{:S(2)}) collective-permute-start(bf16[6,32,1024]{2,1,0:T(8,128)(2,1)S(1)} %collective-permute-done.12.refs_2_), channel_id=1, source_target_pairs={{0,96},{32,0},{64,32},{96,64},{1,97},{33,1},{65,33},{97,65},{2,98}... | collective-permute-start | bytes 1179656 | tf_op jit(solution)/shard_map/gather_over_replicas/ppermute | solution.py:327
  118.5 2.2 %collective-permute-start.15 = (bf16[12,32,1024]{2,1,0:T(8,128)(2,1)S(1)}, bf16[12,32,1024]{2,1,0:T(8,128)(2,1)S(1)}, u32[]{:S(2)}, u32[]{:S(2)}) collective-permute-start(bf16[12,32,1024]{2,1,0:T(8,128)(2,1)S(1)} %pad_maximum_fusion), channel_id=1, source_target_pairs={{0,16},{16,0},{1,17},{17,1},{2,18},{18,2},{3,19},{19,3},{4,20},{20... | collective-permute-start | bytes 2359304 | tf_op jit(solution)/shard_map/gather_over_replicas/ppermute | solution.py:315
  120.7 2.0 %place_early.1.refs_9_ = bf16[48,64,1024]{2,1,0:T(8,128)(2,1)} custom-call(s32[3]{0:T(128)S(1)} %pad_add_fusion.place, bf16[12,32,1024]{2,1,0:T(8,128)(2,1)S(1)} %slice.63.refs_0_, bf16[12,32,1024]{2,1,0:T(8,128)(2,1)S(1)} %collective-permute-done.14.refs_1_, bf16[6,32,1024]{2,1,0:T(8,128)(2,1)S(1)} %collective-permute-done.12.refs_2_, ...), custom_call_target="tpu_custom_call" | custom-call | bytes 4718592 | tf_op jit(solution)/shard_map/gather_over_replicas/place_early/pallas_call | solution.py:302
  125.7 6.2 %collective-permute-done.21.refs_5_ = bf16[6,32,1024]{2,1,0:T(8,128)(2,1)S(1)} collective-permute-done((bf16[6,32,1024]{2,1,0:T(8,128)(2,1)S(1)}, bf16[6,32,1024]{2,1,0:T(8,128)(2,1)S(1)}, u32[]{:S(2)}, u32[]{:S(2)}) %collective-permute-start.21) | collective-permute-done | bytes 393248 | tf_op jit(solution)/shard_map/gather_over_replicas/ppermute | solution.py:327
  135.1 2.5 %place_late.1 = bf16[48,64,1024]{2,1,0:T(8,128)(2,1)} custom-call(s32[3]{0:T(128)S(1)} %pad_add_fusion.place, bf16[12,32,1024]{2,1,0:T(8,128)(2,1)S(1)} %collective-permute-done.15.refs_0_, bf16[6,32,1024]{2,1,0:T(8,128)(2,1)S(1)} %collective-permute-done.17.refs_1_, ...), custom_call_target="tpu_custom_call", output_to_operand_aliasing={{}: (10, {})} | custom-call | bytes 7864320 | tf_op jit(solution)/shard_map/gather_over_replicas/place_late/pallas_call | solution.py:302
  (57 shorter events, 20.9 us)
Async XLA Ops:
  1.2 5.7 %collective-permute-start = (bf16[12,32,1024]{2,1,0:T(8,128)(2,1)S(1)}, bf16[12,32,1024]{2,1,0:T(8,128)(2,1)S(1)}, u32[]{:S(2)}, u32[]{:S(2)}) collective-permute-start(bf16[12,32,1024]{2,1,0:T(8,128)(2,1)S(1)} %dynamic-slice_bitcast_fusion.7), channel_id=1, source_target_pairs={{0,16},{16,0},{1,17},{17,1},{2,18},{18,2},{3,19},{19,3},{4,20},{20... | collective-permute-start | bytes 2359304 | tf_op jit(solution)/shard_map/sum_over_replicas/ppermute | solution.py:206
  6.2 7.5 %collective-permute-start.4 = (bf16[12,32,1024]{2,1,0:T(8,128)(2,1)}, bf16[12,32,1024]{2,1,0:T(8,128)(2,1)}, u32[]{:S(2)}, u32[]{:S(2)}) collective-permute-start(bf16[12,32,1024]{2,1,0:T(8,128)(2,1)} %get-tuple-element.42), channel_id=1, source_target_pairs={{0,16},{16,0},{1,17},{17,1},{2,18},{18,2},{3,19},{19,3},{4,20},{20... | collective-permute-start | bytes 2359304 | tf_op jit(solution)/shard_map/sum_over_replicas/ppermute | solution.py:210
  6.3 22.2 %collective-permute-start.1 = (bf16[12,32,1024]{2,1,0:T(8,128)(2,1)S(1)}, bf16[12,32,1024]{2,1,0:T(8,128)(2,1)}, u32[]{:S(2)}, u32[]{:S(2)}) collective-permute-start(bf16[12,32,1024]{2,1,0:T(8,128)(2,1)S(1)} %get-tuple-element.38), channel_id=1, source_target_pairs={{0,16},{16,0},{1,17},{17,1},{2,18},{18,2},{3,19},{19,3},{4,20},{20... | collective-permute-start | bytes 2359304 | tf_op jit(solution)/shard_map/sum_over_replicas/ppermute | solution.py:210
  6.7 8.5 %collective-permute-start.2 = (bf16[12,32,1024]{2,1,0:T(8,128)(2,1)}, bf16[12,32,1024]{2,1,0:T(8,128)(2,1)}, u32[]{:S(2)}, u32[]{:S(2)}) collective-permute-start(bf16[12,32,1024]{2,1,0:T(8,128)(2,1)} %get-tuple-element.40), channel_id=1, source_target_pairs={{0,16},{16,0},{1,17},{17,1},{2,18},{18,2},{3,19},{19,3},{4,20},{20... | collective-permute-start | bytes 2359304 | tf_op jit(solution)/shard_map/sum_over_replicas/ppermute | solution.py:210
  8.0 16.5 %collective-permute-start.5 = (bf16[6,32,1024]{2,1,0:T(8,128)(2,1)S(1)}, bf16[6,32,1024]{2,1,0:T(8,128)(2,1)}, u32[]{:S(2)}, u32[]{:S(2)}) collective-permute-start(bf16[6,32,1024]{2,1,0:T(8,128)(2,1)S(1)} %get-tuple-element.43), channel_id=1, source_target_pairs={{0,96},{32,0},{64,32},{96,64},{1,97},{33,1},{65,33},{97,65},{2,98}... | collective-permute-start | bytes 1179656 | tf_op jit(solution)/shard_map/sum_over_replicas/ppermute | solution.py:215
  11.9 11.5 %collective-permute-start.8 = (bf16[6,32,1024]{2,1,0:T(8,128)(2,1)}, bf16[6,32,1024]{2,1,0:T(8,128)(2,1)}, u32[]{:S(2)}, u32[]{:S(2)}) collective-permute-start(bf16[6,32,1024]{2,1,0:T(8,128)(2,1)} %get-tuple-element.44), channel_id=1, source_target_pairs={{0,32},{32,64},{64,96},{96,0},{1,33},{33,65},{65,97},{97,1},{2,34}... | collective-permute-start | bytes 1179656 | tf_op jit(solution)/shard_map/sum_over_replicas/ppermute | solution.py:216
  18.0 13.7 %collective-permute-start.3 = (bf16[6,32,1024]{2,1,0:T(8,128)(2,1)S(1)}, bf16[6,32,1024]{2,1,0:T(8,128)(2,1)S(1)}, u32[]{:S(2)}, u32[]{:S(2)}) collective-permute-start(bf16[6,32,1024]{2,1,0:T(8,128)(2,1)S(1)} %slice.56), channel_id=1, source_target_pairs={{0,32},{32,64},{64,96},{96,0},{1,33},{33,65},{65,97},{97,1},{2,34}... | collective-permute-start | bytes 1179656 | tf_op jit(solution)/shard_map/sum_over_replicas/ppermute | solution.py:223
  18.1 13.6 %collective-permute-start.7 = (bf16[6,32,1024]{2,1,0:T(8,128)(2,1)S(1)}, bf16[6,32,1024]{2,1,0:T(8,128)(2,1)S(1)}, u32[]{:S(2)}, u32[]{:S(2)}) collective-permute-start(bf16[6,32,1024]{2,1,0:T(8,128)(2,1)S(1)} %slice.59), channel_id=1, source_target_pairs={{0,96},{32,0},{64,32},{96,64},{1,97},{33,1},{65,33},{97,65},{2,98}... | collective-permute-start | bytes 1179656 | tf_op jit(solution)/shard_map/sum_over_replicas/ppermute | solution.py:224
  24.5 15.6 %collective-permute-start.9 = (bf16[6,32,1024]{2,1,0:T(8,128)(2,1)S(1)}, bf16[6,32,1024]{2,1,0:T(8,128)(2,1)S(1)}, u32[]{:S(2)}, u32[]{:S(2)}) collective-permute-start(bf16[6,32,1024]{2,1,0:T(8,128)(2,1)S(1)} %add_convert_fusion.5), channel_id=1, source_target_pairs={{0,32},{32,64},{64,96},{96,0},{1,33},{33,65},{65,97},{97,1},{2,34}... | collective-permute-start | bytes 1179656 | tf_op jit(solution)/shard_map/sum_over_replicas/ppermute | solution.py:226
  25.7 14.4 %collective-permute-start.6 = (bf16[6,32,1024]{2,1,0:T(8,128)(2,1)S(1)}, bf16[6,32,1024]{2,1,0:T(8,128)(2,1)S(1)}, u32[]{:S(2)}, u32[]{:S(2)}) collective-permute-start(bf16[6,32,1024]{2,1,0:T(8,128)(2,1)S(1)} %add_convert_fusion.7), channel_id=1, source_target_pairs={{0,96},{32,0},{64,32},{96,64},{1,97},{33,1},{65,33},{97,65},{2,98}... | collective-permute-start | bytes 1179656 | tf_op jit(solution)/shard_map/sum_over_replicas/ppermute | solution.py:225
  62.7 5.1 %collective-permute-start.10 = (bf16[512,1024]{1,0:T(8,128)(2,1)S(1)}, bf16[512,1024]{1,0:T(8,128)(2,1)S(1)}, u32[]{:S(2)}, u32[]{:S(2)}) collective-permute-start(bf16[512,1024]{1,0:T(8,128)(2,1)S(1)} %bitcast.22), channel_id=1, source_target_pairs={{0,16},{16,0},{1,17},{17,1},{2,18},{18,2},{3,19},{19,3},{4,20},{20... | collective-permute-start | bytes 3145736 | tf_op jit(solution)/shard_map/rows_to_owner/ppermute | solution.py:243
  76.0 3.5 %collective-permute-start.11 = (bf16[3,512,512]{2,1,0:T(8,128)(2,1)S(1)}, bf16[3,512,512]{2,1,0:T(8,128)(2,1)S(1)}, u32[]{:S(2)}, u32[]{:S(2)}) collective-permute-start(bf16[3,512,512]{2,1,0:T(8,128)(2,1)S(1)} %get-tuple-element.48.root), channel_id=1, source_target_pairs={{0,16},{16,0},{1,17},{17,1},{2,18},{18,2},{3,19},{19,3},{4,20},{20... | collective-permute-start | bytes 4718600 | tf_op jit(solution)/shard_map/ppermute | solution.py:263
  102.1 13.9 %collective-permute-start.14 = (bf16[12,32,1024]{2,1,0:T(8,128)(2,1)S(1)}, bf16[12,32,1024]{2,1,0:T(8,128)(2,1)S(1)}, u32[]{:S(2)}, u32[]{:S(2)}) collective-permute-start(bf16[12,32,1024]{2,1,0:T(8,128)(2,1)S(1)} %slice.63.refs_0_), channel_id=1, source_target_pairs={{0,16},{16,0},{1,17},{17,1},{2,18},{18,2},{3,19},{19,3},{4,20},{20... | collective-permute-start | bytes 2359304 | tf_op jit(solution)/shard_map/gather_over_replicas/ppermute | solution.py:315
  104.1 12.0 %collective-permute-start.13 = (bf16[6,32,1024]{2,1,0:T(8,128)(2,1)S(1)}, bf16[6,32,1024]{2,1,0:T(8,128)(2,1)S(1)}, u32[]{:S(2)}, u32[]{:S(2)}) collective-permute-start(bf16[6,32,1024]{2,1,0:T(8,128)(2,1)S(1)} %get-tuple-element.54), channel_id=1, source_target_pairs={{0,32},{32,64},{64,96},{96,0},{1,33},{33,65},{65,97},{97,1},{2,34}... | collective-permute-start | bytes 1179656 | tf_op jit(solution)/shard_map/gather_over_replicas/ppermute | solution.py:319
  104.1 11.9 %collective-permute-start.12 = (bf16[6,32,1024]{2,1,0:T(8,128)(2,1)S(1)}, bf16[6,32,1024]{2,1,0:T(8,128)(2,1)S(1)}, u32[]{:S(2)}, u32[]{:S(2)}) collective-permute-start(bf16[6,32,1024]{2,1,0:T(8,128)(2,1)S(1)} %get-tuple-element.55), channel_id=1, source_target_pairs={{0,96},{32,0},{64,32},{96,64},{1,97},{33,1},{65,33},{97,65},{2,98}... | collective-permute-start | bytes 1179656 | tf_op jit(solution)/shard_map/gather_over_replicas/ppermute | solution.py:318
  108.2 15.2 %collective-permute-start.17 = (bf16[6,32,1024]{2,1,0:T(8,128)(2,1)S(1)}, bf16[6,32,1024]{2,1,0:T(8,128)(2,1)S(1)}, u32[]{:S(2)}, u32[]{:S(2)}) collective-permute-start(bf16[6,32,1024]{2,1,0:T(8,128)(2,1)S(1)} %get-tuple-element.54), channel_id=1, source_target_pairs={{0,96},{32,0},{64,32},{96,64},{1,97},{33,1},{65,33},{97,65},{2,98}... | collective-permute-start | bytes 1179656 | tf_op jit(solution)/shard_map/gather_over_replicas/ppermute | solution.py:322
  108.2 16.3 %collective-permute-start.18 = (bf16[6,32,1024]{2,1,0:T(8,128)(2,1)S(1)}, bf16[6,32,1024]{2,1,0:T(8,128)(2,1)S(1)}, u32[]{:S(2)}, u32[]{:S(2)}) collective-permute-start(bf16[6,32,1024]{2,1,0:T(8,128)(2,1)S(1)} %get-tuple-element.55), channel_id=1, source_target_pairs={{0,32},{32,64},{64,96},{96,0},{1,33},{33,65},{65,97},{97,1},{2,34}... | collective-permute-start | bytes 1179656 | tf_op jit(solution)/shard_map/gather_over_replicas/ppermute | solution.py:323
  116.1 15.8 %collective-permute-start.21 = (bf16[6,32,1024]{2,1,0:T(8,128)(2,1)S(1)}, bf16[6,32,1024]{2,1,0:T(8,128)(2,1)S(1)}, u32[]{:S(2)}, u32[]{:S(2)}) collective-permute-start(bf16[6,32,1024]{2,1,0:T(8,128)(2,1)S(1)} %collective-permute-done.12.refs_2_), channel_id=1, source_target_pairs={{0,96},{32,0},{64,32},{96,64},{1,97},{33,1},{65,33},{97,65},{2,98}... | collective-permute-start | bytes 1179656 | tf_op jit(solution)/shard_map/gather_over_replicas/ppermute | solution.py:327
  118.4 14.6 %collective-permute-start.22 = (bf16[6,32,1024]{2,1,0:T(8,128)(2,1)S(1)}, bf16[6,32,1024]{2,1,0:T(8,128)(2,1)S(1)}, u32[]{:S(2)}, u32[]{:S(2)}) collective-permute-start(bf16[6,32,1024]{2,1,0:T(8,128)(2,1)S(1)} %collective-permute-done.13.refs_3_), channel_id=1, source_target_pairs={{0,32},{32,64},{64,96},{96,0},{1,33},{33,65},{65,97},{97,1},{2,34}... | collective-permute-start | bytes 1179656 | tf_op jit(solution)/shard_map/gather_over_replicas/ppermute | solution.py:328
  118.5 16.6 %collective-permute-start.15 = (bf16[12,32,1024]{2,1,0:T(8,128)(2,1)S(1)}, bf16[12,32,1024]{2,1,0:T(8,128)(2,1)S(1)}, u32[]{:S(2)}, u32[]{:S(2)}) collective-permute-start(bf16[12,32,1024]{2,1,0:T(8,128)(2,1)S(1)} %pad_maximum_fusion), channel_id=1, source_target_pairs={{0,16},{16,0},{1,17},{17,1},{2,18},{18,2},{3,19},{19,3},{4,20},{20... | collective-permute-start | bytes 2359304 | tf_op jit(solution)/shard_map/gather_over_replicas/ppermute | solution.py:315
  124.5 9.2 %collective-permute-start.19 = (bf16[6,32,1024]{2,1,0:T(8,128)(2,1)S(1)}, bf16[6,32,1024]{2,1,0:T(8,128)(2,1)S(1)}, u32[]{:S(2)}, u32[]{:S(2)}) collective-permute-start(bf16[6,32,1024]{2,1,0:T(8,128)(2,1)S(1)} %collective-permute-done.17.refs_1_), channel_id=1, source_target_pairs={{0,16},{16,0},{1,17},{17,1},{2,18},{18,2},{3,19},{19,3},{4,20},{20... | collective-permute-start | bytes 1179656 | tf_op jit(solution)/shard_map/gather_over_replicas/ppermute | solution.py:315
  125.7 8.0 %collective-permute-start.20 = (bf16[6,32,1024]{2,1,0:T(8,128)(2,1)S(1)}, bf16[6,32,1024]{2,1,0:T(8,128)(2,1)S(1)}, u32[]{:S(2)}, u32[]{:S(2)}) collective-permute-start(bf16[6,32,1024]{2,1,0:T(8,128)(2,1)S(1)} %collective-permute-done.18.refs_2_), channel_id=1, source_target_pairs={{0,16},{16,0},{1,17},{17,1},{2,18},{18,2},{3,19},{19,3},{4,20},{20... | collective-permute-start | bytes 1179656 | tf_op jit(solution)/shard_map/gather_over_replicas/ppermute | solution.py:315
  131.9 2.5 %collective-permute-start.23 = (bf16[6,32,1024]{2,1,0:T(8,128)(2,1)S(1)}, bf16[6,32,1024]{2,1,0:T(8,128)(2,1)S(1)}, u32[]{:S(2)}, u32[]{:S(2)}) collective-permute-start(bf16[6,32,1024]{2,1,0:T(8,128)(2,1)S(1)} %collective-permute-done.21.refs_5_), channel_id=1, source_target_pairs={{0,16},{16,0},{1,17},{17,1},{2,18},{18,2},{3,19},{19,3},{4,20},{20... | collective-permute-start | bytes 1179656 | tf_op jit(solution)/shard_map/gather_over_replicas/ppermute | solution.py:315
  133.0 2.1 %collective-permute-start.24 = (bf16[6,32,1024]{2,1,0:T(8,128)(2,1)S(1)}, bf16[6,32,1024]{2,1,0:T(8,128)(2,1)S(1)}, u32[]{:S(2)}, u32[]{:S(2)}) collective-permute-start(bf16[6,32,1024]{2,1,0:T(8,128)(2,1)S(1)} %collective-permute-done.22.refs_6_), channel_id=1, source_target_pairs={{0,16},{16,0},{1,17},{17,1},{2,18},{18,2},{3,19},{19,3},{4,20},{20... | collective-permute-start | bytes 1179656 | tf_op jit(solution)/shard_map/gather_over_replicas/ppermute | solution.py:315
  (2 other events, 2.9 us)

commit v2 on v1

--- a/solution.py
+++ b/solution.py
@@ -9,6 +9,7 @@
 
 damping = 0.1
 mib = 2**20
+TILE = 256
 ROWS = ((0,), (0,))
 COLUMNS = ((1,), (1,))
 
@@ -21,67 +22,90 @@
     return pl.ds(pl.multiple_of(start, count), count)
 
 
-def root_kernel(place, own, sibling, root, grad, stat, step, square, coupled):
+def root_kernel(place, own, sibling, root, grad, stat, step, square, coupled, fourth):
     core = place[0]
     half, width = own.shape
     grad[rows_at(core * half, half), :] = own[...]
     grad[rows_at((1 - core) * half, half), :] = sibling[...]
-    low, high = slice(0, half), slice(half, width)
-    upper = ((low, low), (low, high), (high, high))
-    eye = lax.broadcasted_iota(jnp.int32, (half, half), 0) == lax.broadcasted_iota(
-        jnp.int32, (half, half), 1
+    count = width // TILE
+    tiles = [slice(i * TILE, (i + 1) * TILE) for i in range(count)]
+    tails = [slice(i * TILE, width) for i in range(count)]
+    eye = lax.broadcasted_iota(jnp.int32, (TILE, TILE), 0) == lax.broadcasted_iota(
+        jnp.int32, (TILE, TILE), 1
     )
 
+    def squares(value):
+        return jnp.sum(value * value, axis=0, keepdims=True)
+
+    def add_up(value):
+        return jnp.sum(value, axis=1, keepdims=True)
+
     def statistic(contract):
-        total = jnp.zeros((1, half), jnp.float32)
-        for r, c in upper:
+        total = jnp.zeros((1, 1), jnp.float32)
+        for i in range(count):
             if contract == ROWS:
-                product = dot(grad[:, r], grad[:, c], ROWS)
+                product = dot(grad[:, tiles[i]], grad[:, tails[i]], ROWS)
             else:
-                product = dot(grad[r, :], grad[c, :], COLUMNS)
+                product = dot(grad[tiles[i], :], grad[tails[i], :], COLUMNS)
             value = product * (1.0 / width)
-            if r == c:
-                value = value + jnp.where(eye, damping, 0.0)
-            stat[r, c] = value
-            squares = jnp.sum(value * value, axis=0, keepdims=True)
-            total = total + (squares if r == c else 2.0 * squares)
+            block = value[:, :TILE] + jnp.where(eye, damping, 0.0)
+            stat[tiles[i], tiles[i]] = block
+            total = total + add_up(squares(block))
+            if i + 1 < count:
+                stat[tiles[i], tails[i + 1]] = value[:, TILE:]
+                total = total + 2.0 * add_up(squares(value[:, TILE:]))
         return total
 
     total = lax.cond(core == 0, lambda: statistic(COLUMNS), lambda: statistic(ROWS))
-    inverse = 4.0 * lax.rsqrt(jnp.sum(total, axis=1, keepdims=True))
-    across, along = {}, {}
-    for r, c in upper:
-        matrix = (stat[r, c] * inverse).astype(jnp.bfloat16).astype(jnp.float32)
-        if r == c:
-            value = ((jnp.where(eye, 5.0, 0.0) - matrix) * 0.25).astype(jnp.bfloat16)
-            both = jnp.where(eye, 4.0 * value.astype(jnp.float32) + matrix, 0.0)
-            across[r.start] = jnp.sum(both, axis=0, keepdims=True)
-            along[r.start] = jnp.sum(both, axis=1, keepdims=True)
+    inverse = 4.0 * lax.rsqrt(total)
+
+    def rest(matrix, i):
+        if i + 1 < count:
+            matrix[tails[i + 1], tiles[i]] = matrix[tiles[i], tails[i + 1]].T
+
+    across, along = [], []
+    for i in range(count):
+        matrix = (stat[tiles[i], tails[i]] * inverse).astype(jnp.bfloat16).astype(jnp.float32)
+        block = matrix[:, :TILE]
+        value = ((jnp.where(eye, 5.0, 0.0) - block) * 0.25).astype(jnp.bfloat16)
+        both = jnp.where(eye, 4.0 * value.astype(jnp.float32) + block, 0.0)
+        across.append(jnp.sum(both, axis=0, keepdims=True))
+        along.append(jnp.sum(both, axis=1, keepdims=True))
+        step[tiles[i], tiles[i]] = value
+        if i + 1 < count:
+            step[tiles[i], tails[i + 1]] = (matrix[:, TILE:] * -0.25).astype(jnp.bfloat16)
+            rest(step, i)
+    across = jnp.concatenate(across, axis=1)
+    for i in range(count):
+        product = dot(step[tiles[i], :], step[:, tails[i]])
+        square[tiles[i], tails[i]] = product.astype(jnp.bfloat16)
+        rest(square, i)
+        value = step[tiles[i], tails[i]].astype(jnp.float32)
+        coupled[tiles[i], tails[i]] = (value * across[:, tails[i]] - 4.0 * product).astype(
+            jnp.bfloat16
+        )
+        if i + 1 < count:
+            below = value[:, TILE:] * along[i] - 4.0 * product[:, TILE:]
+            coupled[tails[i + 1], tiles[i]] = below.astype(jnp.bfloat16).T
+    for i in range(count):
+        product = dot(square[tiles[i], :], square[:, tails[i]])
+        fourth[tiles[i], tails[i]] = product.astype(jnp.bfloat16)
+        rest(fourth, i)
+    for i in range(count):
+        product = dot(fourth[tiles[i], :], coupled[:, tails[i]])
+        value = step[tiles[i], tails[i]].astype(jnp.float32)
+        value = ((5.0 * value - product) * 0.25).astype(jnp.bfloat16)
+        start = i * TILE
+        if start < half:
+            root[0, tiles[i], start:half] = value[:, : half - start]
+            root[1, tiles[i], :] = value[:, half - start :]
+            if start + TILE < half:
+                root[0, start + TILE : half, tiles[i]] = value[:, TILE : half - start].T
         else:
-            value = (matrix * -0.25).astype(jnp.bfloat16)
-        step[r, c] = value
-
-    def times_itself(matrix):
-        one, two, three = (matrix[block] for block in upper)
-        yield upper[0], dot(one, one) + dot(two, two, COLUMNS)
-        yield upper[1], dot(one, two) + dot(two, three)
-        yield upper[2], dot(two, two, ROWS) + dot(three, three)
-
-    for (r, c), product in times_itself(step):
-        square[r, c] = product.astype(jnp.bfloat16)
-        value = step[r, c].astype(jnp.float32)
-        coupled[r, c] = (value * across[c.start] - 4.0 * product).astype(jnp.bfloat16)
-        if r != c:
-            coupled[high, low] = (value * along[r.start] - 4.0 * product).astype(jnp.bfloat16)
-    one, two, three = (product.astype(jnp.bfloat16) for _, product in times_itself(square))
-    products = (
-        dot(one, coupled[low, low]) + dot(two, coupled[high, low], COLUMNS),
-        dot(one, coupled[low, high]) + dot(two, coupled[high, high]),
-        dot(two, coupled[low, high], ROWS) + dot(three, coupled[high, high]),
-    )
-    for (r, c), product in zip(upper, products):
-        value = ((5.0 * step[r, c].astype(jnp.float32) - product) * 0.25).astype(jnp.bfloat16)
-        root[upper.index((r, c))] = value
+            rows, columns = slice(start - half, start - half + TILE), slice(start - half, half)
+            root[2, rows, columns] = value
+            if start + TILE < width:
+                root[2, start - half + TILE : half, rows] = value[:, TILE:].T
 
 
 def from_left(root, matrix, write):
@@ -124,16 +148,21 @@
 
     def write(rows, columns, product):
         raw[rows, columns] = product
-
-    @pl.when(core == 0)
-    def _():
+        square = jnp.sum(product * product, axis=0, keepdims=True)
+        sums.append(jnp.sum(square, axis=1, keepdims=True))
+
+    def left():
+        sums.clear()
+        from_left(root, side, write)
+        return sums[0] + sums[1]
+
+    def right():
+        sums.clear()
         from_right(side, root, write)
-
-    @pl.when(core == 1)
-    def _():
-        from_left(root, side, write)
-
-    raw_sum = jnp.sum(raw[...] * raw[...], axis=0, keepdims=True)
+        return sums[0] + sums[1]
+
+    sums = []
+    raw_sum = lax.cond(core == 0, right, left)
     scale = 1.0 / (width * width)
     grad_mean = jnp.sum(grad_sum[...], axis=1, keepdims=True) * scale
     raw_mean = jnp.sum(raw_sum, axis=1, keepdims=True) * scale
@@ -209,9 +238,7 @@
         )
         got_above, got_below, got_mine = (lax.ppermute(each, "core", swap) for each in sent)
         far = plus(kept, got)
-        far_low, far_high, here, owners = lax.optimization_barrier(
-            (far[:part], far[part:], plane, owned_block)
-        )
+        far_low, far_high, here = lax.optimization_barrier((far[:part], far[part:], plane))
         from_above = lax.ppermute(far_low, "z", down)
         from_below = lax.ppermute(far_high, "z", up)
         kept_above, kept_below, kept_mine = lax.optimization_barrier(
@@ -222,6 +249,7 @@
         mine = plus(kept_mine, got_mine)
         low_below = lax.ppermute(to_above[:part], "z", up)
         high_above = lax.ppermute(to_below[part:], "z", down)
+        low_below, owners = lax.optimization_barrier((low_below, owned_block))
         low_above = lax.ppermute(plus(to_below[:part], from_above), "z", down)
         high_below = lax.ppermute(plus(to_above[part:], from_below), "z", up)
         summed = jnp.concatenate(
@@ -252,10 +280,8 @@
         out_specs=[vmem, vmem],
         scratch_shapes=[
             pltpu.VMEM(square, jnp.float32),
-            pltpu.VMEM(square, jnp.bfloat16),
-            pltpu.VMEM(square, jnp.bfloat16),
-            pltpu.VMEM(square, jnp.bfloat16),
-        ],
+        ]
+        + [pltpu.VMEM(square, jnp.bfloat16)] * 4,
         compiler_params=pltpu.CompilerParams(vmem_limit_bytes=40 * mib),
         cost_estimate=pl.CostEstimate(flops=3 * work, bytes_accessed=6 * mib, transcendentals=0),
         name="inverse_root",

time: 138 us -> 137 us (level)
  other arithmetic: 8.23 us -> 10.9 us
  waiting for transfers between devices: 31.5 us -> 30 us
  Pallas kernels: 19.2 us -> 17.8 us
    convert_element_type x7, other arithmetic: 7.31 us -> 9.97 us  [plus(): return total.astype(jnp.bfloat16)]
  transfers between devices with their start and end apart: 25 -> 25, of which waited for: 11 -> 12; matrix products, arithmetic and copies ran while one was open for 10% -> 11% of each run, Pallas kernels for 4% -> 4%
where the time goes in v2:
time: 137 us; the launch traced here: 136 us
  blocking collectives  41 us (30%)
  waiting for transfers between devices  30 us (22%)
  starting transfers between devices  29.1 us (21%)
  Pallas kernels  17.8 us (13%)
  other arithmetic  10.9 us (8%)
  local copies, waits for them, and re-layouts  6.38 us (5%)
    all_to_all x1, blocking collectives, local(): lax.all_to_all(summed, ('y', 'x'), 0, 0, tiled=True).reshape(half, width)  22 us
    all_to_all x1, blocking collectives, local(): lax.all_to_all(finished.reshape(shards, rows, width), ('y', 'x'), 0, 0, t...  19 us
    convert_element_type x7, other arithmetic, plus(): return total.astype(jnp.bfloat16)  9.97 us
    ppermute x7, starting transfers between devices, other_core(): return lax.ppermute(piece, 'core', swap)  7.65 us
    pallas_call x1, Pallas kernels, local(): pl.pallas_call(root_kernel, out_shape=[jax.ShapeDtypeStruct((3, half, hal...  7.13 us
    ppermute x1, waiting for transfers between devices, local(): high_below = lax.ppermute(plus(to_above[part:], from_below), 'z', up)  7.06 us
    ppermute x1, waiting for transfers between devices, local(): below_high = lax.ppermute(back[part:], 'z', up)  6.39 us
    ppermute x1, waiting for transfers between devices, local(): far_low = lax.ppermute(above_low, 'z', down)  6.17 us
  transfers between devices with their start and end apart: 25, of which 12 were waited for; matrix products, arithmetic and copies ran while one was open for 11% of the time, Pallas kernels for 4%

profile of v2, /device:TPU:1, one launch (start us, length us, event | category | flops | bytes accessed | tf_op | source)
XLA Modules:
  0.0 136.3 jit_solution(9910880009569458946)
XLA Ops:
  0.0 2.1 %dynamic-slice_bitcast_fusion.7 = bf16[12,32,1024]{2,1,0:T(8,128)(2,1)} fusion(bf16[4,12,2,32,1024]{4,3,2,1,0:T(8,128)(2,1)} %bitcast.26, s32[]{:T(128)S(6)} %select_n.72, s32[]{:T(128)S(6)} %select_n.73), kind=kLoop, calls=%fused_computation.17 | loop fusion | bytes 1572872 | tf_op jit(solution)/shard_map/sum_over_replicas/reshape | solution.py:231
  3.5 2.2 %dynamic-slice_bitcast_fusion.3 = (bf16[12,32,1024]{2,1,0:T(8,128)(2,1)S(1)}, bf16[12,32,1024]{2,1,0:T(8,128)(2,1)S(1)}, bf16[12,32,1024]{2,1,0:T(8,128)(2,1)S(1)}, bf16[12,32,1024]{2,1,0:T(8,128)(2,1)S(1)}) fusion(bf16[4,12,2,32,1024]{4,3,2,1,0:T(8,128)(2,1)} %bitcast.27, s32[]{:T(128)S(6)} %select_n.82, s32[]{:T(128)S(6)} %select_n.73, s32[]{:T(128)S(6)} %select_n.80, ...), kind=kLoop, calls=%fused_computation.13 | loop fusion | bytes 6291480 | tf_op jit(solution)/shard_map/sum_over_replicas/reshape | solution.py:231
  8.0 3.9 %collective-permute-start.5 = (bf16[6,32,1024]{2,1,0:T(8,128)(2,1)S(1)}, bf16[6,32,1024]{2,1,0:T(8,128)(2,1)}, u32[]{:S(2)}, u32[]{:S(2)}) collective-permute-start(bf16[6,32,1024]{2,1,0:T(8,128)(2,1)S(1)} %get-tuple-element.45), channel_id=1, source_target_pairs={{0,96},{32,0},{64,32},{96,64},{1,97},{33,1},{65,33},{97,65},{2,98}... | collective-permute-start | bytes 1179656 | tf_op jit(solution)/shard_map/sum_over_replicas/ppermute | solution.py:242
  16.8 2.7 %collective-permute-start.7 = (bf16[6,32,1024]{2,1,0:T(8,128)(2,1)S(1)}, bf16[6,32,1024]{2,1,0:T(8,128)(2,1)S(1)}, u32[]{:S(2)}, u32[]{:S(2)}) collective-permute-start(bf16[6,32,1024]{2,1,0:T(8,128)(2,1)S(1)} %slice.59), channel_id=1, source_target_pairs={{0,96},{32,0},{64,32},{96,64},{1,97},{33,1},{65,33},{97,65},{2,98}... | collective-permute-start | bytes 1179656 | tf_op jit(solution)/shard_map/sum_over_replicas/ppermute | solution.py:251
  19.6 3.6 %collective-permute-done.8 = bf16[6,32,1024]{2,1,0:T(8,128)(2,1)} collective-permute-done((bf16[6,32,1024]{2,1,0:T(8,128)(2,1)S(1)}, bf16[6,32,1024]{2,1,0:T(8,128)(2,1)}, u32[]{:S(2)}, u32[]{:S(2)}) %collective-permute-start.8) | collective-permute-done | bytes 393248 | tf_op jit(solution)/shard_map/sum_over_replicas/ppermute | solution.py:243
  23.2 1.9 %add_convert_fusion.5 = bf16[6,32,1024]{2,1,0:T(8,128)(2,1)} fusion(bf16[6,32,1024]{2,1,0:T(8,128)(2,1)} %collective-permute-done.8, bf16[12,32,1024]{2,1,0:T(8,128)(2,1)S(1)} %add_convert_fusion.1), kind=kLoop, calls=%fused_computation.7 | loop fusion | flops 786432 | bytes 1179648 | tf_op jit(solution)/shard_map/sum_over_replicas/convert_element_type | solution.py:220
  25.1 1.9 %add_convert_fusion.7 = bf16[6,32,1024]{2,1,0:T(8,128)(2,1)} fusion(bf16[6,32,1024]{2,1,0:T(8,128)(2,1)} %collective-permute-done.5, bf16[12,32,1024]{2,1,0:T(8,128)(2,1)S(1)} %add_convert_fusion), kind=kLoop, calls=%fused_computation.9 | loop fusion | flops 786432 | bytes 1179648 | tf_op jit(solution)/shard_map/sum_over_replicas/convert_element_type | solution.py:220
  27.0 2.7 %collective-permute-start.6 = (bf16[6,32,1024]{2,1,0:T(8,128)(2,1)}, bf16[6,32,1024]{2,1,0:T(8,128)(2,1)S(1)}, u32[]{:S(2)}, u32[]{:S(2)}) collective-permute-start(bf16[6,32,1024]{2,1,0:T(8,128)(2,1)} %add_convert_fusion.7), channel_id=1, source_target_pairs={{0,96},{32,0},{64,32},{96,64},{1,97},{33,1},{65,33},{97,65},{2,98}... | collective-permute-start | bytes 1179656 | tf_op jit(solution)/shard_map/sum_over_replicas/ppermute | solution.py:253
  32.9 7.1 %collective-permute-done.9 = bf16[6,32,1024]{2,1,0:T(8,128)(2,1)S(1)} collective-permute-done((bf16[6,32,1024]{2,1,0:T(8,128)(2,1)}, bf16[6,32,1024]{2,1,0:T(8,128)(2,1)S(1)}, u32[]{:S(2)}, u32[]{:S(2)}) %collective-permute-start.9) | collective-permute-done | bytes 393248 | tf_op jit(solution)/shard_map/sum_over_replicas/ppermute | solution.py:254
  40.6 22.0 %all_to_all.10 = bf16[16,32,1024]{2,1,0:T(8,128)(2,1)S(1)} all-to-all(bf16[16,32,1024]{2,1,0:T(8,128)(2,1)S(1)} %maximum_maximum_fusion), channel_id=1, replica_groups=mesh['z'=4,'core'=2,'y'=4,'x'=4] {'y','x'}, dimensions={0} | all-to-all | bytes 2097152 | tf_op jit(solution)/shard_map/rows_to_owner/all_to_all | solution.py:270
  62.5 2.8 %collective-permute-start.10 = (bf16[512,1024]{1,0:T(8,128)(2,1)S(1)}, bf16[512,1024]{1,0:T(8,128)(2,1)S(1)}, u32[]{:S(2)}, u32[]{:S(2)}) collective-permute-start(bf16[512,1024]{1,0:T(8,128)(2,1)S(1)} %bitcast.22), channel_id=1, source_target_pairs={{0,16},{16,0},{1,17},{17,1},{2,18},{18,2},{3,19},{19,3},{4,20},{20... | collective-permute-start | bytes 3145736 | tf_op jit(solution)/shard_map/rows_to_owner/ppermute | solution.py:271
  65.3 2.3 %collective-permute-done.10.sibling = bf16[512,1024]{1,0:T(8,128)(2,1)S(1)} collective-permute-done((bf16[512,1024]{1,0:T(8,128)(2,1)S(1)}, bf16[512,1024]{1,0:T(8,128)(2,1)S(1)}, u32[]{:S(2)}, u32[]{:S(2)}) %collective-permute-start.10) | collective-permute-done | bytes 1048608 | tf_op jit(solution)/shard_map/rows_to_owner/ppermute | solution.py:271
  67.6 7.1 %inverse_root.1 = (bf16[3,512,512]{2,1,0:T(8,128)(2,1)S(1)}, bf16[1024,1024]{1,0:T(8,128)(2,1)S(1)}) custom-call(s32[3]{0:T(128)S(1)} %pad_add_fusion.place, bf16[512,1024]{1,0:T(8,128)(2,1)S(1)} %bitcast.23, bf16[512,1024]{1,0:T(8,128)(2,1)S(1)} %collective-permute-done.10.sibling), custom_call_target="tpu_custom_call" | custom-call | flops 6442450944 | bytes 6291456 | tf_op jit(solution)/shard_map/inverse_root/pallas_call | solution.py:276
  75.1 3.0 %apply_own_root.1 = (bf16[1024,1024]{1,0:T(8,128)(2,1)S(1)}, f32[1,1024]{1,0:T(1,128)S(1)}) custom-call(s32[3]{0:T(128)S(1)} %pad_add_fusion.place, bf16[3,512,512]{2,1,0:T(8,128)(2,1)S(1)} %get-tuple-element.50.root, bf16[1024,1024]{1,0:T(8,128)(2,1)S(1)} %get-tuple-element.51.grad), custom_call_target="tpu_custom_call" | custom-call | flops 2147483648 | bytes 6291456 | tf_op jit(solution)/shard_map/apply_own_root/pallas_call | solution.py:290
  78.2 3.1 %apply_other_root.1 = bf16[512,1024]{1,0:T(8,128)(2,1)S(1)} custom-call(s32[3]{0:T(128)S(1)} %pad_add_fusion.place, bf16[512,1024]{1,0:T(8,128)(2,1)S(1)} %bitcast.24, bf16[1024,1024]{1,0:T(8,128)(2,1)S(1)} %get-tuple-element.52.side, bf16[3,512,512]{2,1,0:T(8,128)(2,1)S(1)} %collective-permute-done.11.root, f32[1,1024]{1,0:T(1,128)S(1)} %get-tuple-element.53.grad_sum), custom_call_target="tpu_custom_call" | custom-call | flops 2147483648 | bytes 6291456 | tf_op jit(solution)/shard_map/apply_other_root/pallas_call | solution.py:299
  81.4 19.0 %all_to_all.11 = bf16[16,32,1024]{2,1,0:T(8,128)(2,1)S(1)} all-to-all(bf16[16,32,1024]{2,1,0:T(8,128)(2,1)S(1)} %bitcast.25), channel_id=1, replica_groups=mesh['z'=4,'core'=2,'y'=4,'x'=4] {'y','x'}, dimensions={0} | all-to-all | bytes 2097152 | tf_op jit(solution)/shard_map/rows_to_shards/all_to_all | solution.py:311
  100.4 1.8 %collective-permute-start.14 = (bf16[12,32,1024]{2,1,0:T(8,128)(2,1)S(1)}, bf16[12,32,1024]{2,1,0:T(8,128)(2,1)S(1)}, u32[]{:S(2)}, u32[]{:S(2)}) collective-permute-start(bf16[12,32,1024]{2,1,0:T(8,128)(2,1)S(1)} %slice.63.refs_0_), channel_id=1, source_target_pairs={{0,16},{16,0},{1,17},{17,1},{2,18},{18,2},{3,19},{19,3},{4,20},{20... | collective-permute-start | bytes 2359304 | tf_op jit(solution)/shard_map/gather_over_replicas/ppermute | solution.py:341
  102.6 2.7 %collective-permute-start.12 = (bf16[6,32,1024]{2,1,0:T(8,128)(2,1)S(1)}, bf16[6,32,1024]{2,1,0:T(8,128)(2,1)S(1)}, u32[]{:S(2)}, u32[]{:S(2)}) collective-permute-start(bf16[6,32,1024]{2,1,0:T(8,128)(2,1)S(1)} %get-tuple-element.57), channel_id=1, source_target_pairs={{0,96},{32,0},{64,32},{96,64},{1,97},{33,1},{65,33},{97,65},{2,98}... | collective-permute-start | bytes 1179656 | tf_op jit(solution)/shard_map/gather_over_replicas/ppermute | solution.py:344
  108.2 6.4 %collective-permute-done.13.refs_3_ = bf16[6,32,1024]{2,1,0:T(8,128)(2,1)S(1)} collective-permute-done((bf16[6,32,1024]{2,1,0:T(8,128)(2,1)S(1)}, bf16[6,32,1024]{2,1,0:T(8,128)(2,1)S(1)}, u32[]{:S(2)}, u32[]{:S(2)}) %collective-permute-start.13) | collective-permute-done | bytes 393248 | tf_op jit(solution)/shard_map/gather_over_replicas/ppermute | solution.py:345
  114.6 2.4 %collective-permute-start.21 = (bf16[6,32,1024]{2,1,0:T(8,128)(2,1)S(1)}, bf16[6,32,1024]{2,1,0:T(8,128)(2,1)S(1)}, u32[]{:S(2)}, u32[]{:S(2)}) collective-permute-start(bf16[6,32,1024]{2,1,0:T(8,128)(2,1)S(1)} %collective-permute-done.12.refs_2_), channel_id=1, source_target_pairs={{0,96},{32,0},{64,32},{96,64},{1,97},{33,1},{65,33},{97,65},{2,98}... | collective-permute-start | bytes 1179656 | tf_op jit(solution)/shard_map/gather_over_replicas/ppermute | solution.py:353
  117.0 2.2 %collective-permute-start.15 = (bf16[12,32,1024]{2,1,0:T(8,128)(2,1)S(1)}, bf16[12,32,1024]{2,1,0:T(8,128)(2,1)S(1)}, u32[]{:S(2)}, u32[]{:S(2)}) collective-permute-start(bf16[12,32,1024]{2,1,0:T(8,128)(2,1)S(1)} %pad_maximum_fusion), channel_id=1, source_target_pairs={{0,16},{16,0},{1,17},{17,1},{2,18},{18,2},{3,19},{19,3},{4,20},{20... | collective-permute-start | bytes 2359304 | tf_op jit(solution)/shard_map/gather_over_replicas/ppermute | solution.py:341
  119.2 2.0 %place_early.1.refs_9_ = bf16[48,64,1024]{2,1,0:T(8,128)(2,1)} custom-call(s32[3]{0:T(128)S(1)} %pad_add_fusion.place, bf16[12,32,1024]{2,1,0:T(8,128)(2,1)S(1)} %slice.63.refs_0_, bf16[12,32,1024]{2,1,0:T(8,128)(2,1)S(1)} %collective-permute-done.14.refs_1_, bf16[6,32,1024]{2,1,0:T(8,128)(2,1)S(1)} %collective-permute-done.12.refs_2_, ...), custom_call_target="tpu_custom_call" | custom-call | bytes 4718592 | tf_op jit(solution)/shard_map/gather_over_replicas/place_early/pallas_call | solution.py:328
  124.2 6.2 %collective-permute-done.21.refs_5_ = bf16[6,32,1024]{2,1,0:T(8,128)(2,1)S(1)} collective-permute-done((bf16[6,32,1024]{2,1,0:T(8,128)(2,1)S(1)}, bf16[6,32,1024]{2,1,0:T(8,128)(2,1)S(1)}, u32[]{:S(2)}, u32[]{:S(2)}) %collective-permute-start.21) | collective-permute-done | bytes 393248 | tf_op jit(solution)/shard_map/gather_over_replicas/ppermute | solution.py:353
  133.6 2.5 %place_late.1 = bf16[48,64,1024]{2,1,0:T(8,128)(2,1)} custom-call(s32[3]{0:T(128)S(1)} %pad_add_fusion.place, bf16[12,32,1024]{2,1,0:T(8,128)(2,1)S(1)} %collective-permute-done.15.refs_0_, bf16[6,32,1024]{2,1,0:T(8,128)(2,1)S(1)} %collective-permute-done.17.refs_1_, ...), custom_call_target="tpu_custom_call", output_to_operand_aliasing={{}: (10, {})} | custom-call | bytes 7864320 | tf_op jit(solution)/shard_map/gather_over_replicas/place_late/pallas_call | solution.py:328
  (57 shorter events, 21.7 us)
Async XLA Ops:
  2.1 4.4 %collective-permute-start = (bf16[12,32,1024]{2,1,0:T(8,128)(2,1)}, bf16[12,32,1024]{2,1,0:T(8,128)(2,1)}, u32[]{:S(2)}, u32[]{:S(2)}) collective-permute-start(bf16[12,32,1024]{2,1,0:T(8,128)(2,1)} %dynamic-slice_bitcast_fusion.7), channel_id=1, source_target_pairs={{0,16},{16,0},{1,17},{17,1},{2,18},{18,2},{3,19},{19,3},{4,20},{20... | collective-permute-start | bytes 2359304 | tf_op jit(solution)/shard_map/sum_over_replicas/ppermute | solution.py:235
  5.7 8.0 %collective-permute-start.4 = (bf16[12,32,1024]{2,1,0:T(8,128)(2,1)S(1)}, bf16[12,32,1024]{2,1,0:T(8,128)(2,1)}, u32[]{:S(2)}, u32[]{:S(2)}) collective-permute-start(bf16[12,32,1024]{2,1,0:T(8,128)(2,1)S(1)} %get-tuple-element.44), channel_id=1, source_target_pairs={{0,16},{16,0},{1,17},{17,1},{2,18},{18,2},{3,19},{19,3},{4,20},{20... | collective-permute-start | bytes 2359304 | tf_op jit(solution)/shard_map/sum_over_replicas/ppermute | solution.py:239
  5.8 23.9 %collective-permute-start.1 = (bf16[12,32,1024]{2,1,0:T(8,128)(2,1)S(1)}, bf16[12,32,1024]{2,1,0:T(8,128)(2,1)}, u32[]{:S(2)}, u32[]{:S(2)}) collective-permute-start(bf16[12,32,1024]{2,1,0:T(8,128)(2,1)S(1)} %get-tuple-element.39), channel_id=1, source_target_pairs={{0,16},{16,0},{1,17},{17,1},{2,18},{18,2},{3,19},{19,3},{4,20},{20... | collective-permute-start | bytes 2359304 | tf_op jit(solution)/shard_map/sum_over_replicas/ppermute | solution.py:239
  6.3 8.9 %collective-permute-start.2 = (bf16[12,32,1024]{2,1,0:T(8,128)(2,1)S(1)}, bf16[12,32,1024]{2,1,0:T(8,128)(2,1)}, u32[]{:S(2)}, u32[]{:S(2)}) collective-permute-start(bf16[12,32,1024]{2,1,0:T(8,128)(2,1)S(1)} %get-tuple-element.41), channel_id=1, source_target_pairs={{0,16},{16,0},{1,17},{17,1},{2,18},{18,2},{3,19},{19,3},{4,20},{20... | collective-permute-start | bytes 2359304 | tf_op jit(solution)/shard_map/sum_over_replicas/ppermute | solution.py:239
  8.0 17.1 %collective-permute-start.5 = (bf16[6,32,1024]{2,1,0:T(8,128)(2,1)S(1)}, bf16[6,32,1024]{2,1,0:T(8,128)(2,1)}, u32[]{:S(2)}, u32[]{:S(2)}) collective-permute-start(bf16[6,32,1024]{2,1,0:T(8,128)(2,1)S(1)} %get-tuple-element.45), channel_id=1, source_target_pairs={{0,96},{32,0},{64,32},{96,64},{1,97},{33,1},{65,33},{97,65},{2,98}... | collective-permute-start | bytes 1179656 | tf_op jit(solution)/shard_map/sum_over_replicas/ppermute | solution.py:242
  11.9 11.3 %collective-permute-start.8 = (bf16[6,32,1024]{2,1,0:T(8,128)(2,1)S(1)}, bf16[6,32,1024]{2,1,0:T(8,128)(2,1)}, u32[]{:S(2)}, u32[]{:S(2)}) collective-permute-start(bf16[6,32,1024]{2,1,0:T(8,128)(2,1)S(1)} %get-tuple-element.46), channel_id=1, source_target_pairs={{0,32},{32,64},{64,96},{96,0},{1,33},{33,65},{65,97},{97,1},{2,34}... | collective-permute-start | bytes 1179656 | tf_op jit(solution)/shard_map/sum_over_replicas/ppermute | solution.py:243
  16.7 14.8 %collective-permute-start.3 = (bf16[6,32,1024]{2,1,0:T(8,128)(2,1)S(1)}, bf16[6,32,1024]{2,1,0:T(8,128)(2,1)S(1)}, u32[]{:S(2)}, u32[]{:S(2)}) collective-permute-start(bf16[6,32,1024]{2,1,0:T(8,128)(2,1)S(1)} %slice.56), channel_id=1, source_target_pairs={{0,32},{32,64},{64,96},{96,0},{1,33},{33,65},{65,97},{97,1},{2,34}... | collective-permute-start | bytes 1179656 | tf_op jit(solution)/shard_map/sum_over_replicas/ppermute | solution.py:250
  16.8 16.1 %collective-permute-start.7 = (bf16[6,32,1024]{2,1,0:T(8,128)(2,1)S(1)}, bf16[6,32,1024]{2,1,0:T(8,128)(2,1)S(1)}, u32[]{:S(2)}, u32[]{:S(2)}) collective-permute-start(bf16[6,32,1024]{2,1,0:T(8,128)(2,1)S(1)} %slice.59), channel_id=1, source_target_pairs={{0,96},{32,0},{64,32},{96,64},{1,97},{33,1},{65,33},{97,65},{2,98}... | collective-permute-start | bytes 1179656 | tf_op jit(solution)/shard_map/sum_over_replicas/ppermute | solution.py:251
  25.1 14.9 %collective-permute-start.9 = (bf16[6,32,1024]{2,1,0:T(8,128)(2,1)}, bf16[6,32,1024]{2,1,0:T(8,128)(2,1)S(1)}, u32[]{:S(2)}, u32[]{:S(2)}) collective-permute-start(bf16[6,32,1024]{2,1,0:T(8,128)(2,1)} %add_convert_fusion.5), channel_id=1, source_target_pairs={{0,32},{32,64},{64,96},{96,0},{1,33},{33,65},{65,97},{97,1},{2,34}... | collective-permute-start | bytes 1179656 | tf_op jit(solution)/shard_map/sum_over_replicas/ppermute | solution.py:254
  27.0 13.0 %collective-permute-start.6 = (bf16[6,32,1024]{2,1,0:T(8,128)(2,1)}, bf16[6,32,1024]{2,1,0:T(8,128)(2,1)S(1)}, u32[]{:S(2)}, u32[]{:S(2)}) collective-permute-start(bf16[6,32,1024]{2,1,0:T(8,128)(2,1)} %add_convert_fusion.7), channel_id=1, source_target_pairs={{0,96},{32,0},{64,32},{96,64},{1,97},{33,1},{65,33},{97,65},{2,98}... | collective-permute-start | bytes 1179656 | tf_op jit(solution)/shard_map/sum_over_replicas/ppermute | solution.py:253
  62.5 5.1 %collective-permute-start.10 = (bf16[512,1024]{1,0:T(8,128)(2,1)S(1)}, bf16[512,1024]{1,0:T(8,128)(2,1)S(1)}, u32[]{:S(2)}, u32[]{:S(2)}) collective-permute-start(bf16[512,1024]{1,0:T(8,128)(2,1)S(1)} %bitcast.22), channel_id=1, source_target_pairs={{0,16},{16,0},{1,17},{17,1},{2,18},{18,2},{3,19},{19,3},{4,20},{20... | collective-permute-start | bytes 3145736 | tf_op jit(solution)/shard_map/rows_to_owner/ppermute | solution.py:271
  74.7 3.5 %collective-permute-start.11 = (bf16[3,512,512]{2,1,0:T(8,128)(2,1)S(1)}, bf16[3,512,512]{2,1,0:T(8,128)(2,1)S(1)}, u32[]{:S(2)}, u32[]{:S(2)}) collective-permute-start(bf16[3,512,512]{2,1,0:T(8,128)(2,1)S(1)} %get-tuple-element.50.root), channel_id=1, source_target_pairs={{0,16},{16,0},{1,17},{17,1},{2,18},{18,2},{3,19},{19,3},{4,20},{20... | collective-permute-start | bytes 4718600 | tf_op jit(solution)/shard_map/ppermute | solution.py:289
  100.4 14.1 %collective-permute-start.14 = (bf16[12,32,1024]{2,1,0:T(8,128)(2,1)S(1)}, bf16[12,32,1024]{2,1,0:T(8,128)(2,1)S(1)}, u32[]{:S(2)}, u32[]{:S(2)}) collective-permute-start(bf16[12,32,1024]{2,1,0:T(8,128)(2,1)S(1)} %slice.63.refs_0_), channel_id=1, source_target_pairs={{0,16},{16,0},{1,17},{17,1},{2,18},{18,2},{3,19},{19,3},{4,20},{20... | collective-permute-start | bytes 2359304 | tf_op jit(solution)/shard_map/gather_over_replicas/ppermute | solution.py:341
  102.3 12.2 %collective-permute-start.13 = (bf16[6,32,1024]{2,1,0:T(8,128)(2,1)S(1)}, bf16[6,32,1024]{2,1,0:T(8,128)(2,1)S(1)}, u32[]{:S(2)}, u32[]{:S(2)}) collective-permute-start(bf16[6,32,1024]{2,1,0:T(8,128)(2,1)S(1)} %get-tuple-element.56), channel_id=1, source_target_pairs={{0,32},{32,64},{64,96},{96,0},{1,33},{33,65},{65,97},{97,1},{2,34}... | collective-permute-start | bytes 1179656 | tf_op jit(solution)/shard_map/gather_over_replicas/ppermute | solution.py:345
  102.6 11.9 %collective-permute-start.12 = (bf16[6,32,1024]{2,1,0:T(8,128)(2,1)S(1)}, bf16[6,32,1024]{2,1,0:T(8,128)(2,1)S(1)}, u32[]{:S(2)}, u32[]{:S(2)}) collective-permute-start(bf16[6,32,1024]{2,1,0:T(8,128)(2,1)S(1)} %get-tuple-element.57), channel_id=1, source_target_pairs={{0,96},{32,0},{64,32},{96,64},{1,97},{33,1},{65,33},{97,65},{2,98}... | collective-permute-start | bytes 1179656 | tf_op jit(solution)/shard_map/gather_over_replicas/ppermute | solution.py:344
  106.7 15.2 %collective-permute-start.17 = (bf16[6,32,1024]{2,1,0:T(8,128)(2,1)S(1)}, bf16[6,32,1024]{2,1,0:T(8,128)(2,1)S(1)}, u32[]{:S(2)}, u32[]{:S(2)}) collective-permute-start(bf16[6,32,1024]{2,1,0:T(8,128)(2,1)S(1)} %get-tuple-element.56), channel_id=1, source_target_pairs={{0,96},{32,0},{64,32},{96,64},{1,97},{33,1},{65,33},{97,65},{2,98}... | collective-permute-start | bytes 1179656 | tf_op jit(solution)/shard_map/gather_over_replicas/ppermute | solution.py:348
  106.7 16.3 %collective-permute-start.18 = (bf16[6,32,1024]{2,1,0:T(8,128)(2,1)S(1)}, bf16[6,32,1024]{2,1,0:T(8,128)(2,1)S(1)}, u32[]{:S(2)}, u32[]{:S(2)}) collective-permute-start(bf16[6,32,1024]{2,1,0:T(8,128)(2,1)S(1)} %get-tuple-element.57), channel_id=1, source_target_pairs={{0,32},{32,64},{64,96},{96,0},{1,33},{33,65},{65,97},{97,1},{2,34}... | collective-permute-start | bytes 1179656 | tf_op jit(solution)/shard_map/gather_over_replicas/ppermute | solution.py:349
  114.6 15.8 %collective-permute-start.21 = (bf16[6,32,1024]{2,1,0:T(8,128)(2,1)S(1)}, bf16[6,32,1024]{2,1,0:T(8,128)(2,1)S(1)}, u32[]{:S(2)}, u32[]{:S(2)}) collective-permute-start(bf16[6,32,1024]{2,1,0:T(8,128)(2,1)S(1)} %collective-permute-done.12.refs_2_), channel_id=1, source_target_pairs={{0,96},{32,0},{64,32},{96,64},{1,97},{33,1},{65,33},{97,65},{2,98}... | collective-permute-start | bytes 1179656 | tf_op jit(solution)/shard_map/gather_over_replicas/ppermute | solution.py:353
  116.9 14.6 %collective-permute-start.22 = (bf16[6,32,1024]{2,1,0:T(8,128)(2,1)S(1)}, bf16[6,32,1024]{2,1,0:T(8,128)(2,1)S(1)}, u32[]{:S(2)}, u32[]{:S(2)}) collective-permute-start(bf16[6,32,1024]{2,1,0:T(8,128)(2,1)S(1)} %collective-permute-done.13.refs_3_), channel_id=1, source_target_pairs={{0,32},{32,64},{64,96},{96,0},{1,33},{33,65},{65,97},{97,1},{2,34}... | collective-permute-start | bytes 1179656 | tf_op jit(solution)/shard_map/gather_over_replicas/ppermute | solution.py:354
  117.0 16.6 %collective-permute-start.15 = (bf16[12,32,1024]{2,1,0:T(8,128)(2,1)S(1)}, bf16[12,32,1024]{2,1,0:T(8,128)(2,1)S(1)}, u32[]{:S(2)}, u32[]{:S(2)}) collective-permute-start(bf16[12,32,1024]{2,1,0:T(8,128)(2,1)S(1)} %pad_maximum_fusion), channel_id=1, source_target_pairs={{0,16},{16,0},{1,17},{17,1},{2,18},{18,2},{3,19},{19,3},{4,20},{20... | collective-permute-start | bytes 2359304 | tf_op jit(solution)/shard_map/gather_over_replicas/ppermute | solution.py:341
  123.0 9.2 %collective-permute-start.19 = (bf16[6,32,1024]{2,1,0:T(8,128)(2,1)S(1)}, bf16[6,32,1024]{2,1,0:T(8,128)(2,1)S(1)}, u32[]{:S(2)}, u32[]{:S(2)}) collective-permute-start(bf16[6,32,1024]{2,1,0:T(8,128)(2,1)S(1)} %collective-permute-done.17.refs_1_), channel_id=1, source_target_pairs={{0,16},{16,0},{1,17},{17,1},{2,18},{18,2},{3,19},{19,3},{4,20},{20... | collective-permute-start | bytes 1179656 | tf_op jit(solution)/shard_map/gather_over_replicas/ppermute | solution.py:341
  124.2 8.0 %collective-permute-start.20 = (bf16[6,32,1024]{2,1,0:T(8,128)(2,1)S(1)}, bf16[6,32,1024]{2,1,0:T(8,128)(2,1)S(1)}, u32[]{:S(2)}, u32[]{:S(2)}) collective-permute-start(bf16[6,32,1024]{2,1,0:T(8,128)(2,1)S(1)} %collective-permute-done.18.refs_2_), channel_id=1, source_target_pairs={{0,16},{16,0},{1,17},{17,1},{2,18},{18,2},{3,19},{19,3},{4,20},{20... | collective-permute-start | bytes 1179656 | tf_op jit(solution)/shard_map/gather_over_replicas/ppermute | solution.py:341
  130.3 2.5 %collective-permute-start.23 = (bf16[6,32,1024]{2,1,0:T(8,128)(2,1)S(1)}, bf16[6,32,1024]{2,1,0:T(8,128)(2,1)S(1)}, u32[]{:S(2)}, u32[]{:S(2)}) collective-permute-start(bf16[6,32,1024]{2,1,0:T(8,128)(2,1)S(1)} %collective-permute-done.21.refs_5_), channel_id=1, source_target_pairs={{0,16},{16,0},{1,17},{17,1},{2,18},{18,2},{3,19},{19,3},{4,20},{20... | collective-permute-start | bytes 1179656 | tf_op jit(solution)/shard_map/gather_over_replicas/ppermute | solution.py:341
  131.5 2.1 %collective-permute-start.24 = (bf16[6,32,1024]{2,1,0:T(8,128)(2,1)S(1)}, bf16[6,32,1024]{2,1,0:T(8,128)(2,1)S(1)}, u32[]{:S(2)}, u32[]{:S(2)}) collective-permute-start(bf16[6,32,1024]{2,1,0:T(8,128)(2,1)S(1)} %collective-permute-done.22.refs_6_), channel_id=1, source_target_pairs={{0,16},{16,0},{1,17},{17,1},{2,18},{18,2},{3,19},{19,3},{4,20},{20... | collective-permute-start | bytes 1179656 | tf_op jit(solution)/shard_map/gather_over_replicas/ppermute | solution.py:341
  (2 other events, 7.8 us)

commit v3 on v2

--- a/solution.py
+++ b/solution.py
@@ -146,22 +146,31 @@
     core = place[0]
     half, width = own.shape
 
-    def write(rows, columns, product):
-        raw[rows, columns] = product
-        square = jnp.sum(product * product, axis=0, keepdims=True)
-        sums.append(jnp.sum(square, axis=1, keepdims=True))
+    sums = []
+
+    def add_up(product):
+        squares = jnp.sum(product * product, axis=0, keepdims=True)
+        sums.append(jnp.sum(squares, axis=1, keepdims=True))
+
+    def write_first(rows, columns, product):
+        raw[:, columns] = product[:half]
+        add_up(product)
+
+    def write_last(rows, columns, product):
+        if rows.start == half:
+            raw[...] = product
+        add_up(product)
+
+    def right():
+        sums.clear()
+        from_right(side, root, write_first)
+        return sums[0] + sums[1]
 
     def left():
         sums.clear()
-        from_left(root, side, write)
+        from_left(root, side, write_last)
         return sums[0] + sums[1]
 
-    def right():
-        sums.clear()
-        from_right(side, root, write)
-        return sums[0] + sums[1]
-
-    sums = []
     raw_sum = lax.cond(core == 0, right, left)
     scale = 1.0 / (width * width)
     grad_mean = jnp.sum(grad_sum[...], axis=1, keepdims=True) * scale
@@ -171,7 +180,7 @@
 
     @pl.when(active)
     def _():
-        out[...] = (raw[rows_at(core * half, half), :] * ratio).astype(jnp.bfloat16)
+        out[...] = (raw[...] * ratio).astype(jnp.bfloat16)
 
     @pl.when(jnp.logical_not(active))
     def _():
@@ -231,12 +240,12 @@
         return sliced.reshape(per_plane, rows, width)
 
     with jax.named_scope("sum_over_replicas"):
-        sent, next_plane = lax.optimization_barrier((rows_of(plane, 2, 1 - core), plane))
+        sent, kept, *others = lax.optimization_barrier(
+            [rows_of(plane, 2, 1 - core), rows_of(plane, 2, core)]
+            + [rows_of(plane, k, 1 - core) for k in (1, 3, 0)]
+        )
         got = lax.ppermute(sent, "core", swap)
-        kept, *sent = lax.optimization_barrier(
-            [rows_of(next_plane, 2, core)] + [rows_of(next_plane, k, 1 - core) for k in (1, 3, 0)]
-        )
-        got_above, got_below, got_mine = (lax.ppermute(each, "core", swap) for each in sent)
+        got_above, got_below, got_mine = (lax.ppermute(each, "core", swap) for each in others)
         far = plus(kept, got)
         far_low, far_high, here = lax.optimization_barrier((far[:part], far[part:], plane))
         from_above = lax.ppermute(far_low, "z", down)
@@ -301,7 +310,7 @@
         out_shape=jax.ShapeDtypeStruct((half, width), jnp.bfloat16),
         in_specs=[smem, vmem, vmem, vmem, vmem],
         out_specs=vmem,
-        scratch_shapes=[pltpu.VMEM(square, jnp.float32)],
+        scratch_shapes=[pltpu.VMEM((half, width), jnp.float32)],
         compiler_params=pltpu.CompilerParams(vmem_limit_bytes=32 * mib),
         cost_estimate=pl.CostEstimate(flops=work, bytes_accessed=6 * mib, transcendentals=0),
         name="apply_other_root",

time: 137 us -> 139 us (1.015)
  waiting for transfers between devices: 30 us -> 32.8 us
    ppermute x1, waiting for transfers between devices: 0.01 us -> 2.75 us  [local(): got = lax.ppermute(sent, 'core', swap)]
    reshape x3 -> x2, local copies, waits for them, and re-layouts: 6.09 us -> 5.33 us  [rows_of(): return sliced.reshape(per_plane, rows, width)]
  transfers between devices with their start and end apart: 25 -> 25, of which waited for: 12 -> 13; matrix products, arithmetic and copies ran while one was open for 11% -> 9% of each run, Pallas kernels for 4% -> 4%
where the time goes in v3:
time: 139 us; the launch traced here: 138 us
  blocking collectives  41.1 us (30%)
  waiting for transfers between devices  32.8 us (24%)
  starting transfers between devices  28.8 us (21%)
  Pallas kernels  17.8 us (13%)
  other arithmetic  10.9 us (8%)
  local copies, waits for them, and re-layouts  5.63 us (4%)
    all_to_all x1, blocking collectives, local(): lax.all_to_all(summed, ('y', 'x'), 0, 0, tiled=True).reshape(half, width)  22.1 us
    all_to_all x1, blocking collectives, local(): lax.all_to_all(finished.reshape(shards, rows, width), ('y', 'x'), 0, 0, t...  19 us
    convert_element_type x7, other arithmetic, plus(): return total.astype(jnp.bfloat16)  9.97 us
    ppermute x7, starting transfers between devices, other_core(): return lax.ppermute(piece, 'core', swap)  7.83 us
    pallas_call x1, Pallas kernels, local(): pl.pallas_call(root_kernel, out_shape=[jax.ShapeDtypeStruct((3, half, hal...  7.12 us
    ppermute x1, waiting for transfers between devices, local(): high_below = lax.ppermute(plus(to_above[part:], from_below), 'z', up)  7.06 us
    ppermute x1, waiting for transfers between devices, local(): below_high = lax.ppermute(back[part:], 'z', up)  6.39 us
    ppermute x1, waiting for transfers between devices, local(): far_low = lax.ppermute(above_low, 'z', down)  6.17 us
  transfers between devices with their start and end apart: 25, of which 13 were waited for; matrix products, arithmetic and copies ran while one was open for 9% of the time, Pallas kernels for 4%

profile of v3, /device:TPU:1, one launch (start us, length us, event | category | flops | bytes accessed | tf_op | source)
XLA Modules:
  0.0 138.1 jit_solution(11443873461608656395)
XLA Ops:
  0.0 3.5 %dynamic-slice_bitcast_fusion.3 = (bf16[12,32,1024]{2,1,0:T(8,128)(2,1)S(1)}, bf16[12,32,1024]{2,1,0:T(8,128)(2,1)S(1)}, bf16[12,32,1024]{2,1,0:T(8,128)(2,1)S(1...) fusion(bf16[4,12,2,32,1024]{4,3,2,1,0:T(8,128)(2,1)} %bitcast.26, s32[]{:T(128)S(6)} %select_n.76, ...), kind=kLoop, calls=%fused_computation.13 | loop fusion | bytes 7864344 | tf_op jit(solution)/shard_map/sum_over_replicas/reshape | solution.py:240
  5.5 2.8 %collective-permute-done = bf16[12,32,1024]{2,1,0:T(8,128)(2,1)} collective-permute-done((bf16[12,32,1024]{2,1,0:T(8,128)(2,1)}, bf16[12,32,1024]{2,1,0:T(8,128)(2,1)}, u32[]{:S(2)}, u32[]{:S(2)}) %collective-permute-start) | collective-permute-done | bytes 786464 | tf_op jit(solution)/shard_map/sum_over_replicas/ppermute | solution.py:247
  9.8 3.9 %collective-permute-start.5 = (bf16[6,32,1024]{2,1,0:T(8,128)(2,1)S(1)}, bf16[6,32,1024]{2,1,0:T(8,128)(2,1)}, u32[]{:S(2)}, u32[]{:S(2)}) collective-permute-start(bf16[6,32,1024]{2,1,0:T(8,128)(2,1)S(1)} %get-tuple-element.43), channel_id=1, source_target_pairs={{0,96},{32,0},{64,32},{96,64},{1,97},{33,1},{65,33},{97,65},{2,98}... | collective-permute-start | bytes 1179656 | tf_op jit(solution)/shard_map/sum_over_replicas/ppermute | solution.py:251
  18.6 2.7 %collective-permute-start.7 = (bf16[6,32,1024]{2,1,0:T(8,128)(2,1)S(1)}, bf16[6,32,1024]{2,1,0:T(8,128)(2,1)S(1)}, u32[]{:S(2)}, u32[]{:S(2)}) collective-permute-start(bf16[6,32,1024]{2,1,0:T(8,128)(2,1)S(1)} %slice.59), channel_id=1, source_target_pairs={{0,96},{32,0},{64,32},{96,64},{1,97},{33,1},{65,33},{97,65},{2,98}... | collective-permute-start | bytes 1179656 | tf_op jit(solution)/shard_map/sum_over_replicas/ppermute | solution.py:260
  21.4 3.7 %collective-permute-done.8 = bf16[6,32,1024]{2,1,0:T(8,128)(2,1)} collective-permute-done((bf16[6,32,1024]{2,1,0:T(8,128)(2,1)S(1)}, bf16[6,32,1024]{2,1,0:T(8,128)(2,1)}, u32[]{:S(2)}, u32[]{:S(2)}) %collective-permute-start.8) | collective-permute-done | bytes 393248 | tf_op jit(solution)/shard_map/sum_over_replicas/ppermute | solution.py:252
  25.1 1.9 %add_convert_fusion.5 = bf16[6,32,1024]{2,1,0:T(8,128)(2,1)} fusion(bf16[6,32,1024]{2,1,0:T(8,128)(2,1)} %collective-permute-done.8, bf16[12,32,1024]{2,1,0:T(8,128)(2,1)S(1)} %add_convert_fusion.1), kind=kLoop, calls=%fused_computation.7 | loop fusion | flops 786432 | bytes 1179648 | tf_op jit(solution)/shard_map/sum_over_replicas/convert_element_type | solution.py:229
  27.0 1.9 %add_convert_fusion.7 = bf16[6,32,1024]{2,1,0:T(8,128)(2,1)} fusion(bf16[6,32,1024]{2,1,0:T(8,128)(2,1)} %collective-permute-done.5, bf16[12,32,1024]{2,1,0:T(8,128)(2,1)S(1)} %add_convert_fusion), kind=kLoop, calls=%fused_computation.9 | loop fusion | flops 786432 | bytes 1179648 | tf_op jit(solution)/shard_map/sum_over_replicas/convert_element_type | solution.py:229
  28.8 2.7 %collective-permute-start.6 = (bf16[6,32,1024]{2,1,0:T(8,128)(2,1)}, bf16[6,32,1024]{2,1,0:T(8,128)(2,1)S(1)}, u32[]{:S(2)}, u32[]{:S(2)}) collective-permute-start(bf16[6,32,1024]{2,1,0:T(8,128)(2,1)} %add_convert_fusion.7), channel_id=1, source_target_pairs={{0,96},{32,0},{64,32},{96,64},{1,97},{33,1},{65,33},{97,65},{2,98}... | collective-permute-start | bytes 1179656 | tf_op jit(solution)/shard_map/sum_over_replicas/ppermute | solution.py:262
  34.8 7.1 %collective-permute-done.9 = bf16[6,32,1024]{2,1,0:T(8,128)(2,1)S(1)} collective-permute-done((bf16[6,32,1024]{2,1,0:T(8,128)(2,1)}, bf16[6,32,1024]{2,1,0:T(8,128)(2,1)S(1)}, u32[]{:S(2)}, u32[]{:S(2)}) %collective-permute-start.9) | collective-permute-done | bytes 393248 | tf_op jit(solution)/shard_map/sum_over_replicas/ppermute | solution.py:263
  42.4 22.1 %all_to_all.10 = bf16[16,32,1024]{2,1,0:T(8,128)(2,1)S(1)} all-to-all(bf16[16,32,1024]{2,1,0:T(8,128)(2,1)S(1)} %maximum_maximum_fusion), channel_id=1, replica_groups=mesh['z'=4,'core'=2,'y'=4,'x'=4] {'y','x'}, dimensions={0} | all-to-all | bytes 2097152 | tf_op jit(solution)/shard_map/rows_to_owner/all_to_all | solution.py:279
  64.5 2.7 %collective-permute-start.10 = (bf16[512,1024]{1,0:T(8,128)(2,1)S(1)}, bf16[512,1024]{1,0:T(8,128)(2,1)S(1)}, u32[]{:S(2)}, u32[]{:S(2)}) collective-permute-start(bf16[512,1024]{1,0:T(8,128)(2,1)S(1)} %bitcast.22), channel_id=1, source_target_pairs={{0,16},{16,0},{1,17},{17,1},{2,18},{18,2},{3,19},{19,3},{4,20},{20... | collective-permute-start | bytes 3145736 | tf_op jit(solution)/shard_map/rows_to_owner/ppermute | solution.py:280
  67.2 2.3 %collective-permute-done.10.sibling = bf16[512,1024]{1,0:T(8,128)(2,1)S(1)} collective-permute-done((bf16[512,1024]{1,0:T(8,128)(2,1)S(1)}, bf16[512,1024]{1,0:T(8,128)(2,1)S(1)}, u32[]{:S(2)}, u32[]{:S(2)}) %collective-permute-start.10) | collective-permute-done | bytes 1048608 | tf_op jit(solution)/shard_map/rows_to_owner/ppermute | solution.py:280
  69.5 7.1 %inverse_root.1 = (bf16[3,512,512]{2,1,0:T(8,128)(2,1)S(1)}, bf16[1024,1024]{1,0:T(8,128)(2,1)S(1)}) custom-call(s32[3]{0:T(128)S(1)} %pad_add_fusion.place, bf16[512,1024]{1,0:T(8,128)(2,1)S(1)} %bitcast.23, bf16[512,1024]{1,0:T(8,128)(2,1)S(1)} %collective-permute-done.10.sibling), custom_call_target="tpu_custom_call" | custom-call | flops 6442450944 | bytes 6291456 | tf_op jit(solution)/shard_map/inverse_root/pallas_call | solution.py:285
  77.0 3.0 %apply_own_root.1 = (bf16[1024,1024]{1,0:T(8,128)(2,1)S(1)}, f32[1,1024]{1,0:T(1,128)S(1)}) custom-call(s32[3]{0:T(128)S(1)} %pad_add_fusion.place, bf16[3,512,512]{2,1,0:T(8,128)(2,1)S(1)} %get-tuple-element.48.root, bf16[1024,1024]{1,0:T(8,128)(2,1)S(1)} %get-tuple-element.49.grad), custom_call_target="tpu_custom_call" | custom-call | flops 2147483648 | bytes 6291456 | tf_op jit(solution)/shard_map/apply_own_root/pallas_call | solution.py:299
  80.1 3.2 %apply_other_root.1 = bf16[512,1024]{1,0:T(8,128)(2,1)S(1)} custom-call(s32[3]{0:T(128)S(1)} %pad_add_fusion.place, bf16[512,1024]{1,0:T(8,128)(2,1)S(1)} %bitcast.24, bf16[1024,1024]{1,0:T(8,128)(2,1)S(1)} %get-tuple-element.50.side, bf16[3,512,512]{2,1,0:T(8,128)(2,1)S(1)} %collective-permute-done.11.root, f32[1,1024]{1,0:T(1,128)S(1)} %get-tuple-element.51.grad_sum), custom_call_target="tpu_custom_call" | custom-call | flops 2147483648 | bytes 6291456 | tf_op jit(solution)/shard_map/apply_other_root/pallas_call | solution.py:308
  83.3 19.0 %all_to_all.11 = bf16[16,32,1024]{2,1,0:T(8,128)(2,1)S(1)} all-to-all(bf16[16,32,1024]{2,1,0:T(8,128)(2,1)S(1)} %bitcast.25), channel_id=1, replica_groups=mesh['z'=4,'core'=2,'y'=4,'x'=4] {'y','x'}, dimensions={0} | all-to-all | bytes 2097152 | tf_op jit(solution)/shard_map/rows_to_shards/all_to_all | solution.py:320
  102.4 2.0 %collective-permute-start.14 = (bf16[12,32,1024]{2,1,0:T(8,128)(2,1)S(1)}, bf16[12,32,1024]{2,1,0:T(8,128)(2,1)S(1)}, u32[]{:S(2)}, u32[]{:S(2)}) collective-permute-start(bf16[12,32,1024]{2,1,0:T(8,128)(2,1)S(1)} %slice.63.refs_0_), channel_id=1, source_target_pairs={{0,16},{16,0},{1,17},{17,1},{2,18},{18,2},{3,19},{19,3},{4,20},{20... | collective-permute-start | bytes 2359304 | tf_op jit(solution)/shard_map/gather_over_replicas/ppermute | solution.py:350
  104.5 2.7 %collective-permute-start.12 = (bf16[6,32,1024]{2,1,0:T(8,128)(2,1)S(1)}, bf16[6,32,1024]{2,1,0:T(8,128)(2,1)S(1)}, u32[]{:S(2)}, u32[]{:S(2)}) collective-permute-start(bf16[6,32,1024]{2,1,0:T(8,128)(2,1)S(1)} %get-tuple-element.55), channel_id=1, source_target_pairs={{0,96},{32,0},{64,32},{96,64},{1,97},{33,1},{65,33},{97,65},{2,98}... | collective-permute-start | bytes 1179656 | tf_op jit(solution)/shard_map/gather_over_replicas/ppermute | solution.py:353
  110.0 6.4 %collective-permute-done.13.refs_3_ = bf16[6,32,1024]{2,1,0:T(8,128)(2,1)S(1)} collective-permute-done((bf16[6,32,1024]{2,1,0:T(8,128)(2,1)S(1)}, bf16[6,32,1024]{2,1,0:T(8,128)(2,1)S(1)}, u32[]{:S(2)}, u32[]{:S(2)}) %collective-permute-start.13) | collective-permute-done | bytes 393248 | tf_op jit(solution)/shard_map/gather_over_replicas/ppermute | solution.py:354
  116.4 2.4 %collective-permute-start.21 = (bf16[6,32,1024]{2,1,0:T(8,128)(2,1)S(1)}, bf16[6,32,1024]{2,1,0:T(8,128)(2,1)S(1)}, u32[]{:S(2)}, u32[]{:S(2)}) collective-permute-start(bf16[6,32,1024]{2,1,0:T(8,128)(2,1)S(1)} %collective-permute-done.12.refs_2_), channel_id=1, source_target_pairs={{0,96},{32,0},{64,32},{96,64},{1,97},{33,1},{65,33},{97,65},{2,98}... | collective-permute-start | bytes 1179656 | tf_op jit(solution)/shard_map/gather_over_replicas/ppermute | solution.py:362
  118.9 2.2 %collective-permute-start.15 = (bf16[12,32,1024]{2,1,0:T(8,128)(2,1)S(1)}, bf16[12,32,1024]{2,1,0:T(8,128)(2,1)S(1)}, u32[]{:S(2)}, u32[]{:S(2)}) collective-permute-start(bf16[12,32,1024]{2,1,0:T(8,128)(2,1)S(1)} %pad_maximum_fusion), channel_id=1, source_target_pairs={{0,16},{16,0},{1,17},{17,1},{2,18},{18,2},{3,19},{19,3},{4,20},{20... | collective-permute-start | bytes 2359304 | tf_op jit(solution)/shard_map/gather_over_replicas/ppermute | solution.py:350
  121.1 2.0 %place_early.1.refs_9_ = bf16[48,64,1024]{2,1,0:T(8,128)(2,1)} custom-call(s32[3]{0:T(128)S(1)} %pad_add_fusion.place, bf16[12,32,1024]{2,1,0:T(8,128)(2,1)S(1)} %slice.63.refs_0_, bf16[12,32,1024]{2,1,0:T(8,128)(2,1)S(1)} %collective-permute-done.14.refs_1_, bf16[6,32,1024]{2,1,0:T(8,128)(2,1)S(1)} %collective-permute-done.12.refs_2_, ...), custom_call_target="tpu_custom_call" | custom-call | bytes 4718592 | tf_op jit(solution)/shard_map/gather_over_replicas/place_early/pallas_call | solution.py:337
  126.0 6.2 %collective-permute-done.21.refs_5_ = bf16[6,32,1024]{2,1,0:T(8,128)(2,1)S(1)} collective-permute-done((bf16[6,32,1024]{2,1,0:T(8,128)(2,1)S(1)}, bf16[6,32,1024]{2,1,0:T(8,128)(2,1)S(1)}, u32[]{:S(2)}, u32[]{:S(2)}) %collective-permute-start.21) | collective-permute-done | bytes 393248 | tf_op jit(solution)/shard_map/gather_over_replicas/ppermute | solution.py:362
  135.4 2.5 %place_late.1 = bf16[48,64,1024]{2,1,0:T(8,128)(2,1)} custom-call(s32[3]{0:T(128)S(1)} %pad_add_fusion.place, bf16[12,32,1024]{2,1,0:T(8,128)(2,1)S(1)} %collective-permute-done.15.refs_0_, bf16[6,32,1024]{2,1,0:T(8,128)(2,1)S(1)} %collective-permute-done.17.refs_1_, ...), custom_call_target="tpu_custom_call", output_to_operand_aliasing={{}: (10, {})} | custom-call | bytes 7864320 | tf_op jit(solution)/shard_map/gather_over_replicas/place_late/pallas_call | solution.py:337
  (56 shorter events, 21.4 us)
Async XLA Ops:
  3.5 4.8 %collective-permute-start = (bf16[12,32,1024]{2,1,0:T(8,128)(2,1)}, bf16[12,32,1024]{2,1,0:T(8,128)(2,1)}, u32[]{:S(2)}, u32[]{:S(2)}) collective-permute-start(bf16[12,32,1024]{2,1,0:T(8,128)(2,1)} %get-tuple-element.34), channel_id=1, source_target_pairs={{0,16},{16,0},{1,17},{17,1},{2,18},{18,2},{3,19},{19,3},{4,20},{20... | collective-permute-start | bytes 2359304 | tf_op jit(solution)/shard_map/sum_over_replicas/ppermute | solution.py:247
  4.9 10.6 %collective-permute-start.4 = (bf16[12,32,1024]{2,1,0:T(8,128)(2,1)S(1)}, bf16[12,32,1024]{2,1,0:T(8,128)(2,1)}, u32[]{:S(2)}, u32[]{:S(2)}) collective-permute-start(bf16[12,32,1024]{2,1,0:T(8,128)(2,1)S(1)} %get-tuple-element.42), channel_id=1, source_target_pairs={{0,16},{16,0},{1,17},{17,1},{2,18},{18,2},{3,19},{19,3},{4,20},{20... | collective-permute-start | bytes 2359304 | tf_op jit(solution)/shard_map/sum_over_replicas/ppermute | solution.py:248
  4.9 26.6 %collective-permute-start.1 = (bf16[12,32,1024]{2,1,0:T(8,128)(2,1)S(1)}, bf16[12,32,1024]{2,1,0:T(8,128)(2,1)}, u32[]{:S(2)}, u32[]{:S(2)}) collective-permute-start(bf16[12,32,1024]{2,1,0:T(8,128)(2,1)S(1)} %get-tuple-element.37), channel_id=1, source_target_pairs={{0,16},{16,0},{1,17},{17,1},{2,18},{18,2},{3,19},{19,3},{4,20},{20... | collective-permute-start | bytes 2359304 | tf_op jit(solution)/shard_map/sum_over_replicas/ppermute | solution.py:248
  5.5 11.6 %collective-permute-start.2 = (bf16[12,32,1024]{2,1,0:T(8,128)(2,1)S(1)}, bf16[12,32,1024]{2,1,0:T(8,128)(2,1)}, u32[]{:S(2)}, u32[]{:S(2)}) collective-permute-start(bf16[12,32,1024]{2,1,0:T(8,128)(2,1)S(1)} %get-tuple-element.39), channel_id=1, source_target_pairs={{0,16},{16,0},{1,17},{17,1},{2,18},{18,2},{3,19},{19,3},{4,20},{20... | collective-permute-start | bytes 2359304 | tf_op jit(solution)/shard_map/sum_over_replicas/ppermute | solution.py:248
  9.8 17.1 %collective-permute-start.5 = (bf16[6,32,1024]{2,1,0:T(8,128)(2,1)S(1)}, bf16[6,32,1024]{2,1,0:T(8,128)(2,1)}, u32[]{:S(2)}, u32[]{:S(2)}) collective-permute-start(bf16[6,32,1024]{2,1,0:T(8,128)(2,1)S(1)} %get-tuple-element.43), channel_id=1, source_target_pairs={{0,96},{32,0},{64,32},{96,64},{1,97},{33,1},{65,33},{97,65},{2,98}... | collective-permute-start | bytes 1179656 | tf_op jit(solution)/shard_map/sum_over_replicas/ppermute | solution.py:251
  13.7 11.3 %collective-permute-start.8 = (bf16[6,32,1024]{2,1,0:T(8,128)(2,1)S(1)}, bf16[6,32,1024]{2,1,0:T(8,128)(2,1)}, u32[]{:S(2)}, u32[]{:S(2)}) collective-permute-start(bf16[6,32,1024]{2,1,0:T(8,128)(2,1)S(1)} %get-tuple-element.44), channel_id=1, source_target_pairs={{0,32},{32,64},{64,96},{96,0},{1,33},{33,65},{65,97},{97,1},{2,34}... | collective-permute-start | bytes 1179656 | tf_op jit(solution)/shard_map/sum_over_replicas/ppermute | solution.py:252
  18.5 14.8 %collective-permute-start.3 = (bf16[6,32,1024]{2,1,0:T(8,128)(2,1)S(1)}, bf16[6,32,1024]{2,1,0:T(8,128)(2,1)S(1)}, u32[]{:S(2)}, u32[]{:S(2)}) collective-permute-start(bf16[6,32,1024]{2,1,0:T(8,128)(2,1)S(1)} %slice.56), channel_id=1, source_target_pairs={{0,32},{32,64},{64,96},{96,0},{1,33},{33,65},{65,97},{97,1},{2,34}... | collective-permute-start | bytes 1179656 | tf_op jit(solution)/shard_map/sum_over_replicas/ppermute | solution.py:259
  18.6 16.1 %collective-permute-start.7 = (bf16[6,32,1024]{2,1,0:T(8,128)(2,1)S(1)}, bf16[6,32,1024]{2,1,0:T(8,128)(2,1)S(1)}, u32[]{:S(2)}, u32[]{:S(2)}) collective-permute-start(bf16[6,32,1024]{2,1,0:T(8,128)(2,1)S(1)} %slice.59), channel_id=1, source_target_pairs={{0,96},{32,0},{64,32},{96,64},{1,97},{33,1},{65,33},{97,65},{2,98}... | collective-permute-start | bytes 1179656 | tf_op jit(solution)/shard_map/sum_over_replicas/ppermute | solution.py:260
  27.0 14.9 %collective-permute-start.9 = (bf16[6,32,1024]{2,1,0:T(8,128)(2,1)}, bf16[6,32,1024]{2,1,0:T(8,128)(2,1)S(1)}, u32[]{:S(2)}, u32[]{:S(2)}) collective-permute-start(bf16[6,32,1024]{2,1,0:T(8,128)(2,1)} %add_convert_fusion.5), channel_id=1, source_target_pairs={{0,32},{32,64},{64,96},{96,0},{1,33},{33,65},{65,97},{97,1},{2,34}... | collective-permute-start | bytes 1179656 | tf_op jit(solution)/shard_map/sum_over_replicas/ppermute | solution.py:263
  28.8 13.0 %collective-permute-start.6 = (bf16[6,32,1024]{2,1,0:T(8,128)(2,1)}, bf16[6,32,1024]{2,1,0:T(8,128)(2,1)S(1)}, u32[]{:S(2)}, u32[]{:S(2)}) collective-permute-start(bf16[6,32,1024]{2,1,0:T(8,128)(2,1)} %add_convert_fusion.7), channel_id=1, source_target_pairs={{0,96},{32,0},{64,32},{96,64},{1,97},{33,1},{65,33},{97,65},{2,98}... | collective-permute-start | bytes 1179656 | tf_op jit(solution)/shard_map/sum_over_replicas/ppermute | solution.py:262
  64.5 5.0 %collective-permute-start.10 = (bf16[512,1024]{1,0:T(8,128)(2,1)S(1)}, bf16[512,1024]{1,0:T(8,128)(2,1)S(1)}, u32[]{:S(2)}, u32[]{:S(2)}) collective-permute-start(bf16[512,1024]{1,0:T(8,128)(2,1)S(1)} %bitcast.22), channel_id=1, source_target_pairs={{0,16},{16,0},{1,17},{17,1},{2,18},{18,2},{3,19},{19,3},{4,20},{20... | collective-permute-start | bytes 3145736 | tf_op jit(solution)/shard_map/rows_to_owner/ppermute | solution.py:280
  76.6 3.5 %collective-permute-start.11 = (bf16[3,512,512]{2,1,0:T(8,128)(2,1)S(1)}, bf16[3,512,512]{2,1,0:T(8,128)(2,1)S(1)}, u32[]{:S(2)}, u32[]{:S(2)}) collective-permute-start(bf16[3,512,512]{2,1,0:T(8,128)(2,1)S(1)} %get-tuple-element.48.root), channel_id=1, source_target_pairs={{0,16},{16,0},{1,17},{17,1},{2,18},{18,2},{3,19},{19,3},{4,20},{20... | collective-permute-start | bytes 4718600 | tf_op jit(solution)/shard_map/ppermute | solution.py:298
  102.4 14.1 %collective-permute-start.14 = (bf16[12,32,1024]{2,1,0:T(8,128)(2,1)S(1)}, bf16[12,32,1024]{2,1,0:T(8,128)(2,1)S(1)}, u32[]{:S(2)}, u32[]{:S(2)}) collective-permute-start(bf16[12,32,1024]{2,1,0:T(8,128)(2,1)S(1)} %slice.63.refs_0_), channel_id=1, source_target_pairs={{0,16},{16,0},{1,17},{17,1},{2,18},{18,2},{3,19},{19,3},{4,20},{20... | collective-permute-start | bytes 2359304 | tf_op jit(solution)/shard_map/gather_over_replicas/ppermute | solution.py:350
  104.4 12.0 %collective-permute-start.13 = (bf16[6,32,1024]{2,1,0:T(8,128)(2,1)S(1)}, bf16[6,32,1024]{2,1,0:T(8,128)(2,1)S(1)}, u32[]{:S(2)}, u32[]{:S(2)}) collective-permute-start(bf16[6,32,1024]{2,1,0:T(8,128)(2,1)S(1)} %get-tuple-element.54), channel_id=1, source_target_pairs={{0,32},{32,64},{64,96},{96,0},{1,33},{33,65},{65,97},{97,1},{2,34}... | collective-permute-start | bytes 1179656 | tf_op jit(solution)/shard_map/gather_over_replicas/ppermute | solution.py:354
  104.5 11.9 %collective-permute-start.12 = (bf16[6,32,1024]{2,1,0:T(8,128)(2,1)S(1)}, bf16[6,32,1024]{2,1,0:T(8,128)(2,1)S(1)}, u32[]{:S(2)}, u32[]{:S(2)}) collective-permute-start(bf16[6,32,1024]{2,1,0:T(8,128)(2,1)S(1)} %get-tuple-element.55), channel_id=1, source_target_pairs={{0,96},{32,0},{64,32},{96,64},{1,97},{33,1},{65,33},{97,65},{2,98}... | collective-permute-start | bytes 1179656 | tf_op jit(solution)/shard_map/gather_over_replicas/ppermute | solution.py:353
  108.6 15.2 %collective-permute-start.17 = (bf16[6,32,1024]{2,1,0:T(8,128)(2,1)S(1)}, bf16[6,32,1024]{2,1,0:T(8,128)(2,1)S(1)}, u32[]{:S(2)}, u32[]{:S(2)}) collective-permute-start(bf16[6,32,1024]{2,1,0:T(8,128)(2,1)S(1)} %get-tuple-element.54), channel_id=1, source_target_pairs={{0,96},{32,0},{64,32},{96,64},{1,97},{33,1},{65,33},{97,65},{2,98}... | collective-permute-start | bytes 1179656 | tf_op jit(solution)/shard_map/gather_over_replicas/ppermute | solution.py:357
  108.6 16.3 %collective-permute-start.18 = (bf16[6,32,1024]{2,1,0:T(8,128)(2,1)S(1)}, bf16[6,32,1024]{2,1,0:T(8,128)(2,1)S(1)}, u32[]{:S(2)}, u32[]{:S(2)}) collective-permute-start(bf16[6,32,1024]{2,1,0:T(8,128)(2,1)S(1)} %get-tuple-element.55), channel_id=1, source_target_pairs={{0,32},{32,64},{64,96},{96,0},{1,33},{33,65},{65,97},{97,1},{2,34}... | collective-permute-start | bytes 1179656 | tf_op jit(solution)/shard_map/gather_over_replicas/ppermute | solution.py:358
  116.4 15.8 %collective-permute-start.21 = (bf16[6,32,1024]{2,1,0:T(8,128)(2,1)S(1)}, bf16[6,32,1024]{2,1,0:T(8,128)(2,1)S(1)}, u32[]{:S(2)}, u32[]{:S(2)}) collective-permute-start(bf16[6,32,1024]{2,1,0:T(8,128)(2,1)S(1)} %collective-permute-done.12.refs_2_), channel_id=1, source_target_pairs={{0,96},{32,0},{64,32},{96,64},{1,97},{33,1},{65,33},{97,65},{2,98}... | collective-permute-start | bytes 1179656 | tf_op jit(solution)/shard_map/gather_over_replicas/ppermute | solution.py:362
  118.8 14.6 %collective-permute-start.22 = (bf16[6,32,1024]{2,1,0:T(8,128)(2,1)S(1)}, bf16[6,32,1024]{2,1,0:T(8,128)(2,1)S(1)}, u32[]{:S(2)}, u32[]{:S(2)}) collective-permute-start(bf16[6,32,1024]{2,1,0:T(8,128)(2,1)S(1)} %collective-permute-done.13.refs_3_), channel_id=1, source_target_pairs={{0,32},{32,64},{64,96},{96,0},{1,33},{33,65},{65,97},{97,1},{2,34}... | collective-permute-start | bytes 1179656 | tf_op jit(solution)/shard_map/gather_over_replicas/ppermute | solution.py:363
  118.9 16.6 %collective-permute-start.15 = (bf16[12,32,1024]{2,1,0:T(8,128)(2,1)S(1)}, bf16[12,32,1024]{2,1,0:T(8,128)(2,1)S(1)}, u32[]{:S(2)}, u32[]{:S(2)}) collective-permute-start(bf16[12,32,1024]{2,1,0:T(8,128)(2,1)S(1)} %pad_maximum_fusion), channel_id=1, source_target_pairs={{0,16},{16,0},{1,17},{17,1},{2,18},{18,2},{3,19},{19,3},{4,20},{20... | collective-permute-start | bytes 2359304 | tf_op jit(solution)/shard_map/gather_over_replicas/ppermute | solution.py:350
  124.8 9.2 %collective-permute-start.19 = (bf16[6,32,1024]{2,1,0:T(8,128)(2,1)S(1)}, bf16[6,32,1024]{2,1,0:T(8,128)(2,1)S(1)}, u32[]{:S(2)}, u32[]{:S(2)}) collective-permute-start(bf16[6,32,1024]{2,1,0:T(8,128)(2,1)S(1)} %collective-permute-done.17.refs_1_), channel_id=1, source_target_pairs={{0,16},{16,0},{1,17},{17,1},{2,18},{18,2},{3,19},{19,3},{4,20},{20... | collective-permute-start | bytes 1179656 | tf_op jit(solution)/shard_map/gather_over_replicas/ppermute | solution.py:350
  126.0 8.0 %collective-permute-start.20 = (bf16[6,32,1024]{2,1,0:T(8,128)(2,1)S(1)}, bf16[6,32,1024]{2,1,0:T(8,128)(2,1)S(1)}, u32[]{:S(2)}, u32[]{:S(2)}) collective-permute-start(bf16[6,32,1024]{2,1,0:T(8,128)(2,1)S(1)} %collective-permute-done.18.refs_2_), channel_id=1, source_target_pairs={{0,16},{16,0},{1,17},{17,1},{2,18},{18,2},{3,19},{19,3},{4,20},{20... | collective-permute-start | bytes 1179656 | tf_op jit(solution)/shard_map/gather_over_replicas/ppermute | solution.py:350
  132.2 2.5 %collective-permute-start.23 = (bf16[6,32,1024]{2,1,0:T(8,128)(2,1)S(1)}, bf16[6,32,1024]{2,1,0:T(8,128)(2,1)S(1)}, u32[]{:S(2)}, u32[]{:S(2)}) collective-permute-start(bf16[6,32,1024]{2,1,0:T(8,128)(2,1)S(1)} %collective-permute-done.21.refs_5_), channel_id=1, source_target_pairs={{0,16},{16,0},{1,17},{17,1},{2,18},{18,2},{3,19},{19,3},{4,20},{20... | collective-permute-start | bytes 1179656 | tf_op jit(solution)/shard_map/gather_over_replicas/ppermute | solution.py:350
  133.3 2.1 %collective-permute-start.24 = (bf16[6,32,1024]{2,1,0:T(8,128)(2,1)S(1)}, bf16[6,32,1024]{2,1,0:T(8,128)(2,1)S(1)}, u32[]{:S(2)}, u32[]{:S(2)}) collective-permute-start(bf16[6,32,1024]{2,1,0:T(8,128)(2,1)S(1)} %collective-permute-done.22.refs_6_), channel_id=1, source_target_pairs={{0,16},{16,0},{1,17},{17,1},{2,18},{18,2},{3,19},{19,3},{4,20},{20... | collective-permute-start | bytes 1179656 | tf_op jit(solution)/shard_map/gather_over_replicas/ppermute | solution.py:350
  (2 other events, 7.8 us)

commit v4 on v2

--- a/solution.py
+++ b/solution.py
@@ -360,14 +360,14 @@
             (other, (0, 0, per_plane, False)),
             (above_low, (1, 0, part, True)),
             (below_high, (3, part, part, True)),
+            (above_high, (1, part, part, True)),
+            (below_low, (3, 0, part, True)),
         )
         above_high, below_low, out = lax.optimization_barrier((above_high, below_low, out))
         return put(
             "place_late",
             out,
             (passed, (1, 0, part, False), (3, part, part, False)),
-            (above_high, (1, part, part, True)),
-            (below_low, (3, 0, part, True)),
             (other_core(above_high), (1, part, part, False)),
             (other_core(below_low), (3, 0, part, False)),
             (far_low, (2, 0, part, True)),

time: 137 us -> 137 us (level)
    ppermute x1, waiting for transfers between devices: 6.17 us -> 3.75 us  [local(): far_low = lax.ppermute(above_low, 'z', down)]
    ppermute x1, waiting for transfers between devices: 0.76 us -> 2.75 us  [local(): above_high = lax.ppermute(high, 'z', down)]
where the time goes in v4:
time: 137 us; the launch traced here: 136 us
  blocking collectives  41 us (30%)
  waiting for transfers between devices  29.6 us (22%)
  starting transfers between devices  29.2 us (21%)
  Pallas kernels  17.9 us (13%)
  other arithmetic  10.9 us (8%)
  local copies, waits for them, and re-layouts  6.41 us (5%)
    all_to_all x1, blocking collectives, local(): lax.all_to_all(summed, ('y', 'x'), 0, 0, tiled=True).reshape(half, width)  22 us
    all_to_all x1, blocking collectives, local(): lax.all_to_all(finished.reshape(shards, rows, width), ('y', 'x'), 0, 0, t...  19 us
    convert_element_type x7, other arithmetic, plus(): return total.astype(jnp.bfloat16)  9.97 us
    ppermute x7, starting transfers between devices, other_core(): return lax.ppermute(piece, 'core', swap)  7.77 us
    pallas_call x1, Pallas kernels, local(): pl.pallas_call(root_kernel, out_shape=[jax.ShapeDtypeStruct((3, half, hal...  7.13 us
    ppermute x1, waiting for transfers between devices, local(): high_below = lax.ppermute(plus(to_above[part:], from_below), 'z', up)  7.06 us
    ppermute x1, waiting for transfers between devices, local(): below_high = lax.ppermute(back[part:], 'z', up)  6.4 us
    reshape x3, local copies, waits for them, and re-layouts, rows_of(): return sliced.reshape(per_plane, rows, width)  6.09 us
  transfers between devices with their start and end apart: 25, of which 12 were waited for; matrix products, arithmetic and copies ran while one was open for 11% of the time, Pallas kernels for 4%

profile of v4, /device:TPU:1, one launch (start us, length us, event | category | flops | bytes accessed | tf_op | source)
XLA Modules:
  0.0 136.0 jit_solution(1371237747554238181)
XLA Ops:
  0.0 2.1 %dynamic-slice_bitcast_fusion.7 = bf16[12,32,1024]{2,1,0:T(8,128)(2,1)} fusion(bf16[4,12,2,32,1024]{4,3,2,1,0:T(8,128)(2,1)} %bitcast.26, s32[]{:T(128)S(6)} %select_n.72, s32[]{:T(128)S(6)} %select_n.73), kind=kLoop, calls=%fused_computation.17 | loop fusion | bytes 1572872 | tf_op jit(solution)/shard_map/sum_over_replicas/reshape | solution.py:231
  3.5 2.2 %dynamic-slice_bitcast_fusion.3 = (bf16[12,32,1024]{2,1,0:T(8,128)(2,1)S(1)}, bf16[12,32,1024]{2,1,0:T(8,128)(2,1)S(1)}, bf16[12,32,1024]{2,1,0:T(8,128)(2,1)S(1)}, bf16[12,32,1024]{2,1,0:T(8,128)(2,1)S(1)}) fusion(bf16[4,12,2,32,1024]{4,3,2,1,0:T(8,128)(2,1)} %bitcast.27, s32[]{:T(128)S(6)} %select_n.82, s32[]{:T(128)S(6)} %select_n.73, s32[]{:T(128)S(6)} %select_n.80, ...), kind=kLoop, calls=%fused_computation.13 | loop fusion | bytes 6291480 | tf_op jit(solution)/shard_map/sum_over_replicas/reshape | solution.py:231
  8.0 3.9 %collective-permute-start.5 = (bf16[6,32,1024]{2,1,0:T(8,128)(2,1)S(1)}, bf16[6,32,1024]{2,1,0:T(8,128)(2,1)}, u32[]{:S(2)}, u32[]{:S(2)}) collective-permute-start(bf16[6,32,1024]{2,1,0:T(8,128)(2,1)S(1)} %get-tuple-element.45), channel_id=1, source_target_pairs={{0,96},{32,0},{64,32},{96,64},{1,97},{33,1},{65,33},{97,65},{2,98}... | collective-permute-start | bytes 1179656 | tf_op jit(solution)/shard_map/sum_over_replicas/ppermute | solution.py:242
  16.8 2.7 %collective-permute-start.7 = (bf16[6,32,1024]{2,1,0:T(8,128)(2,1)S(1)}, bf16[6,32,1024]{2,1,0:T(8,128)(2,1)S(1)}, u32[]{:S(2)}, u32[]{:S(2)}) collective-permute-start(bf16[6,32,1024]{2,1,0:T(8,128)(2,1)S(1)} %slice.59), channel_id=1, source_target_pairs={{0,96},{32,0},{64,32},{96,64},{1,97},{33,1},{65,33},{97,65},{2,98}... | collective-permute-start | bytes 1179656 | tf_op jit(solution)/shard_map/sum_over_replicas/ppermute | solution.py:251
  19.6 3.6 %collective-permute-done.8 = bf16[6,32,1024]{2,1,0:T(8,128)(2,1)} collective-permute-done((bf16[6,32,1024]{2,1,0:T(8,128)(2,1)S(1)}, bf16[6,32,1024]{2,1,0:T(8,128)(2,1)}, u32[]{:S(2)}, u32[]{:S(2)}) %collective-permute-start.8) | collective-permute-done | bytes 393248 | tf_op jit(solution)/shard_map/sum_over_replicas/ppermute | solution.py:243
  23.2 1.9 %add_convert_fusion.5 = bf16[6,32,1024]{2,1,0:T(8,128)(2,1)} fusion(bf16[6,32,1024]{2,1,0:T(8,128)(2,1)} %collective-permute-done.8, bf16[12,32,1024]{2,1,0:T(8,128)(2,1)S(1)} %add_convert_fusion.1), kind=kLoop, calls=%fused_computation.7 | loop fusion | flops 786432 | bytes 1179648 | tf_op jit(solution)/shard_map/sum_over_replicas/convert_element_type | solution.py:220
  25.1 1.9 %add_convert_fusion.7 = bf16[6,32,1024]{2,1,0:T(8,128)(2,1)} fusion(bf16[6,32,1024]{2,1,0:T(8,128)(2,1)} %collective-permute-done.5, bf16[12,32,1024]{2,1,0:T(8,128)(2,1)S(1)} %add_convert_fusion), kind=kLoop, calls=%fused_computation.9 | loop fusion | flops 786432 | bytes 1179648 | tf_op jit(solution)/shard_map/sum_over_replicas/convert_element_type | solution.py:220
  27.0 2.7 %collective-permute-start.6 = (bf16[6,32,1024]{2,1,0:T(8,128)(2,1)}, bf16[6,32,1024]{2,1,0:T(8,128)(2,1)S(1)}, u32[]{:S(2)}, u32[]{:S(2)}) collective-permute-start(bf16[6,32,1024]{2,1,0:T(8,128)(2,1)} %add_convert_fusion.7), channel_id=1, source_target_pairs={{0,96},{32,0},{64,32},{96,64},{1,97},{33,1},{65,33},{97,65},{2,98}... | collective-permute-start | bytes 1179656 | tf_op jit(solution)/shard_map/sum_over_replicas/ppermute | solution.py:253
  32.9 7.1 %collective-permute-done.9 = bf16[6,32,1024]{2,1,0:T(8,128)(2,1)S(1)} collective-permute-done((bf16[6,32,1024]{2,1,0:T(8,128)(2,1)}, bf16[6,32,1024]{2,1,0:T(8,128)(2,1)S(1)}, u32[]{:S(2)}, u32[]{:S(2)}) %collective-permute-start.9) | collective-permute-done | bytes 393248 | tf_op jit(solution)/shard_map/sum_over_replicas/ppermute | solution.py:254
  40.6 22.0 %all_to_all.10 = bf16[16,32,1024]{2,1,0:T(8,128)(2,1)S(1)} all-to-all(bf16[16,32,1024]{2,1,0:T(8,128)(2,1)S(1)} %maximum_maximum_fusion), channel_id=1, replica_groups=mesh['z'=4,'core'=2,'y'=4,'x'=4] {'y','x'}, dimensions={0} | all-to-all | bytes 2097152 | tf_op jit(solution)/shard_map/rows_to_owner/all_to_all | solution.py:270
  62.5 2.8 %collective-permute-start.10 = (bf16[512,1024]{1,0:T(8,128)(2,1)S(1)}, bf16[512,1024]{1,0:T(8,128)(2,1)S(1)}, u32[]{:S(2)}, u32[]{:S(2)}) collective-permute-start(bf16[512,1024]{1,0:T(8,128)(2,1)S(1)} %bitcast.22), channel_id=1, source_target_pairs={{0,16},{16,0},{1,17},{17,1},{2,18},{18,2},{3,19},{19,3},{4,20},{20... | collective-permute-start | bytes 3145736 | tf_op jit(solution)/shard_map/rows_to_owner/ppermute | solution.py:271
  65.3 2.3 %collective-permute-done.10.sibling = bf16[512,1024]{1,0:T(8,128)(2,1)S(1)} collective-permute-done((bf16[512,1024]{1,0:T(8,128)(2,1)S(1)}, bf16[512,1024]{1,0:T(8,128)(2,1)S(1)}, u32[]{:S(2)}, u32[]{:S(2)}) %collective-permute-start.10) | collective-permute-done | bytes 1048608 | tf_op jit(solution)/shard_map/rows_to_owner/ppermute | solution.py:271
  67.6 7.1 %inverse_root.1 = (bf16[3,512,512]{2,1,0:T(8,128)(2,1)S(1)}, bf16[1024,1024]{1,0:T(8,128)(2,1)S(1)}) custom-call(s32[3]{0:T(128)S(1)} %pad_add_fusion.place, bf16[512,1024]{1,0:T(8,128)(2,1)S(1)} %bitcast.23, bf16[512,1024]{1,0:T(8,128)(2,1)S(1)} %collective-permute-done.10.sibling), custom_call_target="tpu_custom_call" | custom-call | flops 6442450944 | bytes 6291456 | tf_op jit(solution)/shard_map/inverse_root/pallas_call | solution.py:276
  75.1 3.0 %apply_own_root.1 = (bf16[1024,1024]{1,0:T(8,128)(2,1)S(1)}, f32[1,1024]{1,0:T(1,128)S(1)}) custom-call(s32[3]{0:T(128)S(1)} %pad_add_fusion.place, bf16[3,512,512]{2,1,0:T(8,128)(2,1)S(1)} %get-tuple-element.50.root, bf16[1024,1024]{1,0:T(8,128)(2,1)S(1)} %get-tuple-element.51.grad), custom_call_target="tpu_custom_call" | custom-call | flops 2147483648 | bytes 6291456 | tf_op jit(solution)/shard_map/apply_own_root/pallas_call | solution.py:290
  78.2 3.2 %apply_other_root.1 = bf16[512,1024]{1,0:T(8,128)(2,1)S(1)} custom-call(s32[3]{0:T(128)S(1)} %pad_add_fusion.place, bf16[512,1024]{1,0:T(8,128)(2,1)S(1)} %bitcast.24, bf16[1024,1024]{1,0:T(8,128)(2,1)S(1)} %get-tuple-element.52.side, bf16[3,512,512]{2,1,0:T(8,128)(2,1)S(1)} %collective-permute-done.11.root, f32[1,1024]{1,0:T(1,128)S(1)} %get-tuple-element.53.grad_sum), custom_call_target="tpu_custom_call" | custom-call | flops 2147483648 | bytes 6291456 | tf_op jit(solution)/shard_map/apply_other_root/pallas_call | solution.py:299
  81.4 19.0 %all_to_all.11 = bf16[16,32,1024]{2,1,0:T(8,128)(2,1)S(1)} all-to-all(bf16[16,32,1024]{2,1,0:T(8,128)(2,1)S(1)} %bitcast.25), channel_id=1, replica_groups=mesh['z'=4,'core'=2,'y'=4,'x'=4] {'y','x'}, dimensions={0} | all-to-all | bytes 2097152 | tf_op jit(solution)/shard_map/rows_to_shards/all_to_all | solution.py:311
  102.7 2.7 %collective-permute-start.12 = (bf16[6,32,1024]{2,1,0:T(8,128)(2,1)S(1)}, bf16[6,32,1024]{2,1,0:T(8,128)(2,1)S(1)}, u32[]{:S(2)}, u32[]{:S(2)}) collective-permute-start(bf16[6,32,1024]{2,1,0:T(8,128)(2,1)S(1)} %get-tuple-element.57), channel_id=1, source_target_pairs={{0,96},{32,0},{64,32},{96,64},{1,97},{33,1},{65,33},{97,65},{2,98}... | collective-permute-start | bytes 1179656 | tf_op jit(solution)/shard_map/gather_over_replicas/ppermute | solution.py:344
  108.2 6.4 %collective-permute-done.13.refs_3_ = bf16[6,32,1024]{2,1,0:T(8,128)(2,1)S(1)} collective-permute-done((bf16[6,32,1024]{2,1,0:T(8,128)(2,1)S(1)}, bf16[6,32,1024]{2,1,0:T(8,128)(2,1)S(1)}, u32[]{:S(2)}, u32[]{:S(2)}) %collective-permute-start.13) | collective-permute-done | bytes 393248 | tf_op jit(solution)/shard_map/gather_over_replicas/ppermute | solution.py:345
  114.6 2.4 %collective-permute-start.21 = (bf16[6,32,1024]{2,1,0:T(8,128)(2,1)S(1)}, bf16[6,32,1024]{2,1,0:T(8,128)(2,1)S(1)}, u32[]{:S(2)}, u32[]{:S(2)}) collective-permute-start(bf16[6,32,1024]{2,1,0:T(8,128)(2,1)S(1)} %collective-permute-done.12.refs_2_), channel_id=1, source_target_pairs={{0,96},{32,0},{64,32},{96,64},{1,97},{33,1},{65,33},{97,65},{2,98}... | collective-permute-start | bytes 1179656 | tf_op jit(solution)/shard_map/gather_over_replicas/ppermute | solution.py:353
  117.0 2.2 %collective-permute-start.15 = (bf16[12,32,1024]{2,1,0:T(8,128)(2,1)S(1)}, bf16[12,32,1024]{2,1,0:T(8,128)(2,1)S(1)}, u32[]{:S(2)}, u32[]{:S(2)}) collective-permute-start(bf16[12,32,1024]{2,1,0:T(8,128)(2,1)S(1)} %pad_maximum_fusion), channel_id=1, source_target_pairs={{0,16},{16,0},{1,17},{17,1},{2,18},{18,2},{3,19},{19,3},{4,20},{20... | collective-permute-start | bytes 2359304 | tf_op jit(solution)/shard_map/gather_over_replicas/ppermute | solution.py:341
  119.2 2.7 %collective-permute-done.17.refs_4_ = bf16[6,32,1024]{2,1,0:T(8,128)(2,1)S(1)} collective-permute-done((bf16[6,32,1024]{2,1,0:T(8,128)(2,1)S(1)}, bf16[6,32,1024]{2,1,0:T(8,128)(2,1)S(1)}, u32[]{:S(2)}, u32[]{:S(2)}) %collective-permute-start.17) | collective-permute-done | bytes 393248 | tf_op jit(solution)/shard_map/gather_over_replicas/ppermute | solution.py:348
  123.0 2.3 %place_early.1.refs_7_ = bf16[48,64,1024]{2,1,0:T(8,128)(2,1)} custom-call(s32[3]{0:T(128)S(1)} %pad_add_fusion.place, bf16[12,32,1024]{2,1,0:T(8,128)(2,1)S(1)} %slice.63.refs_0_, bf16[12,32,1024]{2,1,0:T(8,128)(2,1)S(1)} %collective-permute-done.14.refs_1_, bf16[6,32,1024]{2,1,0:T(8,128)(2,1)S(1)} %collective-permute-done.12.refs_2_, ...), custom_call_target="tpu_custom_call" | custom-call | bytes 6291456 | tf_op jit(solution)/shard_map/gather_over_replicas/place_early/pallas_call | solution.py:328
  126.6 3.8 %collective-permute-done.21.refs_3_ = bf16[6,32,1024]{2,1,0:T(8,128)(2,1)S(1)} collective-permute-done((bf16[6,32,1024]{2,1,0:T(8,128)(2,1)S(1)}, bf16[6,32,1024]{2,1,0:T(8,128)(2,1)S(1)}, u32[]{:S(2)}, u32[]{:S(2)}) %collective-permute-start.21) | collective-permute-done | bytes 393248 | tf_op jit(solution)/shard_map/gather_over_replicas/ppermute | solution.py:353
  133.6 2.3 %place_late.1 = bf16[48,64,1024]{2,1,0:T(8,128)(2,1)} custom-call(s32[3]{0:T(128)S(1)} %pad_add_fusion.place, bf16[12,32,1024]{2,1,0:T(8,128)(2,1)S(1)} %collective-permute-done.15.refs_0_, bf16[6,32,1024]{2,1,0:T(8,128)(2,1)S(1)} %collective-permute-done.19.refs_1_, ...), custom_call_target="tpu_custom_call", output_to_operand_aliasing={{}: (8, {})} | custom-call | bytes 6291456 | tf_op jit(solution)/shard_map/gather_over_replicas/place_late/pallas_call | solution.py:328
  (57 shorter events, 23.0 us)
Async XLA Ops:
  2.1 4.4 %collective-permute-start = (bf16[12,32,1024]{2,1,0:T(8,128)(2,1)}, bf16[12,32,1024]{2,1,0:T(8,128)(2,1)}, u32[]{:S(2)}, u32[]{:S(2)}) collective-permute-start(bf16[12,32,1024]{2,1,0:T(8,128)(2,1)} %dynamic-slice_bitcast_fusion.7), channel_id=1, source_target_pairs={{0,16},{16,0},{1,17},{17,1},{2,18},{18,2},{3,19},{19,3},{4,20},{20... | collective-permute-start | bytes 2359304 | tf_op jit(solution)/shard_map/sum_over_replicas/ppermute | solution.py:235
  5.7 8.0 %collective-permute-start.4 = (bf16[12,32,1024]{2,1,0:T(8,128)(2,1)S(1)}, bf16[12,32,1024]{2,1,0:T(8,128)(2,1)}, u32[]{:S(2)}, u32[]{:S(2)}) collective-permute-start(bf16[12,32,1024]{2,1,0:T(8,128)(2,1)S(1)} %get-tuple-element.44), channel_id=1, source_target_pairs={{0,16},{16,0},{1,17},{17,1},{2,18},{18,2},{3,19},{19,3},{4,20},{20... | collective-permute-start | bytes 2359304 | tf_op jit(solution)/shard_map/sum_over_replicas/ppermute | solution.py:239
  5.8 23.9 %collective-permute-start.1 = (bf16[12,32,1024]{2,1,0:T(8,128)(2,1)S(1)}, bf16[12,32,1024]{2,1,0:T(8,128)(2,1)}, u32[]{:S(2)}, u32[]{:S(2)}) collective-permute-start(bf16[12,32,1024]{2,1,0:T(8,128)(2,1)S(1)} %get-tuple-element.39), channel_id=1, source_target_pairs={{0,16},{16,0},{1,17},{17,1},{2,18},{18,2},{3,19},{19,3},{4,20},{20... | collective-permute-start | bytes 2359304 | tf_op jit(solution)/shard_map/sum_over_replicas/ppermute | solution.py:239
  6.3 8.9 %collective-permute-start.2 = (bf16[12,32,1024]{2,1,0:T(8,128)(2,1)S(1)}, bf16[12,32,1024]{2,1,0:T(8,128)(2,1)}, u32[]{:S(2)}, u32[]{:S(2)}) collective-permute-start(bf16[12,32,1024]{2,1,0:T(8,128)(2,1)S(1)} %get-tuple-element.41), channel_id=1, source_target_pairs={{0,16},{16,0},{1,17},{17,1},{2,18},{18,2},{3,19},{19,3},{4,20},{20... | collective-permute-start | bytes 2359304 | tf_op jit(solution)/shard_map/sum_over_replicas/ppermute | solution.py:239
  8.0 17.1 %collective-permute-start.5 = (bf16[6,32,1024]{2,1,0:T(8,128)(2,1)S(1)}, bf16[6,32,1024]{2,1,0:T(8,128)(2,1)}, u32[]{:S(2)}, u32[]{:S(2)}) collective-permute-start(bf16[6,32,1024]{2,1,0:T(8,128)(2,1)S(1)} %get-tuple-element.45), channel_id=1, source_target_pairs={{0,96},{32,0},{64,32},{96,64},{1,97},{33,1},{65,33},{97,65},{2,98}... | collective-permute-start | bytes 1179656 | tf_op jit(solution)/shard_map/sum_over_replicas/ppermute | solution.py:242
  11.9 11.3 %collective-permute-start.8 = (bf16[6,32,1024]{2,1,0:T(8,128)(2,1)S(1)}, bf16[6,32,1024]{2,1,0:T(8,128)(2,1)}, u32[]{:S(2)}, u32[]{:S(2)}) collective-permute-start(bf16[6,32,1024]{2,1,0:T(8,128)(2,1)S(1)} %get-tuple-element.46), channel_id=1, source_target_pairs={{0,32},{32,64},{64,96},{96,0},{1,33},{33,65},{65,97},{97,1},{2,34}... | collective-permute-start | bytes 1179656 | tf_op jit(solution)/shard_map/sum_over_replicas/ppermute | solution.py:243
  16.7 14.8 %collective-permute-start.3 = (bf16[6,32,1024]{2,1,0:T(8,128)(2,1)S(1)}, bf16[6,32,1024]{2,1,0:T(8,128)(2,1)S(1)}, u32[]{:S(2)}, u32[]{:S(2)}) collective-permute-start(bf16[6,32,1024]{2,1,0:T(8,128)(2,1)S(1)} %slice.56), channel_id=1, source_target_pairs={{0,32},{32,64},{64,96},{96,0},{1,33},{33,65},{65,97},{97,1},{2,34}... | collective-permute-start | bytes 1179656 | tf_op jit(solution)/shard_map/sum_over_replicas/ppermute | solution.py:250
  16.8 16.1 %collective-permute-start.7 = (bf16[6,32,1024]{2,1,0:T(8,128)(2,1)S(1)}, bf16[6,32,1024]{2,1,0:T(8,128)(2,1)S(1)}, u32[]{:S(2)}, u32[]{:S(2)}) collective-permute-start(bf16[6,32,1024]{2,1,0:T(8,128)(2,1)S(1)} %slice.59), channel_id=1, source_target_pairs={{0,96},{32,0},{64,32},{96,64},{1,97},{33,1},{65,33},{97,65},{2,98}... | collective-permute-start | bytes 1179656 | tf_op jit(solution)/shard_map/sum_over_replicas/ppermute | solution.py:251
  25.1 14.9 %collective-permute-start.9 = (bf16[6,32,1024]{2,1,0:T(8,128)(2,1)}, bf16[6,32,1024]{2,1,0:T(8,128)(2,1)S(1)}, u32[]{:S(2)}, u32[]{:S(2)}) collective-permute-start(bf16[6,32,1024]{2,1,0:T(8,128)(2,1)} %add_convert_fusion.5), channel_id=1, source_target_pairs={{0,32},{32,64},{64,96},{96,0},{1,33},{33,65},{65,97},{97,1},{2,34}... | collective-permute-start | bytes 1179656 | tf_op jit(solution)/shard_map/sum_over_replicas/ppermute | solution.py:254
  27.0 13.0 %collective-permute-start.6 = (bf16[6,32,1024]{2,1,0:T(8,128)(2,1)}, bf16[6,32,1024]{2,1,0:T(8,128)(2,1)S(1)}, u32[]{:S(2)}, u32[]{:S(2)}) collective-permute-start(bf16[6,32,1024]{2,1,0:T(8,128)(2,1)} %add_convert_fusion.7), channel_id=1, source_target_pairs={{0,96},{32,0},{64,32},{96,64},{1,97},{33,1},{65,33},{97,65},{2,98}... | collective-permute-start | bytes 1179656 | tf_op jit(solution)/shard_map/sum_over_replicas/ppermute | solution.py:253
  62.5 5.1 %collective-permute-start.10 = (bf16[512,1024]{1,0:T(8,128)(2,1)S(1)}, bf16[512,1024]{1,0:T(8,128)(2,1)S(1)}, u32[]{:S(2)}, u32[]{:S(2)}) collective-permute-start(bf16[512,1024]{1,0:T(8,128)(2,1)S(1)} %bitcast.22), channel_id=1, source_target_pairs={{0,16},{16,0},{1,17},{17,1},{2,18},{18,2},{3,19},{19,3},{4,20},{20... | collective-permute-start | bytes 3145736 | tf_op jit(solution)/shard_map/rows_to_owner/ppermute | solution.py:271
  74.7 3.5 %collective-permute-start.11 = (bf16[3,512,512]{2,1,0:T(8,128)(2,1)S(1)}, bf16[3,512,512]{2,1,0:T(8,128)(2,1)S(1)}, u32[]{:S(2)}, u32[]{:S(2)}) collective-permute-start(bf16[3,512,512]{2,1,0:T(8,128)(2,1)S(1)} %get-tuple-element.50.root), channel_id=1, source_target_pairs={{0,16},{16,0},{1,17},{17,1},{2,18},{18,2},{3,19},{19,3},{4,20},{20... | collective-permute-start | bytes 4718600 | tf_op jit(solution)/shard_map/ppermute | solution.py:289
  100.5 14.1 %collective-permute-start.14 = (bf16[12,32,1024]{2,1,0:T(8,128)(2,1)S(1)}, bf16[12,32,1024]{2,1,0:T(8,128)(2,1)S(1)}, u32[]{:S(2)}, u32[]{:S(2)}) collective-permute-start(bf16[12,32,1024]{2,1,0:T(8,128)(2,1)S(1)} %slice.63.refs_0_), channel_id=1, source_target_pairs={{0,16},{16,0},{1,17},{17,1},{2,18},{18,2},{3,19},{19,3},{4,20},{20... | collective-permute-start | bytes 2359304 | tf_op jit(solution)/shard_map/gather_over_replicas/ppermute | solution.py:341
  102.4 12.2 %collective-permute-start.13 = (bf16[6,32,1024]{2,1,0:T(8,128)(2,1)S(1)}, bf16[6,32,1024]{2,1,0:T(8,128)(2,1)S(1)}, u32[]{:S(2)}, u32[]{:S(2)}) collective-permute-start(bf16[6,32,1024]{2,1,0:T(8,128)(2,1)S(1)} %get-tuple-element.56), channel_id=1, source_target_pairs={{0,32},{32,64},{64,96},{96,0},{1,33},{33,65},{65,97},{97,1},{2,34}... | collective-permute-start | bytes 1179656 | tf_op jit(solution)/shard_map/gather_over_replicas/ppermute | solution.py:345
  102.7 11.9 %collective-permute-start.12 = (bf16[6,32,1024]{2,1,0:T(8,128)(2,1)S(1)}, bf16[6,32,1024]{2,1,0:T(8,128)(2,1)S(1)}, u32[]{:S(2)}, u32[]{:S(2)}) collective-permute-start(bf16[6,32,1024]{2,1,0:T(8,128)(2,1)S(1)} %get-tuple-element.57), channel_id=1, source_target_pairs={{0,96},{32,0},{64,32},{96,64},{1,97},{33,1},{65,33},{97,65},{2,98}... | collective-permute-start | bytes 1179656 | tf_op jit(solution)/shard_map/gather_over_replicas/ppermute | solution.py:344
  106.7 15.2 %collective-permute-start.17 = (bf16[6,32,1024]{2,1,0:T(8,128)(2,1)S(1)}, bf16[6,32,1024]{2,1,0:T(8,128)(2,1)S(1)}, u32[]{:S(2)}, u32[]{:S(2)}) collective-permute-start(bf16[6,32,1024]{2,1,0:T(8,128)(2,1)S(1)} %get-tuple-element.56), channel_id=1, source_target_pairs={{0,96},{32,0},{64,32},{96,64},{1,97},{33,1},{65,33},{97,65},{2,98}... | collective-permute-start | bytes 1179656 | tf_op jit(solution)/shard_map/gather_over_replicas/ppermute | solution.py:348
  106.7 16.3 %collective-permute-start.18 = (bf16[6,32,1024]{2,1,0:T(8,128)(2,1)S(1)}, bf16[6,32,1024]{2,1,0:T(8,128)(2,1)S(1)}, u32[]{:S(2)}, u32[]{:S(2)}) collective-permute-start(bf16[6,32,1024]{2,1,0:T(8,128)(2,1)S(1)} %get-tuple-element.57), channel_id=1, source_target_pairs={{0,32},{32,64},{64,96},{96,0},{1,33},{33,65},{65,97},{97,1},{2,34}... | collective-permute-start | bytes 1179656 | tf_op jit(solution)/shard_map/gather_over_replicas/ppermute | solution.py:349
  114.6 15.8 %collective-permute-start.21 = (bf16[6,32,1024]{2,1,0:T(8,128)(2,1)S(1)}, bf16[6,32,1024]{2,1,0:T(8,128)(2,1)S(1)}, u32[]{:S(2)}, u32[]{:S(2)}) collective-permute-start(bf16[6,32,1024]{2,1,0:T(8,128)(2,1)S(1)} %collective-permute-done.12.refs_2_), channel_id=1, source_target_pairs={{0,96},{32,0},{64,32},{96,64},{1,97},{33,1},{65,33},{97,65},{2,98}... | collective-permute-start | bytes 1179656 | tf_op jit(solution)/shard_map/gather_over_replicas/ppermute | solution.py:353
  117.0 14.6 %collective-permute-start.22 = (bf16[6,32,1024]{2,1,0:T(8,128)(2,1)S(1)}, bf16[6,32,1024]{2,1,0:T(8,128)(2,1)S(1)}, u32[]{:S(2)}, u32[]{:S(2)}) collective-permute-start(bf16[6,32,1024]{2,1,0:T(8,128)(2,1)S(1)} %collective-permute-done.13.refs_3_), channel_id=1, source_target_pairs={{0,32},{32,64},{64,96},{96,0},{1,33},{33,65},{65,97},{97,1},{2,34}... | collective-permute-start | bytes 1179656 | tf_op jit(solution)/shard_map/gather_over_replicas/ppermute | solution.py:354
  117.0 16.6 %collective-permute-start.15 = (bf16[12,32,1024]{2,1,0:T(8,128)(2,1)S(1)}, bf16[12,32,1024]{2,1,0:T(8,128)(2,1)S(1)}, u32[]{:S(2)}, u32[]{:S(2)}) collective-permute-start(bf16[12,32,1024]{2,1,0:T(8,128)(2,1)S(1)} %pad_maximum_fusion), channel_id=1, source_target_pairs={{0,16},{16,0},{1,17},{17,1},{2,18},{18,2},{3,19},{19,3},{4,20},{20... | collective-permute-start | bytes 2359304 | tf_op jit(solution)/shard_map/gather_over_replicas/ppermute | solution.py:341
  125.3 7.0 %collective-permute-start.19 = (bf16[6,32,1024]{2,1,0:T(8,128)(2,1)S(1)}, bf16[6,32,1024]{2,1,0:T(8,128)(2,1)S(1)}, u32[]{:S(2)}, u32[]{:S(2)}) collective-permute-start(bf16[6,32,1024]{2,1,0:T(8,128)(2,1)S(1)} %collective-permute-done.17.refs_4_), channel_id=1, source_target_pairs={{0,16},{16,0},{1,17},{17,1},{2,18},{18,2},{3,19},{19,3},{4,20},{20... | collective-permute-start | bytes 1179656 | tf_op jit(solution)/shard_map/gather_over_replicas/ppermute | solution.py:341
  126.6 5.7 %collective-permute-start.20 = (bf16[6,32,1024]{2,1,0:T(8,128)(2,1)S(1)}, bf16[6,32,1024]{2,1,0:T(8,128)(2,1)S(1)}, u32[]{:S(2)}, u32[]{:S(2)}) collective-permute-start(bf16[6,32,1024]{2,1,0:T(8,128)(2,1)S(1)} %collective-permute-done.18.refs_5_), channel_id=1, source_target_pairs={{0,16},{16,0},{1,17},{17,1},{2,18},{18,2},{3,19},{19,3},{4,20},{20... | collective-permute-start | bytes 1179656 | tf_op jit(solution)/shard_map/gather_over_replicas/ppermute | solution.py:341
  130.4 2.5 %collective-permute-start.23 = (bf16[6,32,1024]{2,1,0:T(8,128)(2,1)S(1)}, bf16[6,32,1024]{2,1,0:T(8,128)(2,1)S(1)}, u32[]{:S(2)}, u32[]{:S(2)}) collective-permute-start(bf16[6,32,1024]{2,1,0:T(8,128)(2,1)S(1)} %collective-permute-done.21.refs_3_), channel_id=1, source_target_pairs={{0,16},{16,0},{1,17},{17,1},{2,18},{18,2},{3,19},{19,3},{4,20},{20... | collective-permute-start | bytes 1179656 | tf_op jit(solution)/shard_map/gather_over_replicas/ppermute | solution.py:341
  131.5 2.1 %collective-permute-start.24 = (bf16[6,32,1024]{2,1,0:T(8,128)(2,1)S(1)}, bf16[6,32,1024]{2,1,0:T(8,128)(2,1)S(1)}, u32[]{:S(2)}, u32[]{:S(2)}) collective-permute-start(bf16[6,32,1024]{2,1,0:T(8,128)(2,1)S(1)} %collective-permute-done.22.refs_4_), channel_id=1, source_target_pairs={{0,16},{16,0},{1,17},{17,1},{2,18},{18,2},{3,19},{19,3},{4,20},{20... | collective-permute-start | bytes 1179656 | tf_op jit(solution)/shard_map/gather_over_replicas/ppermute | solution.py:341
  (2 other events, 7.8 us)

commit v5 on v4

--- a/solution.py
+++ b/solution.py
@@ -20,6 +20,14 @@
 
 def rows_at(start, count):
     return pl.ds(pl.multiple_of(start, count), count)
+
+
+def add_kernel(one, two, *outs):
+    start = 0
+    for out in outs:
+        run = slice(start, start + out.shape[0])
+        out[...] = (one[run].astype(jnp.float32) + two[run].astype(jnp.float32)).astype(out.dtype)
+        start += out.shape[0]
 
 
 def root_kernel(place, own, sibling, root, grad, stat, step, square, coupled, fourth):
@@ -237,8 +245,18 @@
             [rows_of(next_plane, 2, core)] + [rows_of(next_plane, k, 1 - core) for k in (1, 3, 0)]
         )
         got_above, got_below, got_mine = (lax.ppermute(each, "core", swap) for each in sent)
-        far = plus(kept, got)
-        far_low, far_high, here = lax.optimization_barrier((far[:part], far[part:], plane))
+        far_low, far_high = pl.pallas_call(
+            add_kernel,
+            out_shape=[jax.ShapeDtypeStruct((part, rows, width), jnp.bfloat16)] * 2,
+            in_specs=[vmem] * 2,
+            out_specs=[vmem] * 2,
+            compiler_params=pltpu.CompilerParams(vmem_limit_bytes=8 * mib),
+            cost_estimate=pl.CostEstimate(
+                flops=kept.size, bytes_accessed=6 * kept.size, transcendentals=0
+            ),
+            name="add_rows",
+        )(kept, got)
+        far_low, far_high, here = lax.optimization_barrier((far_low, far_high, plane))
         from_above = lax.ppermute(far_low, "z", down)
         from_below = lax.ppermute(far_high, "z", up)
         kept_above, kept_below, kept_mine = lax.optimization_barrier(

time: 137 us -> 136 us (level)
  other arithmetic: 10.9 us -> 7.54 us
  waiting for transfers between devices: 29.6 us -> 31.5 us
    convert_element_type x7 -> x6, other arithmetic: 9.97 us -> 6.55 us  [plus(): return total.astype(jnp.bfloat16)]
    ppermute x1, waiting for transfers between devices: 0.42 us -> 2.51 us  [local(): low_below = lax.ppermute(to_above[:part], 'z', up)]
  transfers between devices with their start and end apart: 25 -> 25, of which waited for: 12 -> 12; matrix products, arithmetic and copies ran while one was open for 11% -> 9% of each run, Pallas kernels for 4% -> 4%
where the time goes in v5:
time: 136 us; the launch traced here: 135 us
  blocking collectives  41 us (30%)
  waiting for transfers between devices  31.5 us (23%)
  starting transfers between devices  29.3 us (22%)
  Pallas kernels  18 us (13%)
  other arithmetic  7.54 us (6%)
  local copies, waits for them, and re-layouts  6.75 us (5%)
    all_to_all x1, blocking collectives, local(): lax.all_to_all(summed, ('y', 'x'), 0, 0, tiled=True).reshape(half, width)  22 us
    all_to_all x1, blocking collectives, local(): lax.all_to_all(finished.reshape(shards, rows, width), ('y', 'x'), 0, 0, t...  19 us
    ppermute x7, starting transfers between devices, other_core(): return lax.ppermute(piece, 'core', swap)  7.79 us
    pallas_call x1, Pallas kernels, local(): pl.pallas_call(root_kernel, out_shape=[jax.ShapeDtypeStruct((3, half, hal...  7.13 us
    ppermute x1, waiting for transfers between devices, local(): high_below = lax.ppermute(plus(to_above[part:], from_below), 'z', up)  6.96 us
    convert_element_type x6, other arithmetic, plus(): return total.astype(jnp.bfloat16)  6.55 us
    reshape x3, local copies, waits for them, and re-layouts, rows_of(): return sliced.reshape(per_plane, rows, width)  6.49 us
    ppermute x1, waiting for transfers between devices, local(): below_high = lax.ppermute(back[part:], 'z', up)  6.4 us
  transfers between devices with their start and end apart: 25, of which 12 were waited for; matrix products, arithmetic and copies ran while one was open for 9% of the time, Pallas kernels for 4%

profile of v5, /device:TPU:1, one launch (start us, length us, event | category | flops | bytes accessed | tf_op | source)
XLA Modules:
  0.0 135.1 jit_solution(13450459633678889637)
XLA Ops:
  2.7 3.5 %dynamic-slice_bitcast_fusion.3 = (bf16[12,32,1024]{2,1,0:T(8,128)(2,1)S(1)}, bf16[12,32,1024]{2,1,0:T(8,128)(2,1)}, bf16[12,32,1024]{2,1,0:T(8,128)(2,1)}, bf16[12,32,1024]{2,1,0:T(8,128)(2,1)S(1)}) fusion(bf16[4,12,2,32,1024]{4,3,2,1,0:T(8,128)(2,1)} %bitcast.43, s32[]{:T(128)S(6)} %select_n.82, s32[]{:T(128)S(6)} %select_n.73, s32[]{:T(128)S(6)} %select_n.80, ...), kind=kLoop, calls=%fused_computation.12 | loop fusion | bytes 6291480 | tf_op jit(solution)/shard_map/sum_over_replicas/reshape | solution.py:239
  7.1 3.9 %collective-permute-start.5 = (bf16[6,32,1024]{2,1,0:T(8,128)(2,1)S(1)}, bf16[6,32,1024]{2,1,0:T(8,128)(2,1)S(1)}, u32[]{:S(2)}, u32[]{:S(2)}) collective-permute-start(bf16[6,32,1024]{2,1,0:T(8,128)(2,1)S(1)} %get-tuple-element.49), channel_id=1, source_target_pairs={{0,96},{32,0},{64,32},{96,64},{1,97},{33,1},{65,33},{97,65},{2,98}... | collective-permute-start | bytes 1179656 | tf_op jit(solution)/shard_map/sum_over_replicas/ppermute | solution.py:260
  11.0 1.8 %dynamic-slice_bitcast_fusion = (bf16[12,32,1024]{2,1,0:T(8,128)(2,1)S(1)}, bf16[12,32,1024]{2,1,0:T(8,128)(2,1)S(1)}, bf16[12,32,1024]{2,1,0:T(8,128)(2,1)S(1)}) fusion(bf16[4,12,2,32,1024]{4,3,2,1,0:T(8,128)(2,1)} %bitcast.44, s32[]{:T(128)S(6)} %select_n.88, s32[]{:T(128)S(6)} %select_n.76, s32[]{:T(128)S(6)} %select_n.86, s32[]{:T(128)S(6)} %select_n.84), kind=kLoop, calls=%fused_computation.9 | loop fusion | bytes 4718608 | tf_op jit(solution)/shard_map/sum_over_replicas/reshape | solution.py:239
  15.9 2.7 %collective-permute-start.7 = (bf16[6,32,1024]{2,1,0:T(8,128)(2,1)S(1)}, bf16[6,32,1024]{2,1,0:T(8,128)(2,1)S(1)}, u32[]{:S(2)}, u32[]{:S(2)}) collective-permute-start(bf16[6,32,1024]{2,1,0:T(8,128)(2,1)S(1)} %slice.49), channel_id=1, source_target_pairs={{0,96},{32,0},{64,32},{96,64},{1,97},{33,1},{65,33},{97,65},{2,98}... | collective-permute-start | bytes 1179656 | tf_op jit(solution)/shard_map/sum_over_replicas/ppermute | solution.py:269
  18.6 3.5 %collective-permute-done.8 = bf16[6,32,1024]{2,1,0:T(8,128)(2,1)S(1)} collective-permute-done((bf16[6,32,1024]{2,1,0:T(8,128)(2,1)S(1)}, bf16[6,32,1024]{2,1,0:T(8,128)(2,1)S(1)}, u32[]{:S(2)}, u32[]{:S(2)}) %collective-permute-start.8) | collective-permute-done | bytes 393248 | tf_op jit(solution)/shard_map/sum_over_replicas/ppermute | solution.py:261
  24.0 2.7 %collective-permute-start.6 = (bf16[6,32,1024]{2,1,0:T(8,128)(2,1)}, bf16[6,32,1024]{2,1,0:T(8,128)(2,1)S(1)}, u32[]{:S(2)}, u32[]{:S(2)}) collective-permute-start(bf16[6,32,1024]{2,1,0:T(8,128)(2,1)} %add_convert_fusion.6), channel_id=1, source_target_pairs={{0,96},{32,0},{64,32},{96,64},{1,97},{33,1},{65,33},{97,65},{2,98}... | collective-permute-start | bytes 1179656 | tf_op jit(solution)/shard_map/sum_over_replicas/ppermute | solution.py:271
  28.1 2.5 %collective-permute-done.3 = bf16[6,32,1024]{2,1,0:T(8,128)(2,1)S(1)} collective-permute-done((bf16[6,32,1024]{2,1,0:T(8,128)(2,1)S(1)}, bf16[6,32,1024]{2,1,0:T(8,128)(2,1)S(1)}, u32[]{:S(2)}, u32[]{:S(2)}) %collective-permute-start.3) | collective-permute-done | bytes 393248 | tf_op jit(solution)/shard_map/sum_over_replicas/ppermute | solution.py:268
  32.0 7.0 %collective-permute-done.9 = bf16[6,32,1024]{2,1,0:T(8,128)(2,1)S(1)} collective-permute-done((bf16[6,32,1024]{2,1,0:T(8,128)(2,1)}, bf16[6,32,1024]{2,1,0:T(8,128)(2,1)S(1)}, u32[]{:S(2)}, u32[]{:S(2)}) %collective-permute-start.9) | collective-permute-done | bytes 393248 | tf_op jit(solution)/shard_map/sum_over_replicas/ppermute | solution.py:272
  39.6 22.0 %all_to_all.10 = bf16[16,32,1024]{2,1,0:T(8,128)(2,1)S(1)} all-to-all(bf16[16,32,1024]{2,1,0:T(8,128)(2,1)S(1)} %maximum_maximum_fusion), channel_id=1, replica_groups=mesh['z'=4,'core'=2,'y'=4,'x'=4] {'y','x'}, dimensions={0} | all-to-all | bytes 2097152 | tf_op jit(solution)/shard_map/rows_to_owner/all_to_all | solution.py:288
  61.6 2.8 %collective-permute-start.10 = (bf16[512,1024]{1,0:T(8,128)(2,1)S(1)}, bf16[512,1024]{1,0:T(8,128)(2,1)S(1)}, u32[]{:S(2)}, u32[]{:S(2)}) collective-permute-start(bf16[512,1024]{1,0:T(8,128)(2,1)S(1)} %bitcast.38), channel_id=1, source_target_pairs={{0,16},{16,0},{1,17},{17,1},{2,18},{18,2},{3,19},{19,3},{4,20},{20... | collective-permute-start | bytes 3145736 | tf_op jit(solution)/shard_map/rows_to_owner/ppermute | solution.py:289
  64.4 2.3 %collective-permute-done.10.sibling = bf16[512,1024]{1,0:T(8,128)(2,1)S(1)} collective-permute-done((bf16[512,1024]{1,0:T(8,128)(2,1)S(1)}, bf16[512,1024]{1,0:T(8,128)(2,1)S(1)}, u32[]{:S(2)}, u32[]{:S(2)}) %collective-permute-start.10) | collective-permute-done | bytes 1048608 | tf_op jit(solution)/shard_map/rows_to_owner/ppermute | solution.py:289
  66.7 7.1 %inverse_root.1 = (bf16[3,512,512]{2,1,0:T(8,128)(2,1)S(1)}, bf16[1024,1024]{1,0:T(8,128)(2,1)S(1)}) custom-call(s32[3]{0:T(128)S(1)} %pad_add_fusion.place, bf16[512,1024]{1,0:T(8,128)(2,1)S(1)} %bitcast.39, bf16[512,1024]{1,0:T(8,128)(2,1)S(1)} %collective-permute-done.10.sibling), custom_call_target="tpu_custom_call" | custom-call | flops 6442450944 | bytes 6291456 | tf_op jit(solution)/shard_map/inverse_root/pallas_call | solution.py:294
  74.2 3.0 %apply_own_root.1 = (bf16[1024,1024]{1,0:T(8,128)(2,1)S(1)}, f32[1,1024]{1,0:T(1,128)S(1)}) custom-call(s32[3]{0:T(128)S(1)} %pad_add_fusion.place, bf16[3,512,512]{2,1,0:T(8,128)(2,1)S(1)} %get-tuple-element.54.root, bf16[1024,1024]{1,0:T(8,128)(2,1)S(1)} %get-tuple-element.55.grad), custom_call_target="tpu_custom_call" | custom-call | flops 2147483648 | bytes 6291456 | tf_op jit(solution)/shard_map/apply_own_root/pallas_call | solution.py:308
  77.3 3.1 %apply_other_root.1 = bf16[512,1024]{1,0:T(8,128)(2,1)S(1)} custom-call(s32[3]{0:T(128)S(1)} %pad_add_fusion.place, bf16[512,1024]{1,0:T(8,128)(2,1)S(1)} %bitcast.40, bf16[1024,1024]{1,0:T(8,128)(2,1)S(1)} %get-tuple-element.56.side, bf16[3,512,512]{2,1,0:T(8,128)(2,1)S(1)} %collective-permute-done.11.root, f32[1,1024]{1,0:T(1,128)S(1)} %get-tuple-element.57.grad_sum), custom_call_target="tpu_custom_call" | custom-call | flops 2147483648 | bytes 6291456 | tf_op jit(solution)/shard_map/apply_other_root/pallas_call | solution.py:317
  80.4 19.0 %all_to_all.11 = bf16[16,32,1024]{2,1,0:T(8,128)(2,1)S(1)} all-to-all(bf16[16,32,1024]{2,1,0:T(8,128)(2,1)S(1)} %bitcast.41), channel_id=1, replica_groups=mesh['z'=4,'core'=2,'y'=4,'x'=4] {'y','x'}, dimensions={0} | all-to-all | bytes 2097152 | tf_op jit(solution)/shard_map/rows_to_shards/all_to_all | solution.py:329
  99.5 1.8 %collective-permute-start.14 = (bf16[12,32,1024]{2,1,0:T(8,128)(2,1)S(1)}, bf16[12,32,1024]{2,1,0:T(8,128)(2,1)S(1)}, u32[]{:S(2)}, u32[]{:S(2)}) collective-permute-start(bf16[12,32,1024]{2,1,0:T(8,128)(2,1)S(1)} %slice.53.refs_0_), channel_id=1, source_target_pairs={{0,16},{16,0},{1,17},{17,1},{2,18},{18,2},{3,19},{19,3},{4,20},{20... | collective-permute-start | bytes 2359304 | tf_op jit(solution)/shard_map/gather_over_replicas/ppermute | solution.py:359
  101.7 2.7 %collective-permute-start.12 = (bf16[6,32,1024]{2,1,0:T(8,128)(2,1)S(1)}, bf16[6,32,1024]{2,1,0:T(8,128)(2,1)S(1)}, u32[]{:S(2)}, u32[]{:S(2)}) collective-permute-start(bf16[6,32,1024]{2,1,0:T(8,128)(2,1)S(1)} %get-tuple-element.61), channel_id=1, source_target_pairs={{0,96},{32,0},{64,32},{96,64},{1,97},{33,1},{65,33},{97,65},{2,98}... | collective-permute-start | bytes 1179656 | tf_op jit(solution)/shard_map/gather_over_replicas/ppermute | solution.py:362
  107.2 6.4 %collective-permute-done.13.refs_3_ = bf16[6,32,1024]{2,1,0:T(8,128)(2,1)S(1)} collective-permute-done((bf16[6,32,1024]{2,1,0:T(8,128)(2,1)S(1)}, bf16[6,32,1024]{2,1,0:T(8,128)(2,1)S(1)}, u32[]{:S(2)}, u32[]{:S(2)}) %collective-permute-start.13) | collective-permute-done | bytes 393248 | tf_op jit(solution)/shard_map/gather_over_replicas/ppermute | solution.py:363
  113.6 2.4 %collective-permute-start.21 = (bf16[6,32,1024]{2,1,0:T(8,128)(2,1)S(1)}, bf16[6,32,1024]{2,1,0:T(8,128)(2,1)S(1)}, u32[]{:S(2)}, u32[]{:S(2)}) collective-permute-start(bf16[6,32,1024]{2,1,0:T(8,128)(2,1)S(1)} %collective-permute-done.12.refs_2_), channel_id=1, source_target_pairs={{0,96},{32,0},{64,32},{96,64},{1,97},{33,1},{65,33},{97,65},{2,98}... | collective-permute-start | bytes 1179656 | tf_op jit(solution)/shard_map/gather_over_replicas/ppermute | solution.py:371
  116.1 2.2 %collective-permute-start.15 = (bf16[12,32,1024]{2,1,0:T(8,128)(2,1)S(1)}, bf16[12,32,1024]{2,1,0:T(8,128)(2,1)S(1)}, u32[]{:S(2)}, u32[]{:S(2)}) collective-permute-start(bf16[12,32,1024]{2,1,0:T(8,128)(2,1)S(1)} %pad_maximum_fusion), channel_id=1, source_target_pairs={{0,16},{16,0},{1,17},{17,1},{2,18},{18,2},{3,19},{19,3},{4,20},{20... | collective-permute-start | bytes 2359304 | tf_op jit(solution)/shard_map/gather_over_replicas/ppermute | solution.py:359
  118.3 2.7 %collective-permute-done.17.refs_4_ = bf16[6,32,1024]{2,1,0:T(8,128)(2,1)S(1)} collective-permute-done((bf16[6,32,1024]{2,1,0:T(8,128)(2,1)S(1)}, bf16[6,32,1024]{2,1,0:T(8,128)(2,1)S(1)}, u32[]{:S(2)}, u32[]{:S(2)}) %collective-permute-start.17) | collective-permute-done | bytes 393248 | tf_op jit(solution)/shard_map/gather_over_replicas/ppermute | solution.py:366
  122.1 2.3 %place_early.1.refs_7_ = bf16[48,64,1024]{2,1,0:T(8,128)(2,1)} custom-call(s32[3]{0:T(128)S(1)} %pad_add_fusion.place, bf16[12,32,1024]{2,1,0:T(8,128)(2,1)S(1)} %slice.53.refs_0_, bf16[12,32,1024]{2,1,0:T(8,128)(2,1)S(1)} %collective-permute-done.14.refs_1_, bf16[6,32,1024]{2,1,0:T(8,128)(2,1)S(1)} %collective-permute-done.12.refs_2_, ...), custom_call_target="tpu_custom_call" | custom-call | bytes 6291456 | tf_op jit(solution)/shard_map/gather_over_replicas/place_early/pallas_call | solution.py:346
  125.7 3.8 %collective-permute-done.21.refs_3_ = bf16[6,32,1024]{2,1,0:T(8,128)(2,1)S(1)} collective-permute-done((bf16[6,32,1024]{2,1,0:T(8,128)(2,1)S(1)}, bf16[6,32,1024]{2,1,0:T(8,128)(2,1)S(1)}, u32[]{:S(2)}, u32[]{:S(2)}) %collective-permute-start.21) | collective-permute-done | bytes 393248 | tf_op jit(solution)/shard_map/gather_over_replicas/ppermute | solution.py:371
  132.6 2.3 %place_late.1 = bf16[48,64,1024]{2,1,0:T(8,128)(2,1)} custom-call(s32[3]{0:T(128)S(1)} %pad_add_fusion.place, bf16[12,32,1024]{2,1,0:T(8,128)(2,1)S(1)} %collective-permute-done.15.refs_0_, bf16[6,32,1024]{2,1,0:T(8,128)(2,1)S(1)} %collective-permute-done.19.refs_1_, ...), custom_call_target="tpu_custom_call", output_to_operand_aliasing={{}: (8, {})} | custom-call | bytes 6291456 | tf_op jit(solution)/shard_map/gather_over_replicas/place_late/pallas_call | solution.py:346
  (56 shorter events, 20.6 us)
Async XLA Ops:
  1.2 5.7 %collective-permute-start = (bf16[12,32,1024]{2,1,0:T(8,128)(2,1)S(1)}, bf16[12,32,1024]{2,1,0:T(8,128)(2,1)S(1)}, u32[]{:S(2)}, u32[]{:S(2)}) collective-permute-start(bf16[12,32,1024]{2,1,0:T(8,128)(2,1)S(1)} %dynamic-slice_bitcast_fusion.7), channel_id=1, source_target_pairs={{0,16},{16,0},{1,17},{17,1},{2,18},{18,2},{3,19},{19,3},{4,20},{20... | collective-permute-start | bytes 2359304 | tf_op jit(solution)/shard_map/sum_over_replicas/ppermute | solution.py:243
  6.2 6.6 %collective-permute-start.4 = (bf16[12,32,1024]{2,1,0:T(8,128)(2,1)}, bf16[12,32,1024]{2,1,0:T(8,128)(2,1)}, u32[]{:S(2)}, u32[]{:S(2)}) collective-permute-start(bf16[12,32,1024]{2,1,0:T(8,128)(2,1)} %get-tuple-element.48), channel_id=1, source_target_pairs={{0,16},{16,0},{1,17},{17,1},{2,18},{18,2},{3,19},{19,3},{4,20},{20... | collective-permute-start | bytes 2359304 | tf_op jit(solution)/shard_map/sum_over_replicas/ppermute | solution.py:247
  6.3 8.0 %collective-permute-start.2 = (bf16[12,32,1024]{2,1,0:T(8,128)(2,1)}, bf16[12,32,1024]{2,1,0:T(8,128)(2,1)}, u32[]{:S(2)}, u32[]{:S(2)}) collective-permute-start(bf16[12,32,1024]{2,1,0:T(8,128)(2,1)} %get-tuple-element.45), channel_id=1, source_target_pairs={{0,16},{16,0},{1,17},{17,1},{2,18},{18,2},{3,19},{19,3},{4,20},{20... | collective-permute-start | bytes 2359304 | tf_op jit(solution)/shard_map/sum_over_replicas/ppermute | solution.py:247
  6.7 19.9 %collective-permute-start.1 = (bf16[12,32,1024]{2,1,0:T(8,128)(2,1)S(1)}, bf16[12,32,1024]{2,1,0:T(8,128)(2,1)}, u32[]{:S(2)}, u32[]{:S(2)}) collective-permute-start(bf16[12,32,1024]{2,1,0:T(8,128)(2,1)S(1)} %get-tuple-element.43), channel_id=1, source_target_pairs={{0,16},{16,0},{1,17},{17,1},{2,18},{18,2},{3,19},{19,3},{4,20},{20... | collective-permute-start | bytes 2359304 | tf_op jit(solution)/shard_map/sum_over_replicas/ppermute | solution.py:247
  7.1 16.0 %collective-permute-start.5 = (bf16[6,32,1024]{2,1,0:T(8,128)(2,1)S(1)}, bf16[6,32,1024]{2,1,0:T(8,128)(2,1)S(1)}, u32[]{:S(2)}, u32[]{:S(2)}) collective-permute-start(bf16[6,32,1024]{2,1,0:T(8,128)(2,1)S(1)} %get-tuple-element.49), channel_id=1, source_target_pairs={{0,96},{32,0},{64,32},{96,64},{1,97},{33,1},{65,33},{97,65},{2,98}... | collective-permute-start | bytes 1179656 | tf_op jit(solution)/shard_map/sum_over_replicas/ppermute | solution.py:260
  11.0 11.2 %collective-permute-start.8 = (bf16[6,32,1024]{2,1,0:T(8,128)(2,1)S(1)}, bf16[6,32,1024]{2,1,0:T(8,128)(2,1)S(1)}, u32[]{:S(2)}, u32[]{:S(2)}) collective-permute-start(bf16[6,32,1024]{2,1,0:T(8,128)(2,1)S(1)} %get-tuple-element.50), channel_id=1, source_target_pairs={{0,32},{32,64},{64,96},{96,0},{1,33},{33,65},{65,97},{97,1},{2,34}... | collective-permute-start | bytes 1179656 | tf_op jit(solution)/shard_map/sum_over_replicas/ppermute | solution.py:261
  15.8 14.8 %collective-permute-start.3 = (bf16[6,32,1024]{2,1,0:T(8,128)(2,1)S(1)}, bf16[6,32,1024]{2,1,0:T(8,128)(2,1)S(1)}, u32[]{:S(2)}, u32[]{:S(2)}) collective-permute-start(bf16[6,32,1024]{2,1,0:T(8,128)(2,1)S(1)} %slice.46), channel_id=1, source_target_pairs={{0,32},{32,64},{64,96},{96,0},{1,33},{33,65},{65,97},{97,1},{2,34}... | collective-permute-start | bytes 1179656 | tf_op jit(solution)/shard_map/sum_over_replicas/ppermute | solution.py:268
  15.9 16.2 %collective-permute-start.7 = (bf16[6,32,1024]{2,1,0:T(8,128)(2,1)S(1)}, bf16[6,32,1024]{2,1,0:T(8,128)(2,1)S(1)}, u32[]{:S(2)}, u32[]{:S(2)}) collective-permute-start(bf16[6,32,1024]{2,1,0:T(8,128)(2,1)S(1)} %slice.49), channel_id=1, source_target_pairs={{0,96},{32,0},{64,32},{96,64},{1,97},{33,1},{65,33},{97,65},{2,98}... | collective-permute-start | bytes 1179656 | tf_op jit(solution)/shard_map/sum_over_replicas/ppermute | solution.py:269
  23.1 16.0 %collective-permute-start.9 = (bf16[6,32,1024]{2,1,0:T(8,128)(2,1)}, bf16[6,32,1024]{2,1,0:T(8,128)(2,1)S(1)}, u32[]{:S(2)}, u32[]{:S(2)}) collective-permute-start(bf16[6,32,1024]{2,1,0:T(8,128)(2,1)} %add_convert_fusion.4), channel_id=1, source_target_pairs={{0,32},{32,64},{64,96},{96,0},{1,33},{33,65},{65,97},{97,1},{2,34}... | collective-permute-start | bytes 1179656 | tf_op jit(solution)/shard_map/sum_over_replicas/ppermute | solution.py:272
  24.0 15.1 %collective-permute-start.6 = (bf16[6,32,1024]{2,1,0:T(8,128)(2,1)}, bf16[6,32,1024]{2,1,0:T(8,128)(2,1)S(1)}, u32[]{:S(2)}, u32[]{:S(2)}) collective-permute-start(bf16[6,32,1024]{2,1,0:T(8,128)(2,1)} %add_convert_fusion.6), channel_id=1, source_target_pairs={{0,96},{32,0},{64,32},{96,64},{1,97},{33,1},{65,33},{97,65},{2,98}... | collective-permute-start | bytes 1179656 | tf_op jit(solution)/shard_map/sum_over_replicas/ppermute | solution.py:271
  61.6 5.1 %collective-permute-start.10 = (bf16[512,1024]{1,0:T(8,128)(2,1)S(1)}, bf16[512,1024]{1,0:T(8,128)(2,1)S(1)}, u32[]{:S(2)}, u32[]{:S(2)}) collective-permute-start(bf16[512,1024]{1,0:T(8,128)(2,1)S(1)} %bitcast.38), channel_id=1, source_target_pairs={{0,16},{16,0},{1,17},{17,1},{2,18},{18,2},{3,19},{19,3},{4,20},{20... | collective-permute-start | bytes 3145736 | tf_op jit(solution)/shard_map/rows_to_owner/ppermute | solution.py:289
  73.8 3.5 %collective-permute-start.11 = (bf16[3,512,512]{2,1,0:T(8,128)(2,1)S(1)}, bf16[3,512,512]{2,1,0:T(8,128)(2,1)S(1)}, u32[]{:S(2)}, u32[]{:S(2)}) collective-permute-start(bf16[3,512,512]{2,1,0:T(8,128)(2,1)S(1)} %get-tuple-element.54.root), channel_id=1, source_target_pairs={{0,16},{16,0},{1,17},{17,1},{2,18},{18,2},{3,19},{19,3},{4,20},{20... | collective-permute-start | bytes 4718600 | tf_op jit(solution)/shard_map/ppermute | solution.py:307
  99.5 14.1 %collective-permute-start.14 = (bf16[12,32,1024]{2,1,0:T(8,128)(2,1)S(1)}, bf16[12,32,1024]{2,1,0:T(8,128)(2,1)S(1)}, u32[]{:S(2)}, u32[]{:S(2)}) collective-permute-start(bf16[12,32,1024]{2,1,0:T(8,128)(2,1)S(1)} %slice.53.refs_0_), channel_id=1, source_target_pairs={{0,16},{16,0},{1,17},{17,1},{2,18},{18,2},{3,19},{19,3},{4,20},{20... | collective-permute-start | bytes 2359304 | tf_op jit(solution)/shard_map/gather_over_replicas/ppermute | solution.py:359
  101.4 12.2 %collective-permute-start.13 = (bf16[6,32,1024]{2,1,0:T(8,128)(2,1)S(1)}, bf16[6,32,1024]{2,1,0:T(8,128)(2,1)S(1)}, u32[]{:S(2)}, u32[]{:S(2)}) collective-permute-start(bf16[6,32,1024]{2,1,0:T(8,128)(2,1)S(1)} %get-tuple-element.60), channel_id=1, source_target_pairs={{0,32},{32,64},{64,96},{96,0},{1,33},{33,65},{65,97},{97,1},{2,34}... | collective-permute-start | bytes 1179656 | tf_op jit(solution)/shard_map/gather_over_replicas/ppermute | solution.py:363
  101.7 11.9 %collective-permute-start.12 = (bf16[6,32,1024]{2,1,0:T(8,128)(2,1)S(1)}, bf16[6,32,1024]{2,1,0:T(8,128)(2,1)S(1)}, u32[]{:S(2)}, u32[]{:S(2)}) collective-permute-start(bf16[6,32,1024]{2,1,0:T(8,128)(2,1)S(1)} %get-tuple-element.61), channel_id=1, source_target_pairs={{0,96},{32,0},{64,32},{96,64},{1,97},{33,1},{65,33},{97,65},{2,98}... | collective-permute-start | bytes 1179656 | tf_op jit(solution)/shard_map/gather_over_replicas/ppermute | solution.py:362
  105.8 15.2 %collective-permute-start.17 = (bf16[6,32,1024]{2,1,0:T(8,128)(2,1)S(1)}, bf16[6,32,1024]{2,1,0:T(8,128)(2,1)S(1)}, u32[]{:S(2)}, u32[]{:S(2)}) collective-permute-start(bf16[6,32,1024]{2,1,0:T(8,128)(2,1)S(1)} %get-tuple-element.60), channel_id=1, source_target_pairs={{0,96},{32,0},{64,32},{96,64},{1,97},{33,1},{65,33},{97,65},{2,98}... | collective-permute-start | bytes 1179656 | tf_op jit(solution)/shard_map/gather_over_replicas/ppermute | solution.py:366
  105.8 16.3 %collective-permute-start.18 = (bf16[6,32,1024]{2,1,0:T(8,128)(2,1)S(1)}, bf16[6,32,1024]{2,1,0:T(8,128)(2,1)S(1)}, u32[]{:S(2)}, u32[]{:S(2)}) collective-permute-start(bf16[6,32,1024]{2,1,0:T(8,128)(2,1)S(1)} %get-tuple-element.61), channel_id=1, source_target_pairs={{0,32},{32,64},{64,96},{96,0},{1,33},{33,65},{65,97},{97,1},{2,34}... | collective-permute-start | bytes 1179656 | tf_op jit(solution)/shard_map/gather_over_replicas/ppermute | solution.py:367
  113.6 15.8 %collective-permute-start.21 = (bf16[6,32,1024]{2,1,0:T(8,128)(2,1)S(1)}, bf16[6,32,1024]{2,1,0:T(8,128)(2,1)S(1)}, u32[]{:S(2)}, u32[]{:S(2)}) collective-permute-start(bf16[6,32,1024]{2,1,0:T(8,128)(2,1)S(1)} %collective-permute-done.12.refs_2_), channel_id=1, source_target_pairs={{0,96},{32,0},{64,32},{96,64},{1,97},{33,1},{65,33},{97,65},{2,98}... | collective-permute-start | bytes 1179656 | tf_op jit(solution)/shard_map/gather_over_replicas/ppermute | solution.py:371
  116.0 14.6 %collective-permute-start.22 = (bf16[6,32,1024]{2,1,0:T(8,128)(2,1)S(1)}, bf16[6,32,1024]{2,1,0:T(8,128)(2,1)S(1)}, u32[]{:S(2)}, u32[]{:S(2)}) collective-permute-start(bf16[6,32,1024]{2,1,0:T(8,128)(2,1)S(1)} %collective-permute-done.13.refs_3_), channel_id=1, source_target_pairs={{0,32},{32,64},{64,96},{96,0},{1,33},{33,65},{65,97},{97,1},{2,34}... | collective-permute-start | bytes 1179656 | tf_op jit(solution)/shard_map/gather_over_replicas/ppermute | solution.py:372
  116.1 16.6 %collective-permute-start.15 = (bf16[12,32,1024]{2,1,0:T(8,128)(2,1)S(1)}, bf16[12,32,1024]{2,1,0:T(8,128)(2,1)S(1)}, u32[]{:S(2)}, u32[]{:S(2)}) collective-permute-start(bf16[12,32,1024]{2,1,0:T(8,128)(2,1)S(1)} %pad_maximum_fusion), channel_id=1, source_target_pairs={{0,16},{16,0},{1,17},{17,1},{2,18},{18,2},{3,19},{19,3},{4,20},{20... | collective-permute-start | bytes 2359304 | tf_op jit(solution)/shard_map/gather_over_replicas/ppermute | solution.py:359
  124.3 7.0 %collective-permute-start.19 = (bf16[6,32,1024]{2,1,0:T(8,128)(2,1)S(1)}, bf16[6,32,1024]{2,1,0:T(8,128)(2,1)S(1)}, u32[]{:S(2)}, u32[]{:S(2)}) collective-permute-start(bf16[6,32,1024]{2,1,0:T(8,128)(2,1)S(1)} %collective-permute-done.17.refs_4_), channel_id=1, source_target_pairs={{0,16},{16,0},{1,17},{17,1},{2,18},{18,2},{3,19},{19,3},{4,20},{20... | collective-permute-start | bytes 1179656 | tf_op jit(solution)/shard_map/gather_over_replicas/ppermute | solution.py:359
  125.6 5.7 %collective-permute-start.20 = (bf16[6,32,1024]{2,1,0:T(8,128)(2,1)S(1)}, bf16[6,32,1024]{2,1,0:T(8,128)(2,1)S(1)}, u32[]{:S(2)}, u32[]{:S(2)}) collective-permute-start(bf16[6,32,1024]{2,1,0:T(8,128)(2,1)S(1)} %collective-permute-done.18.refs_5_), channel_id=1, source_target_pairs={{0,16},{16,0},{1,17},{17,1},{2,18},{18,2},{3,19},{19,3},{4,20},{20... | collective-permute-start | bytes 1179656 | tf_op jit(solution)/shard_map/gather_over_replicas/ppermute | solution.py:359
  129.4 2.5 %collective-permute-start.23 = (bf16[6,32,1024]{2,1,0:T(8,128)(2,1)S(1)}, bf16[6,32,1024]{2,1,0:T(8,128)(2,1)S(1)}, u32[]{:S(2)}, u32[]{:S(2)}) collective-permute-start(bf16[6,32,1024]{2,1,0:T(8,128)(2,1)S(1)} %collective-permute-done.21.refs_3_), channel_id=1, source_target_pairs={{0,16},{16,0},{1,17},{17,1},{2,18},{18,2},{3,19},{19,3},{4,20},{20... | collective-permute-start | bytes 1179656 | tf_op jit(solution)/shard_map/gather_over_replicas/ppermute | solution.py:359
  130.6 2.1 %collective-permute-start.24 = (bf16[6,32,1024]{2,1,0:T(8,128)(2,1)S(1)}, bf16[6,32,1024]{2,1,0:T(8,128)(2,1)S(1)}, u32[]{:S(2)}, u32[]{:S(2)}) collective-permute-start(bf16[6,32,1024]{2,1,0:T(8,128)(2,1)S(1)} %collective-permute-done.22.refs_4_), channel_id=1, source_target_pairs={{0,16},{16,0},{1,17},{17,1},{2,18},{18,2},{3,19},{19,3},{4,20},{20... | collective-permute-start | bytes 1179656 | tf_op jit(solution)/shard_map/gather_over_replicas/ppermute | solution.py:359
  (2 other events, 8.9 us)

commit v6 on v5

--- a/solution.py
+++ b/solution.py
@@ -10,6 +10,7 @@
 damping = 0.1
 mib = 2**20
 TILE = 256
+FETCH_VMEM = 47 * mib
 ROWS = ((0,), (0,))
 COLUMNS = ((1,), (1,))
 
@@ -20,6 +21,25 @@
 
 def rows_at(start, count):
     return pl.ds(pl.multiple_of(start, count), count)
+
+
+def fetch_kernel(wanted, place, source, *refs):
+    *outs, sems = refs
+    core, plane = place[0], place[1]
+    copies = []
+    for index, (out, (shift, mine)) in enumerate(zip(outs, wanted)):
+        count, rows, _ = out.shape
+        half = core if mine else 1 - core
+        first = lax.rem(plane + shift, 4) * count
+        copies.append(
+            pltpu.make_async_copy(
+                source.at[0, pl.ds(first, count), rows_at(half * rows, rows), :], out, sems.at[index]
+            )
+        )
+    for copy in copies:
+        copy.start()
+    for copy in copies:
+        copy.wait()
 
 
 def add_kernel(one, two, *outs):
@@ -241,9 +261,19 @@
     with jax.named_scope("sum_over_replicas"):
         sent, next_plane = lax.optimization_barrier((rows_of(plane, 2, 1 - core), plane))
         got = lax.ppermute(sent, "core", swap)
-        kept, *sent = lax.optimization_barrier(
-            [rows_of(next_plane, 2, core)] + [rows_of(next_plane, k, 1 - core) for k in (1, 3, 0)]
-        )
+        plane_rows = jax.ShapeDtypeStruct((per_plane, rows, width), jnp.bfloat16)
+        kept, *sent = pl.pallas_call(
+            functools.partial(fetch_kernel, ((2, True), (1, False), (3, False), (0, False))),
+            out_shape=[plane_rows] * 4,
+            in_specs=[smem, anywhere],
+            out_specs=[vmem] * 4,
+            scratch_shapes=[pltpu.SemaphoreType.DMA((4,))],
+            compiler_params=pltpu.CompilerParams(vmem_limit_bytes=FETCH_VMEM),
+            cost_estimate=pl.CostEstimate(
+                flops=0, bytes_accessed=16 * plane_rows.size, transcendentals=0
+            ),
+            name="fetch_rows",
+        )(jnp.stack([core, next_plane]).astype(jnp.int32), partials)
         got_above, got_below, got_mine = (lax.ppermute(each, "core", swap) for each in sent)
         far_low, far_high = pl.pallas_call(
             add_kernel,

time: 136 us -> 137 us (level)
  Pallas kernels: 18 us -> 21.3 us
  local copies, waits for them, and re-layouts: 6.75 us -> 4.87 us
    pallas_call x0 -> x1, Pallas kernels: none -> 3.31 us  [local(): pl.pallas_call(functools.partial(fetch_kernel, ((2, True), (1, False), (3...]
    reshape x3 -> x2, local copies, waits for them, and re-layouts: 6.49 us -> 3.87 us  [rows_of(): return sliced.reshape(per_plane, rows, width)]
  transfers between devices with their start and end apart: 25 -> 25, of which waited for: 12 -> 12; matrix products, arithmetic and copies ran while one was open for 9% -> 7% of each run, Pallas kernels for 4% -> 6%
where the time goes in v6:
time: 137 us
  blocking collectives  41 us (30%)
  waiting for transfers between devices  31.4 us (23%)
  starting transfers between devices  29.2 us (21%)
  Pallas kernels  21.3 us (16%)
  other arithmetic  7.85 us (6%)
  local copies, waits for them, and re-layouts  4.87 us (4%)
    all_to_all x1, blocking collectives, local(): lax.all_to_all(summed, ('y', 'x'), 0, 0, tiled=True).reshape(half, width)  22 us
    all_to_all x1, blocking collectives, local(): lax.all_to_all(finished.reshape(shards, rows, width), ('y', 'x'), 0, 0, t...  19.1 us
    ppermute x7, starting transfers between devices, other_core(): return lax.ppermute(piece, 'core', swap)  7.74 us
    pallas_call x1, Pallas kernels, local(): pl.pallas_call(root_kernel, out_shape=[jax.ShapeDtypeStruct((3, half, hal...  7.13 us
    ppermute x1, waiting for transfers between devices, local(): high_below = lax.ppermute(plus(to_above[part:], from_below), 'z', up)  6.93 us
    convert_element_type x6, other arithmetic, plus(): return total.astype(jnp.bfloat16)  6.77 us
    ppermute x1, waiting for transfers between devices, local(): below_high = lax.ppermute(back[part:], 'z', up)  6.39 us
    pallas_call x2, Pallas kernels, put(): pl.pallas_call(functools.partial(place_kernel, targets), out_shape=out_sh...  4.52 us
  transfers between devices with their start and end apart: 25, of which 12 were waited for; matrix products, arithmetic and copies ran while one was open for 7% of the time, Pallas kernels for 6%

profile of v6, /device:TPU:1, one launch (start us, length us, event | category | flops | bytes accessed | tf_op | source)
XLA Modules:
  0.0 136.7 jit_solution(12917600459915968942)
XLA Ops:
  0.0 2.1 %dynamic-slice_bitcast_fusion.3 = bf16[12,32,1024]{2,1,0:T(8,128)(2,1)} fusion(bf16[4,12,2,32,1024]{4,3,2,1,0:T(8,128)(2,1)} %bitcast.27, s32[]{:T(128)S(6)} %select_n.40, s32[]{:T(128)S(6)} %select_n.41), kind=kLoop, calls=%fused_computation.12 | loop fusion | bytes 1572872 | tf_op jit(solution)/shard_map/sum_over_replicas/reshape | solution.py:259
  3.6 3.3 %fetch_rows.1 = (bf16[12,32,1024]{2,1,0:T(8,128)(2,1)S(1)}, bf16[12,32,1024]{2,1,0:T(8,128)(2,1)S(1)}, bf16[12,32,1024]{2,1,0:T(8,128)(2,1)}, bf16[12,32,1024]{2,1,0:T(8,128)(2,1)S(1)}) custom-call(s32[2]{0:T(128)S(1)} %pad_add_fusion.place, bf16[1,48,64,1024]{3,2,1,0:T(8,128)(2,1)} %source.1), custom_call_target="tpu_custom_call" | custom-call | bytes 6291456 | tf_op jit(solution)/shard_map/sum_over_replicas/fetch_rows/pallas_call | solution.py:265
  8.6 3.8 %collective-permute-start.5 = (bf16[6,32,1024]{2,1,0:T(8,128)(2,1)S(1)}, bf16[6,32,1024]{2,1,0:T(8,128)(2,1)S(1)}, u32[]{:S(2)}, u32[]{:S(2)}) collective-permute-start(bf16[6,32,1024]{2,1,0:T(8,128)(2,1)S(1)} %get-tuple-element.49), channel_id=1, source_target_pairs={{0,96},{32,0},{64,32},{96,64},{1,97},{33,1},{65,33},{97,65},{2,98}... | collective-permute-start | bytes 1179656 | tf_op jit(solution)/shard_map/sum_over_replicas/ppermute | solution.py:290
  17.3 2.7 %collective-permute-start.7 = (bf16[6,32,1024]{2,1,0:T(8,128)(2,1)S(1)}, bf16[6,32,1024]{2,1,0:T(8,128)(2,1)S(1)}, u32[]{:S(2)}, u32[]{:S(2)}) collective-permute-start(bf16[6,32,1024]{2,1,0:T(8,128)(2,1)S(1)} %slice.49), channel_id=1, source_target_pairs={{0,96},{32,0},{64,32},{96,64},{1,97},{33,1},{65,33},{97,65},{2,98}... | collective-permute-start | bytes 1179656 | tf_op jit(solution)/shard_map/sum_over_replicas/ppermute | solution.py:299
  20.1 3.9 %collective-permute-done.8 = bf16[6,32,1024]{2,1,0:T(8,128)(2,1)} collective-permute-done((bf16[6,32,1024]{2,1,0:T(8,128)(2,1)}, bf16[6,32,1024]{2,1,0:T(8,128)(2,1)}, u32[]{:S(2)}, u32[]{:S(2)}) %collective-permute-start.8) | collective-permute-done | bytes 393248 | tf_op jit(solution)/shard_map/sum_over_replicas/ppermute | solution.py:291
  23.9 1.9 %add_convert_fusion.4 = bf16[6,32,1024]{2,1,0:T(8,128)(2,1)} fusion(bf16[6,32,1024]{2,1,0:T(8,128)(2,1)} %collective-permute-done.8, bf16[12,32,1024]{2,1,0:T(8,128)(2,1)S(1)} %add_convert_fusion.1), kind=kLoop, calls=%fused_computation.6 | loop fusion | flops 786432 | bytes 1179648 | tf_op jit(solution)/shard_map/sum_over_replicas/convert_element_type | solution.py:248
  25.9 2.7 %collective-permute-start.6 = (bf16[6,32,1024]{2,1,0:T(8,128)(2,1)S(1)}, bf16[6,32,1024]{2,1,0:T(8,128)(2,1)S(1)}, u32[]{:S(2)}, u32[]{:S(2)}) collective-permute-start(bf16[6,32,1024]{2,1,0:T(8,128)(2,1)S(1)} %add_convert_fusion.6), channel_id=1, source_target_pairs={{0,96},{32,0},{64,32},{96,64},{1,97},{33,1},{65,33},{97,65},{2,98}... | collective-permute-start | bytes 1179656 | tf_op jit(solution)/shard_map/sum_over_replicas/ppermute | solution.py:301
  30.1 2.1 %collective-permute-done.3 = bf16[6,32,1024]{2,1,0:T(8,128)(2,1)S(1)} collective-permute-done((bf16[6,32,1024]{2,1,0:T(8,128)(2,1)S(1)}, bf16[6,32,1024]{2,1,0:T(8,128)(2,1)S(1)}, u32[]{:S(2)}, u32[]{:S(2)}) %collective-permute-start.3) | collective-permute-done | bytes 393248 | tf_op jit(solution)/shard_map/sum_over_replicas/ppermute | solution.py:298
  33.7 6.9 %collective-permute-done.9 = bf16[6,32,1024]{2,1,0:T(8,128)(2,1)S(1)} collective-permute-done((bf16[6,32,1024]{2,1,0:T(8,128)(2,1)}, bf16[6,32,1024]{2,1,0:T(8,128)(2,1)S(1)}, u32[]{:S(2)}, u32[]{:S(2)}) %collective-permute-start.9) | collective-permute-done | bytes 393248 | tf_op jit(solution)/shard_map/sum_over_replicas/ppermute | solution.py:302
  41.3 22.0 %all_to_all.10 = bf16[16,32,1024]{2,1,0:T(8,128)(2,1)S(1)} all-to-all(bf16[16,32,1024]{2,1,0:T(8,128)(2,1)S(1)} %maximum_maximum_fusion), channel_id=1, replica_groups=mesh['z'=4,'core'=2,'y'=4,'x'=4] {'y','x'}, dimensions={0} | all-to-all | bytes 2097152 | tf_op jit(solution)/shard_map/rows_to_owner/all_to_all | solution.py:318
  63.2 2.8 %collective-permute-start.10 = (bf16[512,1024]{1,0:T(8,128)(2,1)S(1)}, bf16[512,1024]{1,0:T(8,128)(2,1)S(1)}, u32[]{:S(2)}, u32[]{:S(2)}) collective-permute-start(bf16[512,1024]{1,0:T(8,128)(2,1)S(1)} %bitcast.23), channel_id=1, source_target_pairs={{0,16},{16,0},{1,17},{17,1},{2,18},{18,2},{3,19},{19,3},{4,20},{20... | collective-permute-start | bytes 3145736 | tf_op jit(solution)/shard_map/rows_to_owner/ppermute | solution.py:319
  66.0 2.3 %collective-permute-done.10.sibling = bf16[512,1024]{1,0:T(8,128)(2,1)S(1)} collective-permute-done((bf16[512,1024]{1,0:T(8,128)(2,1)S(1)}, bf16[512,1024]{1,0:T(8,128)(2,1)S(1)}, u32[]{:S(2)}, u32[]{:S(2)}) %collective-permute-start.10) | collective-permute-done | bytes 1048608 | tf_op jit(solution)/shard_map/rows_to_owner/ppermute | solution.py:319
  68.3 7.1 %inverse_root.1 = (bf16[3,512,512]{2,1,0:T(8,128)(2,1)S(1)}, bf16[1024,1024]{1,0:T(8,128)(2,1)S(1)}) custom-call(s32[3]{0:T(128)S(1)} %pad_add_fusion.1.place, bf16[512,1024]{1,0:T(8,128)(2,1)S(1)} %bitcast.24, bf16[512,1024]{1,0:T(8,128)(2,1)S(1)} %collective-permute-done.10.sibling), custom_call_target="tpu_custom_call" | custom-call | flops 6442450944 | bytes 6291456 | tf_op jit(solution)/shard_map/inverse_root/pallas_call | solution.py:324
  75.8 3.0 %apply_own_root.1 = (bf16[1024,1024]{1,0:T(8,128)(2,1)S(1)}, f32[1,1024]{1,0:T(1,128)S(1)}) custom-call(s32[3]{0:T(128)S(1)} %pad_add_fusion.1.place, bf16[3,512,512]{2,1,0:T(8,128)(2,1)S(1)} %get-tuple-element.54.root, bf16[1024,1024]{1,0:T(8,128)(2,1)S(1)} %get-tuple-element.55.grad), custom_call_target="tpu_custom_call" | custom-call | flops 2147483648 | bytes 6291456 | tf_op jit(solution)/shard_map/apply_own_root/pallas_call | solution.py:338
  78.9 3.2 %apply_other_root.1 = bf16[512,1024]{1,0:T(8,128)(2,1)S(1)} custom-call(s32[3]{0:T(128)S(1)} %pad_add_fusion.1.place, bf16[512,1024]{1,0:T(8,128)(2,1)S(1)} %bitcast.25, bf16[1024,1024]{1,0:T(8,128)(2,1)S(1)} %get-tuple-element.56.side, bf16[3,512,512]{2,1,0:T(8,128)(2,1)S(1)} %collective-permute-done.11.root, f32[1,1024]{1,0:T(1,128)S(1)} %get-tuple-element.57.grad_sum), custom_call_target="tpu_custom_call" | custom-call | flops 2147483648 | bytes 6291456 | tf_op jit(solution)/shard_map/apply_other_root/pallas_call | solution.py:347
  82.1 19.1 %all_to_all.11 = bf16[16,32,1024]{2,1,0:T(8,128)(2,1)S(1)} all-to-all(bf16[16,32,1024]{2,1,0:T(8,128)(2,1)S(1)} %bitcast.26), channel_id=1, replica_groups=mesh['z'=4,'core'=2,'y'=4,'x'=4] {'y','x'}, dimensions={0} | all-to-all | bytes 2097152 | tf_op jit(solution)/shard_map/rows_to_shards/all_to_all | solution.py:359
  103.3 2.7 %collective-permute-start.12 = (bf16[6,32,1024]{2,1,0:T(8,128)(2,1)S(1)}, bf16[6,32,1024]{2,1,0:T(8,128)(2,1)S(1)}, u32[]{:S(2)}, u32[]{:S(2)}) collective-permute-start(bf16[6,32,1024]{2,1,0:T(8,128)(2,1)S(1)} %get-tuple-element.61), channel_id=1, source_target_pairs={{0,96},{32,0},{64,32},{96,64},{1,97},{33,1},{65,33},{97,65},{2,98}... | collective-permute-start | bytes 1179656 | tf_op jit(solution)/shard_map/gather_over_replicas/ppermute | solution.py:392
  108.9 6.4 %collective-permute-done.13.refs_3_ = bf16[6,32,1024]{2,1,0:T(8,128)(2,1)S(1)} collective-permute-done((bf16[6,32,1024]{2,1,0:T(8,128)(2,1)S(1)}, bf16[6,32,1024]{2,1,0:T(8,128)(2,1)S(1)}, u32[]{:S(2)}, u32[]{:S(2)}) %collective-permute-start.13) | collective-permute-done | bytes 393248 | tf_op jit(solution)/shard_map/gather_over_replicas/ppermute | solution.py:393
  115.3 2.4 %collective-permute-start.21 = (bf16[6,32,1024]{2,1,0:T(8,128)(2,1)S(1)}, bf16[6,32,1024]{2,1,0:T(8,128)(2,1)S(1)}, u32[]{:S(2)}, u32[]{:S(2)}) collective-permute-start(bf16[6,32,1024]{2,1,0:T(8,128)(2,1)S(1)} %collective-permute-done.12.refs_2_), channel_id=1, source_target_pairs={{0,96},{32,0},{64,32},{96,64},{1,97},{33,1},{65,33},{97,65},{2,98}... | collective-permute-start | bytes 1179656 | tf_op jit(solution)/shard_map/gather_over_replicas/ppermute | solution.py:401
  117.7 2.2 %collective-permute-start.15 = (bf16[12,32,1024]{2,1,0:T(8,128)(2,1)S(1)}, bf16[12,32,1024]{2,1,0:T(8,128)(2,1)S(1)}, u32[]{:S(2)}, u32[]{:S(2)}) collective-permute-start(bf16[12,32,1024]{2,1,0:T(8,128)(2,1)S(1)} %pad_maximum_fusion), channel_id=1, source_target_pairs={{0,16},{16,0},{1,17},{17,1},{2,18},{18,2},{3,19},{19,3},{4,20},{20... | collective-permute-start | bytes 2359304 | tf_op jit(solution)/shard_map/gather_over_replicas/ppermute | solution.py:389
  119.9 2.7 %collective-permute-done.17.refs_4_ = bf16[6,32,1024]{2,1,0:T(8,128)(2,1)S(1)} collective-permute-done((bf16[6,32,1024]{2,1,0:T(8,128)(2,1)S(1)}, bf16[6,32,1024]{2,1,0:T(8,128)(2,1)S(1)}, u32[]{:S(2)}, u32[]{:S(2)}) %collective-permute-start.17) | collective-permute-done | bytes 393248 | tf_op jit(solution)/shard_map/gather_over_replicas/ppermute | solution.py:396
  123.7 2.3 %place_early.1.refs_7_ = bf16[48,64,1024]{2,1,0:T(8,128)(2,1)} custom-call(s32[3]{0:T(128)S(1)} %pad_add_fusion.1.place, bf16[12,32,1024]{2,1,0:T(8,128)(2,1)S(1)} %slice.53.refs_0_, bf16[12,32,1024]{2,1,0:T(8,128)(2,1)S(1)} %collective-permute-done.14.refs_1_, bf16[6,32,1024]{2,1,0:T(8,128)(2,1)S(1)} %collective-permute-done.12.refs_2_, ...), custom_call_target="tpu_custom_call" | custom-call | bytes 6291456 | tf_op jit(solution)/shard_map/gather_over_replicas/place_early/pallas_call | solution.py:376
  127.3 3.7 %collective-permute-done.21.refs_3_ = bf16[6,32,1024]{2,1,0:T(8,128)(2,1)S(1)} collective-permute-done((bf16[6,32,1024]{2,1,0:T(8,128)(2,1)S(1)}, bf16[6,32,1024]{2,1,0:T(8,128)(2,1)S(1)}, u32[]{:S(2)}, u32[]{:S(2)}) %collective-permute-start.21) | collective-permute-done | bytes 393248 | tf_op jit(solution)/shard_map/gather_over_replicas/ppermute | solution.py:401
  134.3 2.3 %place_late.1 = bf16[48,64,1024]{2,1,0:T(8,128)(2,1)} custom-call(s32[3]{0:T(128)S(1)} %pad_add_fusion.1.place, bf16[12,32,1024]{2,1,0:T(8,128)(2,1)S(1)} %collective-permute-done.15.refs_0_, bf16[6,32,1024]{2,1,0:T(8,128)(2,1)S(1)} %collective-permute-done.19.refs_1_, ...), custom_call_target="tpu_custom_call", output_to_operand_aliasing={{}: (8, {})} | custom-call | bytes 6291456 | tf_op jit(solution)/shard_map/gather_over_replicas/place_late/pallas_call | solution.py:376
  (59 shorter events, 22.2 us)
Async XLA Ops:
  2.1 5.6 %collective-permute-start = (bf16[12,32,1024]{2,1,0:T(8,128)(2,1)}, bf16[12,32,1024]{2,1,0:T(8,128)(2,1)S(1)}, u32[]{:S(2)}, u32[]{:S(2)}) collective-permute-start(bf16[12,32,1024]{2,1,0:T(8,128)(2,1)} %dynamic-slice_bitcast_fusion.3), channel_id=1, source_target_pairs={{0,16},{16,0},{1,17},{17,1},{2,18},{18,2},{3,19},{19,3},{4,20},{20... | collective-permute-start | bytes 2359304 | tf_op jit(solution)/shard_map/sum_over_replicas/ppermute | solution.py:263
  6.9 7.4 %collective-permute-start.4 = (bf16[12,32,1024]{2,1,0:T(8,128)(2,1)}, bf16[12,32,1024]{2,1,0:T(8,128)(2,1)}, u32[]{:S(2)}, u32[]{:S(2)}) collective-permute-start(bf16[12,32,1024]{2,1,0:T(8,128)(2,1)} %get-tuple-element.48), channel_id=1, source_target_pairs={{0,16},{16,0},{1,17},{17,1},{2,18},{18,2},{3,19},{19,3},{4,20},{20... | collective-permute-start | bytes 2359304 | tf_op jit(solution)/shard_map/sum_over_replicas/ppermute | solution.py:277
  7.0 8.7 %collective-permute-start.2 = (bf16[12,32,1024]{2,1,0:T(8,128)(2,1)S(1)}, bf16[12,32,1024]{2,1,0:T(8,128)(2,1)}, u32[]{:S(2)}, u32[]{:S(2)}) collective-permute-start(bf16[12,32,1024]{2,1,0:T(8,128)(2,1)S(1)} %get-tuple-element.45), channel_id=1, source_target_pairs={{0,16},{16,0},{1,17},{17,1},{2,18},{18,2},{3,19},{19,3},{4,20},{20... | collective-permute-start | bytes 2359304 | tf_op jit(solution)/shard_map/sum_over_replicas/ppermute | solution.py:277
  7.5 21.2 %collective-permute-start.1 = (bf16[12,32,1024]{2,1,0:T(8,128)(2,1)S(1)}, bf16[12,32,1024]{2,1,0:T(8,128)(2,1)}, u32[]{:S(2)}, u32[]{:S(2)}) collective-permute-start(bf16[12,32,1024]{2,1,0:T(8,128)(2,1)S(1)} %get-tuple-element.43), channel_id=1, source_target_pairs={{0,16},{16,0},{1,17},{17,1},{2,18},{18,2},{3,19},{19,3},{4,20},{20... | collective-permute-start | bytes 2359304 | tf_op jit(solution)/shard_map/sum_over_replicas/ppermute | solution.py:277
  8.6 17.2 %collective-permute-start.5 = (bf16[6,32,1024]{2,1,0:T(8,128)(2,1)S(1)}, bf16[6,32,1024]{2,1,0:T(8,128)(2,1)S(1)}, u32[]{:S(2)}, u32[]{:S(2)}) collective-permute-start(bf16[6,32,1024]{2,1,0:T(8,128)(2,1)S(1)} %get-tuple-element.49), channel_id=1, source_target_pairs={{0,96},{32,0},{64,32},{96,64},{1,97},{33,1},{65,33},{97,65},{2,98}... | collective-permute-start | bytes 1179656 | tf_op jit(solution)/shard_map/sum_over_replicas/ppermute | solution.py:290
  12.4 11.5 %collective-permute-start.8 = (bf16[6,32,1024]{2,1,0:T(8,128)(2,1)}, bf16[6,32,1024]{2,1,0:T(8,128)(2,1)}, u32[]{:S(2)}, u32[]{:S(2)}) collective-permute-start(bf16[6,32,1024]{2,1,0:T(8,128)(2,1)} %copy-done), channel_id=1, source_target_pairs={{0,32},{32,64},{64,96},{96,0},{1,33},{33,65},{65,97},{97,1},{2,34}... | collective-permute-start | bytes 1179656 | tf_op jit(solution)/shard_map/sum_over_replicas/ppermute | solution.py:291
  17.2 15.0 %collective-permute-start.3 = (bf16[6,32,1024]{2,1,0:T(8,128)(2,1)S(1)}, bf16[6,32,1024]{2,1,0:T(8,128)(2,1)S(1)}, u32[]{:S(2)}, u32[]{:S(2)}) collective-permute-start(bf16[6,32,1024]{2,1,0:T(8,128)(2,1)S(1)} %slice.46), channel_id=1, source_target_pairs={{0,32},{32,64},{64,96},{96,0},{1,33},{33,65},{65,97},{97,1},{2,34}... | collective-permute-start | bytes 1179656 | tf_op jit(solution)/shard_map/sum_over_replicas/ppermute | solution.py:298
  17.3 16.4 %collective-permute-start.7 = (bf16[6,32,1024]{2,1,0:T(8,128)(2,1)S(1)}, bf16[6,32,1024]{2,1,0:T(8,128)(2,1)S(1)}, u32[]{:S(2)}, u32[]{:S(2)}) collective-permute-start(bf16[6,32,1024]{2,1,0:T(8,128)(2,1)S(1)} %slice.49), channel_id=1, source_target_pairs={{0,96},{32,0},{64,32},{96,64},{1,97},{33,1},{65,33},{97,65},{2,98}... | collective-permute-start | bytes 1179656 | tf_op jit(solution)/shard_map/sum_over_replicas/ppermute | solution.py:299
  25.8 14.9 %collective-permute-start.9 = (bf16[6,32,1024]{2,1,0:T(8,128)(2,1)}, bf16[6,32,1024]{2,1,0:T(8,128)(2,1)S(1)}, u32[]{:S(2)}, u32[]{:S(2)}) collective-permute-start(bf16[6,32,1024]{2,1,0:T(8,128)(2,1)} %add_convert_fusion.4), channel_id=1, source_target_pairs={{0,32},{32,64},{64,96},{96,0},{1,33},{33,65},{65,97},{97,1},{2,34}... | collective-permute-start | bytes 1179656 | tf_op jit(solution)/shard_map/sum_over_replicas/ppermute | solution.py:302
  25.9 14.7 %collective-permute-start.6 = (bf16[6,32,1024]{2,1,0:T(8,128)(2,1)S(1)}, bf16[6,32,1024]{2,1,0:T(8,128)(2,1)S(1)}, u32[]{:S(2)}, u32[]{:S(2)}) collective-permute-start(bf16[6,32,1024]{2,1,0:T(8,128)(2,1)S(1)} %add_convert_fusion.6), channel_id=1, source_target_pairs={{0,96},{32,0},{64,32},{96,64},{1,97},{33,1},{65,33},{97,65},{2,98}... | collective-permute-start | bytes 1179656 | tf_op jit(solution)/shard_map/sum_over_replicas/ppermute | solution.py:301
  63.2 5.1 %collective-permute-start.10 = (bf16[512,1024]{1,0:T(8,128)(2,1)S(1)}, bf16[512,1024]{1,0:T(8,128)(2,1)S(1)}, u32[]{:S(2)}, u32[]{:S(2)}) collective-permute-start(bf16[512,1024]{1,0:T(8,128)(2,1)S(1)} %bitcast.23), channel_id=1, source_target_pairs={{0,16},{16,0},{1,17},{17,1},{2,18},{18,2},{3,19},{19,3},{4,20},{20... | collective-permute-start | bytes 3145736 | tf_op jit(solution)/shard_map/rows_to_owner/ppermute | solution.py:319
  75.4 3.5 %collective-permute-start.11 = (bf16[3,512,512]{2,1,0:T(8,128)(2,1)S(1)}, bf16[3,512,512]{2,1,0:T(8,128)(2,1)S(1)}, u32[]{:S(2)}, u32[]{:S(2)}) collective-permute-start(bf16[3,512,512]{2,1,0:T(8,128)(2,1)S(1)} %get-tuple-element.54.root), channel_id=1, source_target_pairs={{0,16},{16,0},{1,17},{17,1},{2,18},{18,2},{3,19},{19,3},{4,20},{20... | collective-permute-start | bytes 4718600 | tf_op jit(solution)/shard_map/ppermute | solution.py:337
  101.2 14.0 %collective-permute-start.14 = (bf16[12,32,1024]{2,1,0:T(8,128)(2,1)S(1)}, bf16[12,32,1024]{2,1,0:T(8,128)(2,1)S(1)}, u32[]{:S(2)}, u32[]{:S(2)}) collective-permute-start(bf16[12,32,1024]{2,1,0:T(8,128)(2,1)S(1)} %slice.53.refs_0_), channel_id=1, source_target_pairs={{0,16},{16,0},{1,17},{17,1},{2,18},{18,2},{3,19},{19,3},{4,20},{20... | collective-permute-start | bytes 2359304 | tf_op jit(solution)/shard_map/gather_over_replicas/ppermute | solution.py:389
  103.0 12.2 %collective-permute-start.13 = (bf16[6,32,1024]{2,1,0:T(8,128)(2,1)S(1)}, bf16[6,32,1024]{2,1,0:T(8,128)(2,1)S(1)}, u32[]{:S(2)}, u32[]{:S(2)}) collective-permute-start(bf16[6,32,1024]{2,1,0:T(8,128)(2,1)S(1)} %get-tuple-element.60), channel_id=1, source_target_pairs={{0,32},{32,64},{64,96},{96,0},{1,33},{33,65},{65,97},{97,1},{2,34}... | collective-permute-start | bytes 1179656 | tf_op jit(solution)/shard_map/gather_over_replicas/ppermute | solution.py:393
  103.3 11.9 %collective-permute-start.12 = (bf16[6,32,1024]{2,1,0:T(8,128)(2,1)S(1)}, bf16[6,32,1024]{2,1,0:T(8,128)(2,1)S(1)}, u32[]{:S(2)}, u32[]{:S(2)}) collective-permute-start(bf16[6,32,1024]{2,1,0:T(8,128)(2,1)S(1)} %get-tuple-element.61), channel_id=1, source_target_pairs={{0,96},{32,0},{64,32},{96,64},{1,97},{33,1},{65,33},{97,65},{2,98}... | collective-permute-start | bytes 1179656 | tf_op jit(solution)/shard_map/gather_over_replicas/ppermute | solution.py:392
  107.4 15.2 %collective-permute-start.17 = (bf16[6,32,1024]{2,1,0:T(8,128)(2,1)S(1)}, bf16[6,32,1024]{2,1,0:T(8,128)(2,1)S(1)}, u32[]{:S(2)}, u32[]{:S(2)}) collective-permute-start(bf16[6,32,1024]{2,1,0:T(8,128)(2,1)S(1)} %get-tuple-element.60), channel_id=1, source_target_pairs={{0,96},{32,0},{64,32},{96,64},{1,97},{33,1},{65,33},{97,65},{2,98}... | collective-permute-start | bytes 1179656 | tf_op jit(solution)/shard_map/gather_over_replicas/ppermute | solution.py:396
  107.4 16.3 %collective-permute-start.18 = (bf16[6,32,1024]{2,1,0:T(8,128)(2,1)S(1)}, bf16[6,32,1024]{2,1,0:T(8,128)(2,1)S(1)}, u32[]{:S(2)}, u32[]{:S(2)}) collective-permute-start(bf16[6,32,1024]{2,1,0:T(8,128)(2,1)S(1)} %get-tuple-element.61), channel_id=1, source_target_pairs={{0,32},{32,64},{64,96},{96,0},{1,33},{33,65},{65,97},{97,1},{2,34}... | collective-permute-start | bytes 1179656 | tf_op jit(solution)/shard_map/gather_over_replicas/ppermute | solution.py:397
  115.3 15.8 %collective-permute-start.21 = (bf16[6,32,1024]{2,1,0:T(8,128)(2,1)S(1)}, bf16[6,32,1024]{2,1,0:T(8,128)(2,1)S(1)}, u32[]{:S(2)}, u32[]{:S(2)}) collective-permute-start(bf16[6,32,1024]{2,1,0:T(8,128)(2,1)S(1)} %collective-permute-done.12.refs_2_), channel_id=1, source_target_pairs={{0,96},{32,0},{64,32},{96,64},{1,97},{33,1},{65,33},{97,65},{2,98}... | collective-permute-start | bytes 1179656 | tf_op jit(solution)/shard_map/gather_over_replicas/ppermute | solution.py:401
  117.6 14.6 %collective-permute-start.22 = (bf16[6,32,1024]{2,1,0:T(8,128)(2,1)S(1)}, bf16[6,32,1024]{2,1,0:T(8,128)(2,1)S(1)}, u32[]{:S(2)}, u32[]{:S(2)}) collective-permute-start(bf16[6,32,1024]{2,1,0:T(8,128)(2,1)S(1)} %collective-permute-done.13.refs_3_), channel_id=1, source_target_pairs={{0,32},{32,64},{64,96},{96,0},{1,33},{33,65},{65,97},{97,1},{2,34}... | collective-permute-start | bytes 1179656 | tf_op jit(solution)/shard_map/gather_over_replicas/ppermute | solution.py:402
  117.7 16.6 %collective-permute-start.15 = (bf16[12,32,1024]{2,1,0:T(8,128)(2,1)S(1)}, bf16[12,32,1024]{2,1,0:T(8,128)(2,1)S(1)}, u32[]{:S(2)}, u32[]{:S(2)}) collective-permute-start(bf16[12,32,1024]{2,1,0:T(8,128)(2,1)S(1)} %pad_maximum_fusion), channel_id=1, source_target_pairs={{0,16},{16,0},{1,17},{17,1},{2,18},{18,2},{3,19},{19,3},{4,20},{20... | collective-permute-start | bytes 2359304 | tf_op jit(solution)/shard_map/gather_over_replicas/ppermute | solution.py:389
  126.0 7.0 %collective-permute-start.19 = (bf16[6,32,1024]{2,1,0:T(8,128)(2,1)S(1)}, bf16[6,32,1024]{2,1,0:T(8,128)(2,1)S(1)}, u32[]{:S(2)}, u32[]{:S(2)}) collective-permute-start(bf16[6,32,1024]{2,1,0:T(8,128)(2,1)S(1)} %collective-permute-done.17.refs_4_), channel_id=1, source_target_pairs={{0,16},{16,0},{1,17},{17,1},{2,18},{18,2},{3,19},{19,3},{4,20},{20... | collective-permute-start | bytes 1179656 | tf_op jit(solution)/shard_map/gather_over_replicas/ppermute | solution.py:389
  127.2 5.7 %collective-permute-start.20 = (bf16[6,32,1024]{2,1,0:T(8,128)(2,1)S(1)}, bf16[6,32,1024]{2,1,0:T(8,128)(2,1)S(1)}, u32[]{:S(2)}, u32[]{:S(2)}) collective-permute-start(bf16[6,32,1024]{2,1,0:T(8,128)(2,1)S(1)} %collective-permute-done.18.refs_5_), channel_id=1, source_target_pairs={{0,16},{16,0},{1,17},{17,1},{2,18},{18,2},{3,19},{19,3},{4,20},{20... | collective-permute-start | bytes 1179656 | tf_op jit(solution)/shard_map/gather_over_replicas/ppermute | solution.py:389
  131.1 2.5 %collective-permute-start.23 = (bf16[6,32,1024]{2,1,0:T(8,128)(2,1)S(1)}, bf16[6,32,1024]{2,1,0:T(8,128)(2,1)S(1)}, u32[]{:S(2)}, u32[]{:S(2)}) collective-permute-start(bf16[6,32,1024]{2,1,0:T(8,128)(2,1)S(1)} %collective-permute-done.21.refs_3_), channel_id=1, source_target_pairs={{0,16},{16,0},{1,17},{17,1},{2,18},{18,2},{3,19},{19,3},{4,20},{20... | collective-permute-start | bytes 1179656 | tf_op jit(solution)/shard_map/gather_over_replicas/ppermute | solution.py:389
  132.2 2.1 %collective-permute-start.24 = (bf16[6,32,1024]{2,1,0:T(8,128)(2,1)S(1)}, bf16[6,32,1024]{2,1,0:T(8,128)(2,1)S(1)}, u32[]{:S(2)}, u32[]{:S(2)}) collective-permute-start(bf16[6,32,1024]{2,1,0:T(8,128)(2,1)S(1)} %collective-permute-done.22.refs_4_), channel_id=1, source_target_pairs={{0,16},{16,0},{1,17},{17,1},{2,18},{18,2},{3,19},{19,3},{4,20},{20... | collective-permute-start | bytes 1179656 | tf_op jit(solution)/shard_map/gather_over_replicas/ppermute | solution.py:389
  (3 other events, 8.6 us)

commit v7 on v5

--- a/solution.py
+++ b/solution.py
@@ -28,6 +28,17 @@
         run = slice(start, start + out.shape[0])
         out[...] = (one[run].astype(jnp.float32) + two[run].astype(jnp.float32)).astype(out.dtype)
         start += out.shape[0]
+
+
+def sum_kernel(mine, low_below, low_above, high_above, high_below, out):
+    count, part = mine.shape[0], low_below.shape[0]
+    for run, one, two in (
+        (slice(0, part), low_below, low_above),
+        (slice(part, count), high_above, high_below),
+    ):
+        total = mine[run].astype(jnp.float32) + one[...].astype(jnp.float32)
+        out[run] = (total + two[...].astype(jnp.float32)).astype(out.dtype)
+    out[count:] = jnp.zeros((out.shape[0] - count, *out.shape[1:]), out.dtype)
 
 
 def root_kernel(place, own, sibling, root, grad, stat, step, square, coupled, fourth):
@@ -270,14 +281,17 @@
         low_below, owners = lax.optimization_barrier((low_below, owned_block))
         low_above = lax.ppermute(plus(to_below[:part], from_above), "z", down)
         high_below = lax.ppermute(plus(to_above[part:], from_below), "z", up)
-        summed = jnp.concatenate(
-            [
-                plus(mine[:part], low_below, low_above),
-                plus(mine[part:], high_above, high_below),
-                jnp.zeros((shards - per_plane, rows, width), jnp.bfloat16),
-            ],
-            axis=0,
-        )
+        summed = pl.pallas_call(
+            sum_kernel,
+            out_shape=jax.ShapeDtypeStruct((shards, rows, width), jnp.bfloat16),
+            in_specs=[vmem] * 5,
+            out_specs=vmem,
+            compiler_params=pltpu.CompilerParams(vmem_limit_bytes=8 * mib),
+            cost_estimate=pl.CostEstimate(
+                flops=2 * mine.size, bytes_accessed=8 * mine.size, transcendentals=0
+            ),
+            name="sum_rows",
+        )(mine, low_below, low_above, high_above, high_below)
 
     block = plane * per_plane + slot
     active = jnp.any(owners == block) & (slot < per_plane)

time: 136 us -> 135 us (level)
    convert_element_type x6 -> x5, other arithmetic: 6.55 us -> 6.1 us  [plus(): return total.astype(jnp.bfloat16)]
  transfers between devices with their start and end apart: 25 -> 25, of which waited for: 12 -> 11; matrix products, arithmetic and copies ran while one was open for 9% -> 9% of each run, Pallas kernels for 4% -> 4%
where the time goes in v7:
time: 135 us
  blocking collectives  41 us (30%)
  waiting for transfers between devices  31.7 us (23%)
  starting transfers between devices  29.3 us (22%)
  Pallas kernels  18.3 us (14%)
  other arithmetic  6.87 us (5%)
  local copies, waits for them, and re-layouts  6.66 us (5%)
    all_to_all x1, blocking collectives, local(): lax.all_to_all(summed, ('y', 'x'), 0, 0, tiled=True).reshape(half, width)  22 us
    all_to_all x1, blocking collectives, local(): lax.all_to_all(finished.reshape(shards, rows, width), ('y', 'x'), 0, 0, t...  19 us
    ppermute x7, starting transfers between devices, other_core(): return lax.ppermute(piece, 'core', swap)  7.78 us
    ppermute x1, waiting for transfers between devices, local(): high_below = lax.ppermute(plus(to_above[part:], from_below), 'z', up)  7.15 us
    pallas_call x1, Pallas kernels, local(): pl.pallas_call(root_kernel, out_shape=[jax.ShapeDtypeStruct((3, half, hal...  7.12 us
    reshape x3, local copies, waits for them, and re-layouts, rows_of(): return sliced.reshape(per_plane, rows, width)  6.47 us
    ppermute x1, waiting for transfers between devices, local(): below_high = lax.ppermute(back[part:], 'z', up)  6.4 us
    convert_element_type x5, other arithmetic, plus(): return total.astype(jnp.bfloat16)  6.1 us
  transfers between devices with their start and end apart: 25, of which 11 were waited for; matrix products, arithmetic and copies ran while one was open for 9% of the time, Pallas kernels for 4%

profile of v7, /device:TPU:1, one launch (start us, length us, event | category | flops | bytes accessed | tf_op | source)
XLA Modules:
  0.0 134.7 jit_solution(7463441098976748459)
XLA Ops:
  2.7 3.5 %dynamic-slice_bitcast_fusion.3 = (bf16[12,32,1024]{2,1,0:T(8,128)(2,1)S(1)}, bf16[12,32,1024]{2,1,0:T(8,128)(2,1)}, bf16[12,32,1024]{2,1,0:T(8,128)(2,1)}, bf16[12,32,1024]{2,1,0:T(8,128)(2,1)S(1)}) fusion(bf16[4,12,2,32,1024]{4,3,2,1,0:T(8,128)(2,1)} %bitcast.43, s32[]{:T(128)S(6)} %select_n.82, s32[]{:T(128)S(6)} %select_n.73, s32[]{:T(128)S(6)} %select_n.80, ...), kind=kLoop, calls=%fused_computation.9 | loop fusion | bytes 6291480 | tf_op jit(solution)/shard_map/sum_over_replicas/reshape | solution.py:250
  7.0 3.9 %collective-permute-start.5 = (bf16[6,32,1024]{2,1,0:T(8,128)(2,1)S(1)}, bf16[6,32,1024]{2,1,0:T(8,128)(2,1)S(1)}, u32[]{:S(2)}, u32[]{:S(2)}) collective-permute-start(bf16[6,32,1024]{2,1,0:T(8,128)(2,1)S(1)} %get-tuple-element.49), channel_id=1, source_target_pairs={{0,96},{32,0},{64,32},{96,64},{1,97},{33,1},{65,33},{97,65},{2,98}... | collective-permute-start | bytes 1179656 | tf_op jit(solution)/shard_map/sum_over_replicas/ppermute | solution.py:271
  10.9 1.8 %dynamic-slice_bitcast_fusion = (bf16[12,32,1024]{2,1,0:T(8,128)(2,1)S(1)}, bf16[12,32,1024]{2,1,0:T(8,128)(2,1)S(1)}, bf16[12,32,1024]{2,1,0:T(8,128)(2,1)S(1)}) fusion(bf16[4,12,2,32,1024]{4,3,2,1,0:T(8,128)(2,1)} %bitcast.44, s32[]{:T(128)S(6)} %select_n.88, s32[]{:T(128)S(6)} %select_n.76, s32[]{:T(128)S(6)} %select_n.86, s32[]{:T(128)S(6)} %select_n.84), kind=kLoop, calls=%fused_computation.6 | loop fusion | bytes 4718608 | tf_op jit(solution)/shard_map/sum_over_replicas/reshape | solution.py:250
  15.8 2.7 %collective-permute-start.7 = (bf16[6,32,1024]{2,1,0:T(8,128)(2,1)S(1)}, bf16[6,32,1024]{2,1,0:T(8,128)(2,1)S(1)}, u32[]{:S(2)}, u32[]{:S(2)}) collective-permute-start(bf16[6,32,1024]{2,1,0:T(8,128)(2,1)S(1)} %slice.39), channel_id=1, source_target_pairs={{0,96},{32,0},{64,32},{96,64},{1,97},{33,1},{65,33},{97,65},{2,98}... | collective-permute-start | bytes 1179656 | tf_op jit(solution)/shard_map/sum_over_replicas/ppermute | solution.py:280
  18.5 3.5 %collective-permute-done.8 = bf16[6,32,1024]{2,1,0:T(8,128)(2,1)S(1)} collective-permute-done((bf16[6,32,1024]{2,1,0:T(8,128)(2,1)S(1)}, bf16[6,32,1024]{2,1,0:T(8,128)(2,1)S(1)}, u32[]{:S(2)}, u32[]{:S(2)}) %collective-permute-start.8) | collective-permute-done | bytes 393248 | tf_op jit(solution)/shard_map/sum_over_replicas/ppermute | solution.py:272
  23.9 2.7 %collective-permute-start.6 = (bf16[6,32,1024]{2,1,0:T(8,128)(2,1)}, bf16[6,32,1024]{2,1,0:T(8,128)(2,1)S(1)}, u32[]{:S(2)}, u32[]{:S(2)}) collective-permute-start(bf16[6,32,1024]{2,1,0:T(8,128)(2,1)} %add_convert_fusion.4), channel_id=1, source_target_pairs={{0,96},{32,0},{64,32},{96,64},{1,97},{33,1},{65,33},{97,65},{2,98}... | collective-permute-start | bytes 1179656 | tf_op jit(solution)/shard_map/sum_over_replicas/ppermute | solution.py:282
  28.0 2.5 %collective-permute-done.3.low_below = bf16[6,32,1024]{2,1,0:T(8,128)(2,1)S(1)} collective-permute-done((bf16[6,32,1024]{2,1,0:T(8,128)(2,1)S(1)}, bf16[6,32,1024]{2,1,0:T(8,128)(2,1)S(1)}, u32[]{:S(2)}, u32[]{:S(2)}) %collective-permute-start.3) | collective-permute-done | bytes 393248 | tf_op jit(solution)/shard_map/sum_over_replicas/ppermute | solution.py:279
  31.8 7.2 %collective-permute-done.9.high_below = bf16[6,32,1024]{2,1,0:T(8,128)(2,1)S(1)} collective-permute-done((bf16[6,32,1024]{2,1,0:T(8,128)(2,1)}, bf16[6,32,1024]{2,1,0:T(8,128)(2,1)S(1)}, u32[]{:S(2)}, u32[]{:S(2)}) %collective-permute-start.9) | collective-permute-done | bytes 393248 | tf_op jit(solution)/shard_map/sum_over_replicas/ppermute | solution.py:283
  39.2 22.0 %all_to_all.10 = bf16[16,32,1024]{2,1,0:T(8,128)(2,1)S(1)} all-to-all(bf16[16,32,1024]{2,1,0:T(8,128)(2,1)S(1)} %sum_rows.1), channel_id=1, replica_groups=mesh['z'=4,'core'=2,'y'=4,'x'=4] {'y','x'}, dimensions={0} | all-to-all | bytes 2097152 | tf_op jit(solution)/shard_map/rows_to_owner/all_to_all | solution.py:302
  61.2 2.8 %collective-permute-start.10 = (bf16[512,1024]{1,0:T(8,128)(2,1)S(1)}, bf16[512,1024]{1,0:T(8,128)(2,1)S(1)}, u32[]{:S(2)}, u32[]{:S(2)}) collective-permute-start(bf16[512,1024]{1,0:T(8,128)(2,1)S(1)} %bitcast.38), channel_id=1, source_target_pairs={{0,16},{16,0},{1,17},{17,1},{2,18},{18,2},{3,19},{19,3},{4,20},{20... | collective-permute-start | bytes 3145736 | tf_op jit(solution)/shard_map/rows_to_owner/ppermute | solution.py:303
  64.0 2.3 %collective-permute-done.10.sibling = bf16[512,1024]{1,0:T(8,128)(2,1)S(1)} collective-permute-done((bf16[512,1024]{1,0:T(8,128)(2,1)S(1)}, bf16[512,1024]{1,0:T(8,128)(2,1)S(1)}, u32[]{:S(2)}, u32[]{:S(2)}) %collective-permute-start.10) | collective-permute-done | bytes 1048608 | tf_op jit(solution)/shard_map/rows_to_owner/ppermute | solution.py:303
  66.3 7.1 %inverse_root.1 = (bf16[3,512,512]{2,1,0:T(8,128)(2,1)S(1)}, bf16[1024,1024]{1,0:T(8,128)(2,1)S(1)}) custom-call(s32[3]{0:T(128)S(1)} %pad_add_fusion.place, bf16[512,1024]{1,0:T(8,128)(2,1)S(1)} %bitcast.39, bf16[512,1024]{1,0:T(8,128)(2,1)S(1)} %collective-permute-done.10.sibling), custom_call_target="tpu_custom_call" | custom-call | flops 6442450944 | bytes 6291456 | tf_op jit(solution)/shard_map/inverse_root/pallas_call | solution.py:308
  73.8 3.0 %apply_own_root.1 = (bf16[1024,1024]{1,0:T(8,128)(2,1)S(1)}, f32[1,1024]{1,0:T(1,128)S(1)}) custom-call(s32[3]{0:T(128)S(1)} %pad_add_fusion.place, bf16[3,512,512]{2,1,0:T(8,128)(2,1)S(1)} %get-tuple-element.54.root, bf16[1024,1024]{1,0:T(8,128)(2,1)S(1)} %get-tuple-element.55.grad), custom_call_target="tpu_custom_call" | custom-call | flops 2147483648 | bytes 6291456 | tf_op jit(solution)/shard_map/apply_own_root/pallas_call | solution.py:322
  76.9 3.2 %apply_other_root.1 = bf16[512,1024]{1,0:T(8,128)(2,1)S(1)} custom-call(s32[3]{0:T(128)S(1)} %pad_add_fusion.place, bf16[512,1024]{1,0:T(8,128)(2,1)S(1)} %bitcast.40, bf16[1024,1024]{1,0:T(8,128)(2,1)S(1)} %get-tuple-element.56.side, bf16[3,512,512]{2,1,0:T(8,128)(2,1)S(1)} %collective-permute-done.11.root, f32[1,1024]{1,0:T(1,128)S(1)} %get-tuple-element.57.grad_sum), custom_call_target="tpu_custom_call" | custom-call | flops 2147483648 | bytes 6291456 | tf_op jit(solution)/shard_map/apply_other_root/pallas_call | solution.py:331
  80.1 19.0 %all_to_all.11 = bf16[16,32,1024]{2,1,0:T(8,128)(2,1)S(1)} all-to-all(bf16[16,32,1024]{2,1,0:T(8,128)(2,1)S(1)} %bitcast.41), channel_id=1, replica_groups=mesh['z'=4,'core'=2,'y'=4,'x'=4] {'y','x'}, dimensions={0} | all-to-all | bytes 2097152 | tf_op jit(solution)/shard_map/rows_to_shards/all_to_all | solution.py:343
  99.1 1.8 %collective-permute-start.14 = (bf16[12,32,1024]{2,1,0:T(8,128)(2,1)S(1)}, bf16[12,32,1024]{2,1,0:T(8,128)(2,1)S(1)}, u32[]{:S(2)}, u32[]{:S(2)}) collective-permute-start(bf16[12,32,1024]{2,1,0:T(8,128)(2,1)S(1)} %slice.43.refs_0_), channel_id=1, source_target_pairs={{0,16},{16,0},{1,17},{17,1},{2,18},{18,2},{3,19},{19,3},{4,20},{20... | collective-permute-start | bytes 2359304 | tf_op jit(solution)/shard_map/gather_over_replicas/ppermute | solution.py:373
  101.3 2.7 %collective-permute-start.12 = (bf16[6,32,1024]{2,1,0:T(8,128)(2,1)S(1)}, bf16[6,32,1024]{2,1,0:T(8,128)(2,1)S(1)}, u32[]{:S(2)}, u32[]{:S(2)}) collective-permute-start(bf16[6,32,1024]{2,1,0:T(8,128)(2,1)S(1)} %get-tuple-element.61), channel_id=1, source_target_pairs={{0,96},{32,0},{64,32},{96,64},{1,97},{33,1},{65,33},{97,65},{2,98}... | collective-permute-start | bytes 1179656 | tf_op jit(solution)/shard_map/gather_over_replicas/ppermute | solution.py:376
  106.9 6.4 %collective-permute-done.13.refs_3_ = bf16[6,32,1024]{2,1,0:T(8,128)(2,1)S(1)} collective-permute-done((bf16[6,32,1024]{2,1,0:T(8,128)(2,1)S(1)}, bf16[6,32,1024]{2,1,0:T(8,128)(2,1)S(1)}, u32[]{:S(2)}, u32[]{:S(2)}) %collective-permute-start.13) | collective-permute-done | bytes 393248 | tf_op jit(solution)/shard_map/gather_over_replicas/ppermute | solution.py:377
  113.3 2.4 %collective-permute-start.21 = (bf16[6,32,1024]{2,1,0:T(8,128)(2,1)S(1)}, bf16[6,32,1024]{2,1,0:T(8,128)(2,1)S(1)}, u32[]{:S(2)}, u32[]{:S(2)}) collective-permute-start(bf16[6,32,1024]{2,1,0:T(8,128)(2,1)S(1)} %collective-permute-done.12.refs_2_), channel_id=1, source_target_pairs={{0,96},{32,0},{64,32},{96,64},{1,97},{33,1},{65,33},{97,65},{2,98}... | collective-permute-start | bytes 1179656 | tf_op jit(solution)/shard_map/gather_over_replicas/ppermute | solution.py:385
  115.7 2.2 %collective-permute-start.15 = (bf16[12,32,1024]{2,1,0:T(8,128)(2,1)S(1)}, bf16[12,32,1024]{2,1,0:T(8,128)(2,1)S(1)}, u32[]{:S(2)}, u32[]{:S(2)}) collective-permute-start(bf16[12,32,1024]{2,1,0:T(8,128)(2,1)S(1)} %pad_maximum_fusion), channel_id=1, source_target_pairs={{0,16},{16,0},{1,17},{17,1},{2,18},{18,2},{3,19},{19,3},{4,20},{20... | collective-permute-start | bytes 2359304 | tf_op jit(solution)/shard_map/gather_over_replicas/ppermute | solution.py:373
  117.9 2.7 %collective-permute-done.17.refs_4_ = bf16[6,32,1024]{2,1,0:T(8,128)(2,1)S(1)} collective-permute-done((bf16[6,32,1024]{2,1,0:T(8,128)(2,1)S(1)}, bf16[6,32,1024]{2,1,0:T(8,128)(2,1)S(1)}, u32[]{:S(2)}, u32[]{:S(2)}) %collective-permute-start.17) | collective-permute-done | bytes 393248 | tf_op jit(solution)/shard_map/gather_over_replicas/ppermute | solution.py:380
  121.7 2.3 %place_early.1.refs_7_ = bf16[48,64,1024]{2,1,0:T(8,128)(2,1)} custom-call(s32[3]{0:T(128)S(1)} %pad_add_fusion.place, bf16[12,32,1024]{2,1,0:T(8,128)(2,1)S(1)} %slice.43.refs_0_, bf16[12,32,1024]{2,1,0:T(8,128)(2,1)S(1)} %collective-permute-done.14.refs_1_, bf16[6,32,1024]{2,1,0:T(8,128)(2,1)S(1)} %collective-permute-done.12.refs_2_, ...), custom_call_target="tpu_custom_call" | custom-call | bytes 6291456 | tf_op jit(solution)/shard_map/gather_over_replicas/place_early/pallas_call | solution.py:360
  125.3 3.8 %collective-permute-done.21.refs_3_ = bf16[6,32,1024]{2,1,0:T(8,128)(2,1)S(1)} collective-permute-done((bf16[6,32,1024]{2,1,0:T(8,128)(2,1)S(1)}, bf16[6,32,1024]{2,1,0:T(8,128)(2,1)S(1)}, u32[]{:S(2)}, u32[]{:S(2)}) %collective-permute-start.21) | collective-permute-done | bytes 393248 | tf_op jit(solution)/shard_map/gather_over_replicas/ppermute | solution.py:385
  132.3 2.3 %place_late.1 = bf16[48,64,1024]{2,1,0:T(8,128)(2,1)} custom-call(s32[3]{0:T(128)S(1)} %pad_add_fusion.place, bf16[12,32,1024]{2,1,0:T(8,128)(2,1)S(1)} %collective-permute-done.15.refs_0_, bf16[6,32,1024]{2,1,0:T(8,128)(2,1)S(1)} %collective-permute-done.19.refs_1_, ...), custom_call_target="tpu_custom_call", output_to_operand_aliasing={{}: (8, {})} | custom-call | bytes 6291456 | tf_op jit(solution)/shard_map/gather_over_replicas/place_late/pallas_call | solution.py:360
  (53 shorter events, 20.2 us)
Async XLA Ops:
  1.2 5.6 %collective-permute-start = (bf16[12,32,1024]{2,1,0:T(8,128)(2,1)S(1)}, bf16[12,32,1024]{2,1,0:T(8,128)(2,1)S(1)}, u32[]{:S(2)}, u32[]{:S(2)}) collective-permute-start(bf16[12,32,1024]{2,1,0:T(8,128)(2,1)S(1)} %dynamic-slice_bitcast_fusion.7), channel_id=1, source_target_pairs={{0,16},{16,0},{1,17},{17,1},{2,18},{18,2},{3,19},{19,3},{4,20},{20... | collective-permute-start | bytes 2359304 | tf_op jit(solution)/shard_map/sum_over_replicas/ppermute | solution.py:254
  6.2 6.6 %collective-permute-start.4 = (bf16[12,32,1024]{2,1,0:T(8,128)(2,1)}, bf16[12,32,1024]{2,1,0:T(8,128)(2,1)}, u32[]{:S(2)}, u32[]{:S(2)}) collective-permute-start(bf16[12,32,1024]{2,1,0:T(8,128)(2,1)} %get-tuple-element.48), channel_id=1, source_target_pairs={{0,16},{16,0},{1,17},{17,1},{2,18},{18,2},{3,19},{19,3},{4,20},{20... | collective-permute-start | bytes 2359304 | tf_op jit(solution)/shard_map/sum_over_replicas/ppermute | solution.py:258
  6.3 7.9 %collective-permute-start.2 = (bf16[12,32,1024]{2,1,0:T(8,128)(2,1)}, bf16[12,32,1024]{2,1,0:T(8,128)(2,1)}, u32[]{:S(2)}, u32[]{:S(2)}) collective-permute-start(bf16[12,32,1024]{2,1,0:T(8,128)(2,1)} %get-tuple-element.45), channel_id=1, source_target_pairs={{0,16},{16,0},{1,17},{17,1},{2,18},{18,2},{3,19},{19,3},{4,20},{20... | collective-permute-start | bytes 2359304 | tf_op jit(solution)/shard_map/sum_over_replicas/ppermute | solution.py:258
  6.7 19.9 %collective-permute-start.1 = (bf16[12,32,1024]{2,1,0:T(8,128)(2,1)S(1)}, bf16[12,32,1024]{2,1,0:T(8,128)(2,1)}, u32[]{:S(2)}, u32[]{:S(2)}) collective-permute-start(bf16[12,32,1024]{2,1,0:T(8,128)(2,1)S(1)} %get-tuple-element.43), channel_id=1, source_target_pairs={{0,16},{16,0},{1,17},{17,1},{2,18},{18,2},{3,19},{19,3},{4,20},{20... | collective-permute-start | bytes 2359304 | tf_op jit(solution)/shard_map/sum_over_replicas/ppermute | solution.py:258
  7.0 16.0 %collective-permute-start.5 = (bf16[6,32,1024]{2,1,0:T(8,128)(2,1)S(1)}, bf16[6,32,1024]{2,1,0:T(8,128)(2,1)S(1)}, u32[]{:S(2)}, u32[]{:S(2)}) collective-permute-start(bf16[6,32,1024]{2,1,0:T(8,128)(2,1)S(1)} %get-tuple-element.49), channel_id=1, source_target_pairs={{0,96},{32,0},{64,32},{96,64},{1,97},{33,1},{65,33},{97,65},{2,98}... | collective-permute-start | bytes 1179656 | tf_op jit(solution)/shard_map/sum_over_replicas/ppermute | solution.py:271
  10.9 11.2 %collective-permute-start.8 = (bf16[6,32,1024]{2,1,0:T(8,128)(2,1)S(1)}, bf16[6,32,1024]{2,1,0:T(8,128)(2,1)S(1)}, u32[]{:S(2)}, u32[]{:S(2)}) collective-permute-start(bf16[6,32,1024]{2,1,0:T(8,128)(2,1)S(1)} %get-tuple-element.50), channel_id=1, source_target_pairs={{0,32},{32,64},{64,96},{96,0},{1,33},{33,65},{65,97},{97,1},{2,34}... | collective-permute-start | bytes 1179656 | tf_op jit(solution)/shard_map/sum_over_replicas/ppermute | solution.py:272
  15.7 14.8 %collective-permute-start.3 = (bf16[6,32,1024]{2,1,0:T(8,128)(2,1)S(1)}, bf16[6,32,1024]{2,1,0:T(8,128)(2,1)S(1)}, u32[]{:S(2)}, u32[]{:S(2)}) collective-permute-start(bf16[6,32,1024]{2,1,0:T(8,128)(2,1)S(1)} %slice.37), channel_id=1, source_target_pairs={{0,32},{32,64},{64,96},{96,0},{1,33},{33,65},{65,97},{97,1},{2,34}... | collective-permute-start | bytes 1179656 | tf_op jit(solution)/shard_map/sum_over_replicas/ppermute | solution.py:279
  15.8 16.0 %collective-permute-start.7 = (bf16[6,32,1024]{2,1,0:T(8,128)(2,1)S(1)}, bf16[6,32,1024]{2,1,0:T(8,128)(2,1)S(1)}, u32[]{:S(2)}, u32[]{:S(2)}) collective-permute-start(bf16[6,32,1024]{2,1,0:T(8,128)(2,1)S(1)} %slice.39), channel_id=1, source_target_pairs={{0,96},{32,0},{64,32},{96,64},{1,97},{33,1},{65,33},{97,65},{2,98}... | collective-permute-start | bytes 1179656 | tf_op jit(solution)/shard_map/sum_over_replicas/ppermute | solution.py:280
  23.0 16.0 %collective-permute-start.9 = (bf16[6,32,1024]{2,1,0:T(8,128)(2,1)}, bf16[6,32,1024]{2,1,0:T(8,128)(2,1)S(1)}, u32[]{:S(2)}, u32[]{:S(2)}) collective-permute-start(bf16[6,32,1024]{2,1,0:T(8,128)(2,1)} %add_convert_fusion.3), channel_id=1, source_target_pairs={{0,32},{32,64},{64,96},{96,0},{1,33},{33,65},{65,97},{97,1},{2,34}... | collective-permute-start | bytes 1179656 | tf_op jit(solution)/shard_map/sum_over_replicas/ppermute | solution.py:283
  23.9 15.1 %collective-permute-start.6 = (bf16[6,32,1024]{2,1,0:T(8,128)(2,1)}, bf16[6,32,1024]{2,1,0:T(8,128)(2,1)S(1)}, u32[]{:S(2)}, u32[]{:S(2)}) collective-permute-start(bf16[6,32,1024]{2,1,0:T(8,128)(2,1)} %add_convert_fusion.4), channel_id=1, source_target_pairs={{0,96},{32,0},{64,32},{96,64},{1,97},{33,1},{65,33},{97,65},{2,98}... | collective-permute-start | bytes 1179656 | tf_op jit(solution)/shard_map/sum_over_replicas/ppermute | solution.py:282
  61.2 5.1 %collective-permute-start.10 = (bf16[512,1024]{1,0:T(8,128)(2,1)S(1)}, bf16[512,1024]{1,0:T(8,128)(2,1)S(1)}, u32[]{:S(2)}, u32[]{:S(2)}) collective-permute-start(bf16[512,1024]{1,0:T(8,128)(2,1)S(1)} %bitcast.38), channel_id=1, source_target_pairs={{0,16},{16,0},{1,17},{17,1},{2,18},{18,2},{3,19},{19,3},{4,20},{20... | collective-permute-start | bytes 3145736 | tf_op jit(solution)/shard_map/rows_to_owner/ppermute | solution.py:303
  73.4 3.5 %collective-permute-start.11 = (bf16[3,512,512]{2,1,0:T(8,128)(2,1)S(1)}, bf16[3,512,512]{2,1,0:T(8,128)(2,1)S(1)}, u32[]{:S(2)}, u32[]{:S(2)}) collective-permute-start(bf16[3,512,512]{2,1,0:T(8,128)(2,1)S(1)} %get-tuple-element.54.root), channel_id=1, source_target_pairs={{0,16},{16,0},{1,17},{17,1},{2,18},{18,2},{3,19},{19,3},{4,20},{20... | collective-permute-start | bytes 4718600 | tf_op jit(solution)/shard_map/ppermute | solution.py:321
  99.1 14.1 %collective-permute-start.14 = (bf16[12,32,1024]{2,1,0:T(8,128)(2,1)S(1)}, bf16[12,32,1024]{2,1,0:T(8,128)(2,1)S(1)}, u32[]{:S(2)}, u32[]{:S(2)}) collective-permute-start(bf16[12,32,1024]{2,1,0:T(8,128)(2,1)S(1)} %slice.43.refs_0_), channel_id=1, source_target_pairs={{0,16},{16,0},{1,17},{17,1},{2,18},{18,2},{3,19},{19,3},{4,20},{20... | collective-permute-start | bytes 2359304 | tf_op jit(solution)/shard_map/gather_over_replicas/ppermute | solution.py:373
  101.0 12.2 %collective-permute-start.13 = (bf16[6,32,1024]{2,1,0:T(8,128)(2,1)S(1)}, bf16[6,32,1024]{2,1,0:T(8,128)(2,1)S(1)}, u32[]{:S(2)}, u32[]{:S(2)}) collective-permute-start(bf16[6,32,1024]{2,1,0:T(8,128)(2,1)S(1)} %get-tuple-element.60), channel_id=1, source_target_pairs={{0,32},{32,64},{64,96},{96,0},{1,33},{33,65},{65,97},{97,1},{2,34}... | collective-permute-start | bytes 1179656 | tf_op jit(solution)/shard_map/gather_over_replicas/ppermute | solution.py:377
  101.3 11.9 %collective-permute-start.12 = (bf16[6,32,1024]{2,1,0:T(8,128)(2,1)S(1)}, bf16[6,32,1024]{2,1,0:T(8,128)(2,1)S(1)}, u32[]{:S(2)}, u32[]{:S(2)}) collective-permute-start(bf16[6,32,1024]{2,1,0:T(8,128)(2,1)S(1)} %get-tuple-element.61), channel_id=1, source_target_pairs={{0,96},{32,0},{64,32},{96,64},{1,97},{33,1},{65,33},{97,65},{2,98}... | collective-permute-start | bytes 1179656 | tf_op jit(solution)/shard_map/gather_over_replicas/ppermute | solution.py:376
  105.4 15.2 %collective-permute-start.17 = (bf16[6,32,1024]{2,1,0:T(8,128)(2,1)S(1)}, bf16[6,32,1024]{2,1,0:T(8,128)(2,1)S(1)}, u32[]{:S(2)}, u32[]{:S(2)}) collective-permute-start(bf16[6,32,1024]{2,1,0:T(8,128)(2,1)S(1)} %get-tuple-element.60), channel_id=1, source_target_pairs={{0,96},{32,0},{64,32},{96,64},{1,97},{33,1},{65,33},{97,65},{2,98}... | collective-permute-start | bytes 1179656 | tf_op jit(solution)/shard_map/gather_over_replicas/ppermute | solution.py:380
  105.4 16.3 %collective-permute-start.18 = (bf16[6,32,1024]{2,1,0:T(8,128)(2,1)S(1)}, bf16[6,32,1024]{2,1,0:T(8,128)(2,1)S(1)}, u32[]{:S(2)}, u32[]{:S(2)}) collective-permute-start(bf16[6,32,1024]{2,1,0:T(8,128)(2,1)S(1)} %get-tuple-element.61), channel_id=1, source_target_pairs={{0,32},{32,64},{64,96},{96,0},{1,33},{33,65},{65,97},{97,1},{2,34}... | collective-permute-start | bytes 1179656 | tf_op jit(solution)/shard_map/gather_over_replicas/ppermute | solution.py:381
  113.3 15.8 %collective-permute-start.21 = (bf16[6,32,1024]{2,1,0:T(8,128)(2,1)S(1)}, bf16[6,32,1024]{2,1,0:T(8,128)(2,1)S(1)}, u32[]{:S(2)}, u32[]{:S(2)}) collective-permute-start(bf16[6,32,1024]{2,1,0:T(8,128)(2,1)S(1)} %collective-permute-done.12.refs_2_), channel_id=1, source_target_pairs={{0,96},{32,0},{64,32},{96,64},{1,97},{33,1},{65,33},{97,65},{2,98}... | collective-permute-start | bytes 1179656 | tf_op jit(solution)/shard_map/gather_over_replicas/ppermute | solution.py:385
  115.6 14.6 %collective-permute-start.22 = (bf16[6,32,1024]{2,1,0:T(8,128)(2,1)S(1)}, bf16[6,32,1024]{2,1,0:T(8,128)(2,1)S(1)}, u32[]{:S(2)}, u32[]{:S(2)}) collective-permute-start(bf16[6,32,1024]{2,1,0:T(8,128)(2,1)S(1)} %collective-permute-done.13.refs_3_), channel_id=1, source_target_pairs={{0,32},{32,64},{64,96},{96,0},{1,33},{33,65},{65,97},{97,1},{2,34}... | collective-permute-start | bytes 1179656 | tf_op jit(solution)/shard_map/gather_over_replicas/ppermute | solution.py:386
  115.7 16.6 %collective-permute-start.15 = (bf16[12,32,1024]{2,1,0:T(8,128)(2,1)S(1)}, bf16[12,32,1024]{2,1,0:T(8,128)(2,1)S(1)}, u32[]{:S(2)}, u32[]{:S(2)}) collective-permute-start(bf16[12,32,1024]{2,1,0:T(8,128)(2,1)S(1)} %pad_maximum_fusion), channel_id=1, source_target_pairs={{0,16},{16,0},{1,17},{17,1},{2,18},{18,2},{3,19},{19,3},{4,20},{20... | collective-permute-start | bytes 2359304 | tf_op jit(solution)/shard_map/gather_over_replicas/ppermute | solution.py:373
  123.9 7.0 %collective-permute-start.19 = (bf16[6,32,1024]{2,1,0:T(8,128)(2,1)S(1)}, bf16[6,32,1024]{2,1,0:T(8,128)(2,1)S(1)}, u32[]{:S(2)}, u32[]{:S(2)}) collective-permute-start(bf16[6,32,1024]{2,1,0:T(8,128)(2,1)S(1)} %collective-permute-done.17.refs_4_), channel_id=1, source_target_pairs={{0,16},{16,0},{1,17},{17,1},{2,18},{18,2},{3,19},{19,3},{4,20},{20... | collective-permute-start | bytes 1179656 | tf_op jit(solution)/shard_map/gather_over_replicas/ppermute | solution.py:373
  125.2 5.7 %collective-permute-start.20 = (bf16[6,32,1024]{2,1,0:T(8,128)(2,1)S(1)}, bf16[6,32,1024]{2,1,0:T(8,128)(2,1)S(1)}, u32[]{:S(2)}, u32[]{:S(2)}) collective-permute-start(bf16[6,32,1024]{2,1,0:T(8,128)(2,1)S(1)} %collective-permute-done.18.refs_5_), channel_id=1, source_target_pairs={{0,16},{16,0},{1,17},{17,1},{2,18},{18,2},{3,19},{19,3},{4,20},{20... | collective-permute-start | bytes 1179656 | tf_op jit(solution)/shard_map/gather_over_replicas/ppermute | solution.py:373
  129.1 2.5 %collective-permute-start.23 = (bf16[6,32,1024]{2,1,0:T(8,128)(2,1)S(1)}, bf16[6,32,1024]{2,1,0:T(8,128)(2,1)S(1)}, u32[]{:S(2)}, u32[]{:S(2)}) collective-permute-start(bf16[6,32,1024]{2,1,0:T(8,128)(2,1)S(1)} %collective-permute-done.21.refs_3_), channel_id=1, source_target_pairs={{0,16},{16,0},{1,17},{17,1},{2,18},{18,2},{3,19},{19,3},{4,20},{20... | collective-permute-start | bytes 1179656 | tf_op jit(solution)/shard_map/gather_over_replicas/ppermute | solution.py:373
  130.2 2.1 %collective-permute-start.24 = (bf16[6,32,1024]{2,1,0:T(8,128)(2,1)S(1)}, bf16[6,32,1024]{2,1,0:T(8,128)(2,1)S(1)}, u32[]{:S(2)}, u32[]{:S(2)}) collective-permute-start(bf16[6,32,1024]{2,1,0:T(8,128)(2,1)S(1)} %collective-permute-done.22.refs_4_), channel_id=1, source_target_pairs={{0,16},{16,0},{1,17},{17,1},{2,18},{18,2},{3,19},{19,3},{4,20},{20... | collective-permute-start | bytes 1179656 | tf_op jit(solution)/shard_map/gather_over_replicas/ppermute | solution.py:373
  (2 other events, 8.9 us)

commit v8 on v7

--- a/solution.py
+++ b/solution.py
@@ -249,6 +249,21 @@
         )
         return sliced.reshape(per_plane, rows, width)
 
+    def add(one, two, runs):
+        return pl.pallas_call(
+            add_kernel,
+            out_shape=[
+                jax.ShapeDtypeStruct((one.shape[0] // runs, rows, width), jnp.bfloat16)
+            ] * runs,
+            in_specs=[vmem] * 2,
+            out_specs=[vmem] * runs,
+            compiler_params=pltpu.CompilerParams(vmem_limit_bytes=8 * mib),
+            cost_estimate=pl.CostEstimate(
+                flops=one.size, bytes_accessed=6 * one.size, transcendentals=0
+            ),
+            name="add_rows",
+        )(one, two)
+
     with jax.named_scope("sum_over_replicas"):
         sent, next_plane = lax.optimization_barrier((rows_of(plane, 2, 1 - core), plane))
         got = lax.ppermute(sent, "core", swap)
@@ -256,17 +271,7 @@
             [rows_of(next_plane, 2, core)] + [rows_of(next_plane, k, 1 - core) for k in (1, 3, 0)]
         )
         got_above, got_below, got_mine = (lax.ppermute(each, "core", swap) for each in sent)
-        far_low, far_high = pl.pallas_call(
-            add_kernel,
-            out_shape=[jax.ShapeDtypeStruct((part, rows, width), jnp.bfloat16)] * 2,
-            in_specs=[vmem] * 2,
-            out_specs=[vmem] * 2,
-            compiler_params=pltpu.CompilerParams(vmem_limit_bytes=8 * mib),
-            cost_estimate=pl.CostEstimate(
-                flops=kept.size, bytes_accessed=6 * kept.size, transcendentals=0
-            ),
-            name="add_rows",
-        )(kept, got)
+        far_low, far_high = add(kept, got, 2)
         far_low, far_high, here = lax.optimization_barrier((far_low, far_high, plane))
         from_above = lax.ppermute(far_low, "z", down)
         from_below = lax.ppermute(far_high, "z", up)
@@ -279,8 +284,8 @@
         low_below = lax.ppermute(to_above[:part], "z", up)
         high_above = lax.ppermute(to_below[part:], "z", down)
         low_below, owners = lax.optimization_barrier((low_below, owned_block))
-        low_above = lax.ppermute(plus(to_below[:part], from_above), "z", down)
-        high_below = lax.ppermute(plus(to_above[part:], from_below), "z", up)
+        low_above = lax.ppermute(*add(to_below[:part], from_above, 1), "z", down)
+        high_below = lax.ppermute(*add(to_above[part:], from_below, 1), "z", up)
         summed = pl.pallas_call(
             sum_kernel,
             out_shape=jax.ShapeDtypeStruct((shards, rows, width), jnp.bfloat16),

time: 135 us -> 135 us (level)
  other arithmetic: 6.87 us -> 4.28 us
    ppermute x1, waiting for transfers between devices: 2.51 us -> 6.31 us  [local(): low_below = lax.ppermute(to_above[:part], 'z', up)]
    ppermute x1, waiting for transfers between devices: 3.53 us -> 0.01 us  [local(): from_below = lax.ppermute(far_high, 'z', up)]
    convert_element_type x5 -> x2, other arithmetic: 6.1 us -> 3.5 us  [plus(): return total.astype(jnp.bfloat16)]
  transfers between devices with their start and end apart: 25 -> 25, of which waited for: 11 -> 13; matrix products, arithmetic and copies ran while one was open for 9% -> 8% of each run, Pallas kernels for 4% -> 4%
where the time goes in v8:
time: 135 us
  blocking collectives  41 us (30%)
  waiting for transfers between devices  32.5 us (24%)
  starting transfers between devices  30.1 us (22%)
  Pallas kernels  18.5 us (14%)
  local copies, waits for them, and re-layouts  7.46 us (6%)
  other arithmetic  4.28 us (3%)
    all_to_all x1, blocking collectives, local(): lax.all_to_all(summed, ('y', 'x'), 0, 0, tiled=True).reshape(half, width)  22 us
    all_to_all x1, blocking collectives, local(): lax.all_to_all(finished.reshape(shards, rows, width), ('y', 'x'), 0, 0, t...  19 us
    ppermute x7, starting transfers between devices, other_core(): return lax.ppermute(piece, 'core', swap)  7.77 us
    pallas_call x1, Pallas kernels, local(): pl.pallas_call(root_kernel, out_shape=[jax.ShapeDtypeStruct((3, half, hal...  7.13 us
    reshape x3, local copies, waits for them, and re-layouts, rows_of(): return sliced.reshape(per_plane, rows, width)  6.48 us
    ppermute x1, waiting for transfers between devices, local(): below_high = lax.ppermute(back[part:], 'z', up)  6.4 us
    ppermute x1, waiting for transfers between devices, local(): low_below = lax.ppermute(to_above[:part], 'z', up)  6.31 us
    pallas_call x2, Pallas kernels, put(): pl.pallas_call(functools.partial(place_kernel, targets), out_shape=out_sh...  4.52 us
  transfers between devices with their start and end apart: 25, of which 13 were waited for; matrix products, arithmetic and copies ran while one was open for 8% of the time, Pallas kernels for 4%

profile of v8, /device:TPU:1, one launch (start us, length us, event | category | flops | bytes accessed | tf_op | source)
XLA Modules:
  0.0 134.7 jit_solution(1282140620247095280)
XLA Ops:
  2.7 3.5 %dynamic-slice_bitcast_fusion.3 = (bf16[12,32,1024]{2,1,0:T(8,128)(2,1)S(1)}, bf16[12,32,1024]{2,1,0:T(8,128)(2,1)}, bf16[12,32,1024]{2,1,0:T(8,128)(2,1)}, bf16[12,32,1024]{2,1,0:T(8,128)(2,1)S(1)}) fusion(bf16[4,12,2,32,1024]{4,3,2,1,0:T(8,128)(2,1)} %bitcast.43, s32[]{:T(128)S(6)} %select_n.82, s32[]{:T(128)S(6)} %select_n.73, s32[]{:T(128)S(6)} %select_n.80, ...), kind=kLoop, calls=%fused_computation.7 | loop fusion | bytes 6291480 | tf_op jit(solution)/shard_map/sum_over_replicas/reshape | solution.py:250
  7.0 3.9 %collective-permute-start.5 = (bf16[6,32,1024]{2,1,0:T(8,128)(2,1)S(1)}, bf16[6,32,1024]{2,1,0:T(8,128)(2,1)S(1)}, u32[]{:S(2)}, u32[]{:S(2)}) collective-permute-start(bf16[6,32,1024]{2,1,0:T(8,128)(2,1)S(1)} %get-tuple-element.49), channel_id=1, source_target_pairs={{0,96},{32,0},{64,32},{96,64},{1,97},{33,1},{65,33},{97,65},{2,98}... | collective-permute-start | bytes 1179656 | tf_op jit(solution)/shard_map/sum_over_replicas/ppermute | solution.py:276
  10.9 1.8 %dynamic-slice_bitcast_fusion = (bf16[12,32,1024]{2,1,0:T(8,128)(2,1)S(1)}, bf16[12,32,1024]{2,1,0:T(8,128)(2,1)S(1)}, bf16[12,32,1024]{2,1,0:T(8,128)(2,1)S(1)}) fusion(bf16[4,12,2,32,1024]{4,3,2,1,0:T(8,128)(2,1)} %bitcast.44, s32[]{:T(128)S(6)} %select_n.88, s32[]{:T(128)S(6)} %select_n.76, s32[]{:T(128)S(6)} %select_n.86, s32[]{:T(128)S(6)} %select_n.84), kind=kLoop, calls=%fused_computation.4 | loop fusion | bytes 4718608 | tf_op jit(solution)/shard_map/sum_over_replicas/reshape | solution.py:250
  12.8 2.1 %add_convert_fusion = (bf16[12,32,1024]{2,1,0:T(8,128)(2,1)S(1)}, bf16[12,32,1024]{2,1,0:T(8,128)(2,1)S(1)}) fusion(bf16[12,32,1024]{2,1,0:T(8,128)(2,1)} %collective-permute-done.4, bf16[12,32,1024]{2,1,0:T(8,128)(2,1)S(1)} %get-tuple-element.47, bf16[12,32,1024]{2,1,0:T(8,128)(2,1)} %collective-permute-done.2, bf16[12,32,1024]{2,1,0:T(8,128)(2,1)S(1)} %get-tuple-element.44), kind=kLoop, calls=%fused_computation | loop fusion | flops 3145728 | bytes 4718592 | tf_op jit(solution)/shard_map/sum_over_replicas/convert_element_type | solution.py:239
  15.8 2.7 %collective-permute-start.7 = (bf16[6,32,1024]{2,1,0:T(8,128)(2,1)}, bf16[6,32,1024]{2,1,0:T(8,128)(2,1)S(1)}, u32[]{:S(2)}, u32[]{:S(2)}) collective-permute-start(bf16[6,32,1024]{2,1,0:T(8,128)(2,1)} %get-tuple-element.78), channel_id=1, source_target_pairs={{0,96},{32,0},{64,32},{96,64},{1,97},{33,1},{65,33},{97,65},{2,98}... | collective-permute-start | bytes 1179656 | tf_op jit(solution)/shard_map/sum_over_replicas/ppermute | solution.py:285
  19.1 3.5 %collective-permute-start.6 = (bf16[6,32,1024]{2,1,0:T(8,128)(2,1)S(1)}, bf16[6,32,1024]{2,1,0:T(8,128)(2,1)S(1)}, u32[]{:S(2)}, u32[]{:S(2)}) collective-permute-start(bf16[6,32,1024]{2,1,0:T(8,128)(2,1)S(1)} %add_rows.4), channel_id=1, source_target_pairs={{0,96},{32,0},{64,32},{96,64},{1,97},{33,1},{65,33},{97,65},{2,98}... | collective-permute-start | bytes 1179656 | tf_op jit(solution)/shard_map/sum_over_replicas/ppermute | solution.py:287
  24.2 6.3 %collective-permute-done.3.low_below = bf16[6,32,1024]{2,1,0:T(8,128)(2,1)S(1)} collective-permute-done((bf16[6,32,1024]{2,1,0:T(8,128)(2,1)S(1)}, bf16[6,32,1024]{2,1,0:T(8,128)(2,1)S(1)}, u32[]{:S(2)}, u32[]{:S(2)}) %collective-permute-start.3) | collective-permute-done | bytes 393248 | tf_op jit(solution)/shard_map/sum_over_replicas/ppermute | solution.py:284
  31.8 4.1 %collective-permute-done.6.low_above = bf16[6,32,1024]{2,1,0:T(8,128)(2,1)S(1)} collective-permute-done((bf16[6,32,1024]{2,1,0:T(8,128)(2,1)S(1)}, bf16[6,32,1024]{2,1,0:T(8,128)(2,1)S(1)}, u32[]{:S(2)}, u32[]{:S(2)}) %collective-permute-start.6) | collective-permute-done | bytes 393248 | tf_op jit(solution)/shard_map/sum_over_replicas/ppermute | solution.py:287
  35.9 3.0 %collective-permute-done.9.high_below = bf16[6,32,1024]{2,1,0:T(8,128)(2,1)S(1)} collective-permute-done((bf16[6,32,1024]{2,1,0:T(8,128)(2,1)S(1)}, bf16[6,32,1024]{2,1,0:T(8,128)(2,1)S(1)}, u32[]{:S(2)}, u32[]{:S(2)}) %collective-permute-start.9) | collective-permute-done | bytes 393248 | tf_op jit(solution)/shard_map/sum_over_replicas/ppermute | solution.py:288
  39.2 22.0 %all_to_all.10 = bf16[16,32,1024]{2,1,0:T(8,128)(2,1)S(1)} all-to-all(bf16[16,32,1024]{2,1,0:T(8,128)(2,1)S(1)} %sum_rows.1), channel_id=1, replica_groups=mesh['z'=4,'core'=2,'y'=4,'x'=4] {'y','x'}, dimensions={0} | all-to-all | bytes 2097152 | tf_op jit(solution)/shard_map/rows_to_owner/all_to_all | solution.py:307
  61.2 2.8 %collective-permute-start.10 = (bf16[512,1024]{1,0:T(8,128)(2,1)S(1)}, bf16[512,1024]{1,0:T(8,128)(2,1)S(1)}, u32[]{:S(2)}, u32[]{:S(2)}) collective-permute-start(bf16[512,1024]{1,0:T(8,128)(2,1)S(1)} %bitcast.38), channel_id=1, source_target_pairs={{0,16},{16,0},{1,17},{17,1},{2,18},{18,2},{3,19},{19,3},{4,20},{20... | collective-permute-start | bytes 3145736 | tf_op jit(solution)/shard_map/rows_to_owner/ppermute | solution.py:308
  64.0 2.3 %collective-permute-done.10.sibling = bf16[512,1024]{1,0:T(8,128)(2,1)S(1)} collective-permute-done((bf16[512,1024]{1,0:T(8,128)(2,1)S(1)}, bf16[512,1024]{1,0:T(8,128)(2,1)S(1)}, u32[]{:S(2)}, u32[]{:S(2)}) %collective-permute-start.10) | collective-permute-done | bytes 1048608 | tf_op jit(solution)/shard_map/rows_to_owner/ppermute | solution.py:308
  66.3 7.1 %inverse_root.1 = (bf16[3,512,512]{2,1,0:T(8,128)(2,1)S(1)}, bf16[1024,1024]{1,0:T(8,128)(2,1)S(1)}) custom-call(s32[3]{0:T(128)S(1)} %pad_add_fusion.place, bf16[512,1024]{1,0:T(8,128)(2,1)S(1)} %bitcast.39, bf16[512,1024]{1,0:T(8,128)(2,1)S(1)} %collective-permute-done.10.sibling), custom_call_target="tpu_custom_call" | custom-call | flops 6442450944 | bytes 6291456 | tf_op jit(solution)/shard_map/inverse_root/pallas_call | solution.py:313
  73.8 3.0 %apply_own_root.1 = (bf16[1024,1024]{1,0:T(8,128)(2,1)S(1)}, f32[1,1024]{1,0:T(1,128)S(1)}) custom-call(s32[3]{0:T(128)S(1)} %pad_add_fusion.place, bf16[3,512,512]{2,1,0:T(8,128)(2,1)S(1)} %get-tuple-element.54.root, bf16[1024,1024]{1,0:T(8,128)(2,1)S(1)} %get-tuple-element.55.grad), custom_call_target="tpu_custom_call" | custom-call | flops 2147483648 | bytes 6291456 | tf_op jit(solution)/shard_map/apply_own_root/pallas_call | solution.py:327
  76.9 3.2 %apply_other_root.1 = bf16[512,1024]{1,0:T(8,128)(2,1)S(1)} custom-call(s32[3]{0:T(128)S(1)} %pad_add_fusion.place, bf16[512,1024]{1,0:T(8,128)(2,1)S(1)} %bitcast.40, bf16[1024,1024]{1,0:T(8,128)(2,1)S(1)} %get-tuple-element.56.side, bf16[3,512,512]{2,1,0:T(8,128)(2,1)S(1)} %collective-permute-done.11.root, f32[1,1024]{1,0:T(1,128)S(1)} %get-tuple-element.57.grad_sum), custom_call_target="tpu_custom_call" | custom-call | flops 2147483648 | bytes 6291456 | tf_op jit(solution)/shard_map/apply_other_root/pallas_call | solution.py:336
  80.1 19.0 %all_to_all.11 = bf16[16,32,1024]{2,1,0:T(8,128)(2,1)S(1)} all-to-all(bf16[16,32,1024]{2,1,0:T(8,128)(2,1)S(1)} %bitcast.41), channel_id=1, replica_groups=mesh['z'=4,'core'=2,'y'=4,'x'=4] {'y','x'}, dimensions={0} | all-to-all | bytes 2097152 | tf_op jit(solution)/shard_map/rows_to_shards/all_to_all | solution.py:348
  101.3 2.7 %collective-permute-start.12 = (bf16[6,32,1024]{2,1,0:T(8,128)(2,1)S(1)}, bf16[6,32,1024]{2,1,0:T(8,128)(2,1)S(1)}, u32[]{:S(2)}, u32[]{:S(2)}) collective-permute-start(bf16[6,32,1024]{2,1,0:T(8,128)(2,1)S(1)} %get-tuple-element.61), channel_id=1, source_target_pairs={{0,96},{32,0},{64,32},{96,64},{1,97},{33,1},{65,33},{97,65},{2,98}... | collective-permute-start | bytes 1179656 | tf_op jit(solution)/shard_map/gather_over_replicas/ppermute | solution.py:381
  106.9 6.4 %collective-permute-done.13.refs_3_ = bf16[6,32,1024]{2,1,0:T(8,128)(2,1)S(1)} collective-permute-done((bf16[6,32,1024]{2,1,0:T(8,128)(2,1)S(1)}, bf16[6,32,1024]{2,1,0:T(8,128)(2,1)S(1)}, u32[]{:S(2)}, u32[]{:S(2)}) %collective-permute-start.13) | collective-permute-done | bytes 393248 | tf_op jit(solution)/shard_map/gather_over_replicas/ppermute | solution.py:382
  113.3 2.4 %collective-permute-start.21 = (bf16[6,32,1024]{2,1,0:T(8,128)(2,1)S(1)}, bf16[6,32,1024]{2,1,0:T(8,128)(2,1)S(1)}, u32[]{:S(2)}, u32[]{:S(2)}) collective-permute-start(bf16[6,32,1024]{2,1,0:T(8,128)(2,1)S(1)} %collective-permute-done.12.refs_2_), channel_id=1, source_target_pairs={{0,96},{32,0},{64,32},{96,64},{1,97},{33,1},{65,33},{97,65},{2,98}... | collective-permute-start | bytes 1179656 | tf_op jit(solution)/shard_map/gather_over_replicas/ppermute | solution.py:390
  115.7 2.2 %collective-permute-start.15 = (bf16[12,32,1024]{2,1,0:T(8,128)(2,1)S(1)}, bf16[12,32,1024]{2,1,0:T(8,128)(2,1)S(1)}, u32[]{:S(2)}, u32[]{:S(2)}) collective-permute-start(bf16[12,32,1024]{2,1,0:T(8,128)(2,1)S(1)} %pad_maximum_fusion), channel_id=1, source_target_pairs={{0,16},{16,0},{1,17},{17,1},{2,18},{18,2},{3,19},{19,3},{4,20},{20... | collective-permute-start | bytes 2359304 | tf_op jit(solution)/shard_map/gather_over_replicas/ppermute | solution.py:378
  117.9 2.7 %collective-permute-done.17.refs_4_ = bf16[6,32,1024]{2,1,0:T(8,128)(2,1)S(1)} collective-permute-done((bf16[6,32,1024]{2,1,0:T(8,128)(2,1)S(1)}, bf16[6,32,1024]{2,1,0:T(8,128)(2,1)S(1)}, u32[]{:S(2)}, u32[]{:S(2)}) %collective-permute-start.17) | collective-permute-done | bytes 393248 | tf_op jit(solution)/shard_map/gather_over_replicas/ppermute | solution.py:385
  121.7 2.3 %place_early.1.refs_7_ = bf16[48,64,1024]{2,1,0:T(8,128)(2,1)} custom-call(s32[3]{0:T(128)S(1)} %pad_add_fusion.place, bf16[12,32,1024]{2,1,0:T(8,128)(2,1)S(1)} %slice.43.refs_0_, bf16[12,32,1024]{2,1,0:T(8,128)(2,1)S(1)} %collective-permute-done.14.refs_1_, bf16[6,32,1024]{2,1,0:T(8,128)(2,1)S(1)} %collective-permute-done.12.refs_2_, ...), custom_call_target="tpu_custom_call" | custom-call | bytes 6291456 | tf_op jit(solution)/shard_map/gather_over_replicas/place_early/pallas_call | solution.py:365
  125.3 3.8 %collective-permute-done.21.refs_3_ = bf16[6,32,1024]{2,1,0:T(8,128)(2,1)S(1)} collective-permute-done((bf16[6,32,1024]{2,1,0:T(8,128)(2,1)S(1)}, bf16[6,32,1024]{2,1,0:T(8,128)(2,1)S(1)}, u32[]{:S(2)}, u32[]{:S(2)}) %collective-permute-start.21) | collective-permute-done | bytes 393248 | tf_op jit(solution)/shard_map/gather_over_replicas/ppermute | solution.py:390
  132.3 2.3 %place_late.1 = bf16[48,64,1024]{2,1,0:T(8,128)(2,1)} custom-call(s32[3]{0:T(128)S(1)} %pad_add_fusion.place, bf16[12,32,1024]{2,1,0:T(8,128)(2,1)S(1)} %collective-permute-done.15.refs_0_, bf16[6,32,1024]{2,1,0:T(8,128)(2,1)S(1)} %collective-permute-done.19.refs_1_, ...), custom_call_target="tpu_custom_call", output_to_operand_aliasing={{}: (8, {})} | custom-call | bytes 6291456 | tf_op jit(solution)/shard_map/gather_over_replicas/place_late/pallas_call | solution.py:365
  (52 shorter events, 18.9 us)
Async XLA Ops:
  1.2 5.6 %collective-permute-start = (bf16[12,32,1024]{2,1,0:T(8,128)(2,1)S(1)}, bf16[12,32,1024]{2,1,0:T(8,128)(2,1)S(1)}, u32[]{:S(2)}, u32[]{:S(2)}) collective-permute-start(bf16[12,32,1024]{2,1,0:T(8,128)(2,1)S(1)} %dynamic-slice_bitcast_fusion.7), channel_id=1, source_target_pairs={{0,16},{16,0},{1,17},{17,1},{2,18},{18,2},{3,19},{19,3},{4,20},{20... | collective-permute-start | bytes 2359304 | tf_op jit(solution)/shard_map/sum_over_replicas/ppermute | solution.py:269
  6.2 6.6 %collective-permute-start.2 = (bf16[12,32,1024]{2,1,0:T(8,128)(2,1)}, bf16[12,32,1024]{2,1,0:T(8,128)(2,1)}, u32[]{:S(2)}, u32[]{:S(2)}) collective-permute-start(bf16[12,32,1024]{2,1,0:T(8,128)(2,1)} %get-tuple-element.45), channel_id=1, source_target_pairs={{0,16},{16,0},{1,17},{17,1},{2,18},{18,2},{3,19},{19,3},{4,20},{20... | collective-permute-start | bytes 2359304 | tf_op jit(solution)/shard_map/sum_over_replicas/ppermute | solution.py:273
  6.3 6.5 %collective-permute-start.4 = (bf16[12,32,1024]{2,1,0:T(8,128)(2,1)}, bf16[12,32,1024]{2,1,0:T(8,128)(2,1)}, u32[]{:S(2)}, u32[]{:S(2)}) collective-permute-start(bf16[12,32,1024]{2,1,0:T(8,128)(2,1)} %get-tuple-element.48), channel_id=1, source_target_pairs={{0,16},{16,0},{1,17},{17,1},{2,18},{18,2},{3,19},{19,3},{4,20},{20... | collective-permute-start | bytes 2359304 | tf_op jit(solution)/shard_map/sum_over_replicas/ppermute | solution.py:273
  6.7 16.1 %collective-permute-start.1 = (bf16[12,32,1024]{2,1,0:T(8,128)(2,1)S(1)}, bf16[12,32,1024]{2,1,0:T(8,128)(2,1)}, u32[]{:S(2)}, u32[]{:S(2)}) collective-permute-start(bf16[12,32,1024]{2,1,0:T(8,128)(2,1)S(1)} %get-tuple-element.43), channel_id=1, source_target_pairs={{0,16},{16,0},{1,17},{17,1},{2,18},{18,2},{3,19},{19,3},{4,20},{20... | collective-permute-start | bytes 2359304 | tf_op jit(solution)/shard_map/sum_over_replicas/ppermute | solution.py:273
  7.0 12.0 %collective-permute-start.5 = (bf16[6,32,1024]{2,1,0:T(8,128)(2,1)S(1)}, bf16[6,32,1024]{2,1,0:T(8,128)(2,1)S(1)}, u32[]{:S(2)}, u32[]{:S(2)}) collective-permute-start(bf16[6,32,1024]{2,1,0:T(8,128)(2,1)S(1)} %get-tuple-element.49), channel_id=1, source_target_pairs={{0,96},{32,0},{64,32},{96,64},{1,97},{33,1},{65,33},{97,65},{2,98}... | collective-permute-start | bytes 1179656 | tf_op jit(solution)/shard_map/sum_over_replicas/ppermute | solution.py:276
  10.9 11.6 %collective-permute-start.8 = (bf16[6,32,1024]{2,1,0:T(8,128)(2,1)S(1)}, bf16[6,32,1024]{2,1,0:T(8,128)(2,1)S(1)}, u32[]{:S(2)}, u32[]{:S(2)}) collective-permute-start(bf16[6,32,1024]{2,1,0:T(8,128)(2,1)S(1)} %get-tuple-element.50), channel_id=1, source_target_pairs={{0,32},{32,64},{64,96},{96,0},{1,33},{33,65},{65,97},{97,1},{2,34}... | collective-permute-start | bytes 1179656 | tf_op jit(solution)/shard_map/sum_over_replicas/ppermute | solution.py:277
  14.9 15.6 %collective-permute-start.3 = (bf16[6,32,1024]{2,1,0:T(8,128)(2,1)S(1)}, bf16[6,32,1024]{2,1,0:T(8,128)(2,1)S(1)}, u32[]{:S(2)}, u32[]{:S(2)}) collective-permute-start(bf16[6,32,1024]{2,1,0:T(8,128)(2,1)S(1)} %get-tuple-element.77), channel_id=1, source_target_pairs={{0,32},{32,64},{64,96},{96,0},{1,33},{33,65},{65,97},{97,1},{2,34}... | collective-permute-start | bytes 1179656 | tf_op jit(solution)/shard_map/sum_over_replicas/ppermute | solution.py:284
  15.8 16.0 %collective-permute-start.7 = (bf16[6,32,1024]{2,1,0:T(8,128)(2,1)}, bf16[6,32,1024]{2,1,0:T(8,128)(2,1)S(1)}, u32[]{:S(2)}, u32[]{:S(2)}) collective-permute-start(bf16[6,32,1024]{2,1,0:T(8,128)(2,1)} %get-tuple-element.78), channel_id=1, source_target_pairs={{0,96},{32,0},{64,32},{96,64},{1,97},{33,1},{65,33},{97,65},{2,98}... | collective-permute-start | bytes 1179656 | tf_op jit(solution)/shard_map/sum_over_replicas/ppermute | solution.py:285
  19.1 16.8 %collective-permute-start.6 = (bf16[6,32,1024]{2,1,0:T(8,128)(2,1)S(1)}, bf16[6,32,1024]{2,1,0:T(8,128)(2,1)S(1)}, u32[]{:S(2)}, u32[]{:S(2)}) collective-permute-start(bf16[6,32,1024]{2,1,0:T(8,128)(2,1)S(1)} %add_rows.4), channel_id=1, source_target_pairs={{0,96},{32,0},{64,32},{96,64},{1,97},{33,1},{65,33},{97,65},{2,98}... | collective-permute-start | bytes 1179656 | tf_op jit(solution)/shard_map/sum_over_replicas/ppermute | solution.py:287
  22.7 16.3 %collective-permute-start.9 = (bf16[6,32,1024]{2,1,0:T(8,128)(2,1)S(1)}, bf16[6,32,1024]{2,1,0:T(8,128)(2,1)S(1)}, u32[]{:S(2)}, u32[]{:S(2)}) collective-permute-start(bf16[6,32,1024]{2,1,0:T(8,128)(2,1)S(1)} %add_rows.5), channel_id=1, source_target_pairs={{0,32},{32,64},{64,96},{96,0},{1,33},{33,65},{65,97},{97,1},{2,34}... | collective-permute-start | bytes 1179656 | tf_op jit(solution)/shard_map/sum_over_replicas/ppermute | solution.py:288
  61.2 5.1 %collective-permute-start.10 = (bf16[512,1024]{1,0:T(8,128)(2,1)S(1)}, bf16[512,1024]{1,0:T(8,128)(2,1)S(1)}, u32[]{:S(2)}, u32[]{:S(2)}) collective-permute-start(bf16[512,1024]{1,0:T(8,128)(2,1)S(1)} %bitcast.38), channel_id=1, source_target_pairs={{0,16},{16,0},{1,17},{17,1},{2,18},{18,2},{3,19},{19,3},{4,20},{20... | collective-permute-start | bytes 3145736 | tf_op jit(solution)/shard_map/rows_to_owner/ppermute | solution.py:308
  73.4 3.5 %collective-permute-start.11 = (bf16[3,512,512]{2,1,0:T(8,128)(2,1)S(1)}, bf16[3,512,512]{2,1,0:T(8,128)(2,1)S(1)}, u32[]{:S(2)}, u32[]{:S(2)}) collective-permute-start(bf16[3,512,512]{2,1,0:T(8,128)(2,1)S(1)} %get-tuple-element.54.root), channel_id=1, source_target_pairs={{0,16},{16,0},{1,17},{17,1},{2,18},{18,2},{3,19},{19,3},{4,20},{20... | collective-permute-start | bytes 4718600 | tf_op jit(solution)/shard_map/ppermute | solution.py:326
  99.1 14.1 %collective-permute-start.14 = (bf16[12,32,1024]{2,1,0:T(8,128)(2,1)S(1)}, bf16[12,32,1024]{2,1,0:T(8,128)(2,1)S(1)}, u32[]{:S(2)}, u32[]{:S(2)}) collective-permute-start(bf16[12,32,1024]{2,1,0:T(8,128)(2,1)S(1)} %slice.43.refs_0_), channel_id=1, source_target_pairs={{0,16},{16,0},{1,17},{17,1},{2,18},{18,2},{3,19},{19,3},{4,20},{20... | collective-permute-start | bytes 2359304 | tf_op jit(solution)/shard_map/gather_over_replicas/ppermute | solution.py:378
  101.0 12.2 %collective-permute-start.13 = (bf16[6,32,1024]{2,1,0:T(8,128)(2,1)S(1)}, bf16[6,32,1024]{2,1,0:T(8,128)(2,1)S(1)}, u32[]{:S(2)}, u32[]{:S(2)}) collective-permute-start(bf16[6,32,1024]{2,1,0:T(8,128)(2,1)S(1)} %get-tuple-element.60), channel_id=1, source_target_pairs={{0,32},{32,64},{64,96},{96,0},{1,33},{33,65},{65,97},{97,1},{2,34}... | collective-permute-start | bytes 1179656 | tf_op jit(solution)/shard_map/gather_over_replicas/ppermute | solution.py:382
  101.3 11.9 %collective-permute-start.12 = (bf16[6,32,1024]{2,1,0:T(8,128)(2,1)S(1)}, bf16[6,32,1024]{2,1,0:T(8,128)(2,1)S(1)}, u32[]{:S(2)}, u32[]{:S(2)}) collective-permute-start(bf16[6,32,1024]{2,1,0:T(8,128)(2,1)S(1)} %get-tuple-element.61), channel_id=1, source_target_pairs={{0,96},{32,0},{64,32},{96,64},{1,97},{33,1},{65,33},{97,65},{2,98}... | collective-permute-start | bytes 1179656 | tf_op jit(solution)/shard_map/gather_over_replicas/ppermute | solution.py:381
  105.4 15.2 %collective-permute-start.17 = (bf16[6,32,1024]{2,1,0:T(8,128)(2,1)S(1)}, bf16[6,32,1024]{2,1,0:T(8,128)(2,1)S(1)}, u32[]{:S(2)}, u32[]{:S(2)}) collective-permute-start(bf16[6,32,1024]{2,1,0:T(8,128)(2,1)S(1)} %get-tuple-element.60), channel_id=1, source_target_pairs={{0,96},{32,0},{64,32},{96,64},{1,97},{33,1},{65,33},{97,65},{2,98}... | collective-permute-start | bytes 1179656 | tf_op jit(solution)/shard_map/gather_over_replicas/ppermute | solution.py:385
  105.4 16.3 %collective-permute-start.18 = (bf16[6,32,1024]{2,1,0:T(8,128)(2,1)S(1)}, bf16[6,32,1024]{2,1,0:T(8,128)(2,1)S(1)}, u32[]{:S(2)}, u32[]{:S(2)}) collective-permute-start(bf16[6,32,1024]{2,1,0:T(8,128)(2,1)S(1)} %get-tuple-element.61), channel_id=1, source_target_pairs={{0,32},{32,64},{64,96},{96,0},{1,33},{33,65},{65,97},{97,1},{2,34}... | collective-permute-start | bytes 1179656 | tf_op jit(solution)/shard_map/gather_over_replicas/ppermute | solution.py:386
  113.3 15.8 %collective-permute-start.21 = (bf16[6,32,1024]{2,1,0:T(8,128)(2,1)S(1)}, bf16[6,32,1024]{2,1,0:T(8,128)(2,1)S(1)}, u32[]{:S(2)}, u32[]{:S(2)}) collective-permute-start(bf16[6,32,1024]{2,1,0:T(8,128)(2,1)S(1)} %collective-permute-done.12.refs_2_), channel_id=1, source_target_pairs={{0,96},{32,0},{64,32},{96,64},{1,97},{33,1},{65,33},{97,65},{2,98}... | collective-permute-start | bytes 1179656 | tf_op jit(solution)/shard_map/gather_over_replicas/ppermute | solution.py:390
  115.6 14.6 %collective-permute-start.22 = (bf16[6,32,1024]{2,1,0:T(8,128)(2,1)S(1)}, bf16[6,32,1024]{2,1,0:T(8,128)(2,1)S(1)}, u32[]{:S(2)}, u32[]{:S(2)}) collective-permute-start(bf16[6,32,1024]{2,1,0:T(8,128)(2,1)S(1)} %collective-permute-done.13.refs_3_), channel_id=1, source_target_pairs={{0,32},{32,64},{64,96},{96,0},{1,33},{33,65},{65,97},{97,1},{2,34}... | collective-permute-start | bytes 1179656 | tf_op jit(solution)/shard_map/gather_over_replicas/ppermute | solution.py:391
  115.7 16.6 %collective-permute-start.15 = (bf16[12,32,1024]{2,1,0:T(8,128)(2,1)S(1)}, bf16[12,32,1024]{2,1,0:T(8,128)(2,1)S(1)}, u32[]{:S(2)}, u32[]{:S(2)}) collective-permute-start(bf16[12,32,1024]{2,1,0:T(8,128)(2,1)S(1)} %pad_maximum_fusion), channel_id=1, source_target_pairs={{0,16},{16,0},{1,17},{17,1},{2,18},{18,2},{3,19},{19,3},{4,20},{20... | collective-permute-start | bytes 2359304 | tf_op jit(solution)/shard_map/gather_over_replicas/ppermute | solution.py:378
  123.9 7.0 %collective-permute-start.19 = (bf16[6,32,1024]{2,1,0:T(8,128)(2,1)S(1)}, bf16[6,32,1024]{2,1,0:T(8,128)(2,1)S(1)}, u32[]{:S(2)}, u32[]{:S(2)}) collective-permute-start(bf16[6,32,1024]{2,1,0:T(8,128)(2,1)S(1)} %collective-permute-done.17.refs_4_), channel_id=1, source_target_pairs={{0,16},{16,0},{1,17},{17,1},{2,18},{18,2},{3,19},{19,3},{4,20},{20... | collective-permute-start | bytes 1179656 | tf_op jit(solution)/shard_map/gather_over_replicas/ppermute | solution.py:378
  125.2 5.7 %collective-permute-start.20 = (bf16[6,32,1024]{2,1,0:T(8,128)(2,1)S(1)}, bf16[6,32,1024]{2,1,0:T(8,128)(2,1)S(1)}, u32[]{:S(2)}, u32[]{:S(2)}) collective-permute-start(bf16[6,32,1024]{2,1,0:T(8,128)(2,1)S(1)} %collective-permute-done.18.refs_5_), channel_id=1, source_target_pairs={{0,16},{16,0},{1,17},{17,1},{2,18},{18,2},{3,19},{19,3},{4,20},{20... | collective-permute-start | bytes 1179656 | tf_op jit(solution)/shard_map/gather_over_replicas/ppermute | solution.py:378
  129.1 2.5 %collective-permute-start.23 = (bf16[6,32,1024]{2,1,0:T(8,128)(2,1)S(1)}, bf16[6,32,1024]{2,1,0:T(8,128)(2,1)S(1)}, u32[]{:S(2)}, u32[]{:S(2)}) collective-permute-start(bf16[6,32,1024]{2,1,0:T(8,128)(2,1)S(1)} %collective-permute-done.21.refs_3_), channel_id=1, source_target_pairs={{0,16},{16,0},{1,17},{17,1},{2,18},{18,2},{3,19},{19,3},{4,20},{20... | collective-permute-start | bytes 1179656 | tf_op jit(solution)/shard_map/gather_over_replicas/ppermute | solution.py:378
  130.2 2.1 %collective-permute-start.24 = (bf16[6,32,1024]{2,1,0:T(8,128)(2,1)S(1)}, bf16[6,32,1024]{2,1,0:T(8,128)(2,1)S(1)}, u32[]{:S(2)}, u32[]{:S(2)}) collective-permute-start(bf16[6,32,1024]{2,1,0:T(8,128)(2,1)S(1)} %collective-permute-done.22.refs_4_), channel_id=1, source_target_pairs={{0,16},{16,0},{1,17},{17,1},{2,18},{18,2},{3,19},{19,3},{4,20},{20... | collective-permute-start | bytes 1179656 | tf_op jit(solution)/shard_map/gather_over_replicas/ppermute | solution.py:378
  (2 other events, 9.3 us)
